TPU v7x, 32 devices: a whole 2x2x4 slice. The times are simulated.
32 devices in a mesh: rep: 8 (over y, x, core), dom: 4 (over z).
Axes of the slice: x: 2, y: 2, z: 4, core: 2. Of those that a mesh axis runs over, the one named last changes fastest.
Arguments:
- block_input: bfloat16 [32, 8, 16, 320], P(('rep', 'dom')), may hold values from -36 to 36
- cotangent: bfloat16 [32, 8, 16, 320], P(('rep', 'dom')), may hold values from -6 to 6
- timesteps: int32 [32], P(('rep', 'dom')), may hold values from 0 to 999
- owner_map: int32 [4], replicated, may hold values from 0 to 3, each once
- time_weight: bfloat16 [1280, 320], replicated, may hold values from -0.15625 to 0.15625
- first_weight: bfloat16 [2880, 320], P('dom'), may hold values from -0.109375 to 0.109375
- second_weight: bfloat16 [2880, 320], P('dom'), may hold values from -0.109375 to 0.109375
Outputs:
- block_output: bfloat16 [32, 8, 16, 320], P(('rep', 'dom'))
- first_grad: float32 [2880, 320], P('dom')
- second_grad: float32 [2880, 320], P('dom')
Inputs may be any that keep to these rules, and one draw needn't show every extreme that they name: `owner_map`: each dom index holds exactly one block.
All inputs are finite; a program needn't handle non-finite values.
Results may differ from a plain program's by a relative error of at most 0.0064.
Values may be sent and summed in bfloat16 or wider, within the bound.
No kernel may reach another device: no remote copies, remote signals or barrier semaphores. Data moves between devices by JAX's collectives and lax.ppermute only.
A program may use at most 64 MiB of HBM per device.

v0:
```python
import math

import jax
import jax.numpy as jnp
from jax import lax
from jax.sharding import PartitionSpec as P

C = 320
GROUPS = 32
TEMB = 1280
HEIGHT = 8
WIDTH = 16


norm_eps = 1e-05


def columns(activation):
    padded = jnp.pad(activation, ((1, 1), (1, 1), (0, 0)))
    pieces = []
    for row_tap in range(3):
        for col_tap in range(3):
            pieces.append(padded[row_tap : row_tap + HEIGHT, col_tap : col_tap + WIDTH, :])
    return jnp.concatenate(pieces, axis=-1).reshape(HEIGHT * WIDTH, 9 * C)


def tap_window(activation, first_tap, tap_count):
    padded = jnp.pad(activation, ((1, 1), (1, 1), (0, 0)))
    pieces = []
    for offset in range(tap_count):
        tap_index = first_tap + offset
        pieces.append(
            lax.dynamic_slice(padded, (tap_index // 3, tap_index % 3, 0), (HEIGHT, WIDTH, C))
        )
    return jnp.concatenate(pieces, axis=-1).reshape(HEIGHT * WIDTH, tap_count * C)


def spread_back(gathered):
    framed = jnp.pad(gathered.reshape(HEIGHT, WIDTH, 9, C), ((1, 1), (1, 1), (0, 0), (0, 0)))
    result = jnp.zeros((HEIGHT, WIDTH, C), jnp.float32)
    for row_tap in range(3):
        for col_tap in range(3):
            result = (
                result
                + framed[
                    2 - row_tap : 2 - row_tap + HEIGHT,
                    2 - col_tap : 2 - col_tap + WIDTH,
                    3 * row_tap + col_tap,
                    :,
                ]
            )
    return result.reshape(HEIGHT * WIDTH, C)


def group_norm(values):
    grouped = values.reshape(HEIGHT * WIDTH, GROUPS, C // GROUPS)
    center = jnp.mean(grouped, axis=(0, 2), keepdims=True)
    spread = jnp.mean(jnp.square(grouped - center), axis=(0, 2), keepdims=True)
    inverse_std = lax.rsqrt(spread + norm_eps)
    return (((grouped - center) * inverse_std).reshape(HEIGHT * WIDTH, C), inverse_std)


def norm_back(incoming, normed, inverse_std):
    grouped_grad = incoming.reshape(HEIGHT * WIDTH, GROUPS, C // GROUPS)
    grouped_norm = normed.reshape(HEIGHT * WIDTH, GROUPS, C // GROUPS)
    mean_grad = jnp.mean(grouped_grad, axis=(0, 2), keepdims=True)
    mean_prod = jnp.mean(grouped_grad * grouped_norm, axis=(0, 2), keepdims=True)
    return (inverse_std * (grouped_grad - mean_grad - grouped_norm * mean_prod)).reshape(
        HEIGHT * WIDTH, C
    )


def time_bias(timestep, time_weight):
    half_dim = TEMB // 2
    frequency = jnp.exp(-math.log(10000.0) * jnp.arange(half_dim, dtype=jnp.float32) / half_dim)
    angles = timestep.astype(jnp.float32) * frequency
    embedded = jnp.concatenate([jnp.cos(angles), jnp.sin(angles)])
    activated = jax.nn.silu(embedded).astype(jnp.bfloat16)
    return jnp.dot(activated[None, :], time_weight, preferred_element_type=jnp.float32)


def logical_order(stored, owner_map, group_size, block_rows):
    blocks = stored.reshape(group_size, block_rows, C)
    return jnp.take(blocks, owner_map, axis=0).reshape(9 * C, C)


def transposed_product(cols_rows, grad_rows):
    return lax.dot_general(
        cols_rows, grad_rows, (((0,), (0,)), ((), ())), preferred_element_type=jnp.float32
    )


def second_owner_sum(term_rounded, inverse, group_size, block_rows):
    stored_blocks = jnp.take(term_rounded.reshape(group_size, block_rows, C), inverse, axis=0)
    arrived = lax.all_to_all(stored_blocks, "dom", split_axis=0, concat_axis=0, tiled=True)
    return jnp.sum(arrived.astype(jnp.float32), axis=0)


def body(block_input, cotangent, timesteps, owner_map, time_weight, first_weight, second_weight):
    pixels = HEIGHT * WIDTH
    group_size = lax.axis_size("dom")
    block_rows = first_weight.shape[0]
    samples_total = lax.axis_size("rep") * group_size
    block_ids = jnp.arange(group_size, dtype=jnp.int32)
    matches = (owner_map[None, :] == block_ids[:, None]).astype(jnp.int32)
    inverse = jnp.sum(matches * block_ids[None, :], axis=1)
    source = block_input[0].astype(jnp.float32).reshape(pixels, C)
    normed, unused_std = group_norm(source)
    first_act = jax.nn.silu(normed).astype(jnp.bfloat16)
    first_cols = columns(first_act.reshape(HEIGHT, WIDTH, C))
    bias_row = time_bias(timesteps[0], time_weight)
    weight_piece = lax.all_gather(first_weight, "dom", axis=0, tiled=True)
    count = weight_piece.shape[0] // block_rows
    pieces = weight_piece.reshape(count, block_rows, C)

    def add_block(total, item):
        position, block = item
        logical_index = inverse[position]
        columns_taken = lax.dynamic_slice_in_dim(
            first_cols, logical_index * block_rows, block_rows, 1
        )
        return (total + jnp.dot(columns_taken, block, preferred_element_type=jnp.float32), None)

    total, unused_rest = lax.scan(
        add_block, jnp.zeros((pixels, C), jnp.float32), (jnp.arange(count, dtype=jnp.int32), pieces)
    )
    first_conv = total + bias_row
    second_stored = lax.all_gather(second_weight, "dom", axis=0, tiled=True)
    second_logic = logical_order(second_stored, owner_map, group_size, block_rows)
    second_norm, second_std = group_norm(first_conv)
    second_act = jax.nn.silu(second_norm).astype(jnp.bfloat16)
    second_cols = columns(second_act.reshape(HEIGHT, WIDTH, C))
    block_output = (
        source + jnp.dot(second_cols, second_logic, preferred_element_type=jnp.float32)
    ).astype(jnp.bfloat16)
    upstream = cotangent[0].reshape(pixels, C)
    second_term = transposed_product(second_cols, upstream).astype(jnp.bfloat16)
    second_owned = second_owner_sum(second_term, inverse, group_size, block_rows)
    second_back = lax.dot_general(
        upstream, second_logic, (((1,), (1,)), ((), ())), preferred_element_type=jnp.float32
    )
    act_grad = spread_back(second_back)
    gate_value = jax.nn.sigmoid(second_norm)
    norm_grad = act_grad * gate_value * (1.0 + second_norm * (1.0 - gate_value))
    conv_grad = norm_back(norm_grad, second_norm, second_std).astype(jnp.bfloat16)
    own_logical = inverse[lax.axis_index("dom")]
    tap_count = min(9, block_rows // C + 2)
    first_tap = jnp.minimum(own_logical * block_rows // C, 9 - tap_count)
    column_start = own_logical * block_rows - first_tap * C
    act_piece = lax.all_gather(first_act.reshape(1, HEIGHT, WIDTH, C), "dom", axis=0, tiled=True)
    grad_piece = lax.all_gather(conv_grad.reshape(1, HEIGHT, WIDTH, C), "dom", axis=0, tiled=True)

    def add_one(total, pair):
        act_one, grad_one = pair
        window = tap_window(act_one, first_tap, tap_count)
        owned_cols = lax.dynamic_slice_in_dim(window, column_start, block_rows, 1)
        term = transposed_product(owned_cols, grad_one.reshape(pixels, C))
        return (
            total + lax.optimization_barrier(term.astype(jnp.bfloat16)).astype(jnp.float32),
            None,
        )

    total, unused_rest = lax.scan(
        add_one, jnp.zeros((block_rows, C), jnp.float32), (act_piece, grad_piece)
    )
    second_total, first_total = lax.psum((second_owned, total), "rep")
    return (
        block_output.reshape(1, HEIGHT, WIDTH, C),
        first_total / samples_total,
        second_total / samples_total,
    )


def solution(mesh):
    placed = (
        P(("rep", "dom"), None, None, None),
        P(("rep", "dom"), None, None, None),
        P(("rep", "dom")),
        P(),
        P(),
        P("dom", None),
        P("dom", None),
    )
    return jax.shard_map(
        body,
        mesh=mesh,
        in_specs=placed,
        out_specs=(P(("rep", "dom"), None, None, None), P("dom", None), P("dom", None)),
        check_vma=False,
    )
```

profile of v0, /device:TPU:0, one launch (start us, length us, event | category | flops | bytes accessed | tf_op | source)
XLA Modules:
  0.0 300.7 jit_solution(4473818408638728736)
XLA Ops:
  11.4 1.0 multiply_convert_fusion.4
  12.3 1.6 multiply_convert_fusion.3
  18.3 1.2 concatenate.60
  19.7 21.8 %all_gather.14 = bf16[4,8,16,320]{3,2,1,0:T(8,128)(2,1)} all-gather(bf16[1,8,16,320]{3,2,1,0:T(8,128)(2,1)S(1)} %multiply_convert_fusion.1), channel_id=1, replica_groups=mesh['rep'=8,'dom'=4] {'dom'}, dimensions={0}, use_global_device_ids=true | all-gather | bytes 409600 | tf_op jit(solution)/shard_map/all_gather | solution.py:150
  41.8 20.4 %all-gather.5.cloned.1.call-done = bf16[4,720,320]{1,2,0:T(8,128)(2,1)} async-done(((bf16[1,720,320]{1,2,0:T(8,128)(2,1)}), bf16[4,720,320]{1,2,0:T(8,128)(2,1)}) %all-gather.5.cloned.1.call-update) | async-done | bytes 1843216 | tf_op jit(solution)/shard_map/all_gather | solution.py:112
  62.2 20.9 %while.25 = (s32[]{:T(128)}, f32[128,320]{0,1:T(8,128)S(1)}, s32[4]{0:T(128)S(1)}, s32[4]{0:T(128)S(1)}, bf16[128,2880]{1,0:T(8,128)(2,1)S(1)}, /*index=5*/bf16[...) while((s32[]{:T(128)}, f32[128,320]{0,1:T(8,128)S(1)}, ...), condition=%wide.region_6.7_spmd.clone, body=%wide.region_5.6_spmd.clone.sunk | while | flops 59064328 | bytes 1016547 | solution.py:124
  66.0 1.4 convolution_add_fusion.3
  71.2 1.4 convolution_add_fusion.3
  76.4 1.4 convolution_add_fusion.3
  81.7 1.4 convolution_add_fusion.3
  84.2 22.0 %all-gather.7.cloned.1.call-done = bf16[4,720,320]{1,2,0:T(8,128)(2,1)} async-done(((bf16[1,720,320]{1,2,0:T(8,128)(2,1)}), bf16[4,720,320]{1,2,0:T(8,128)(2,1)}) %all-gather.7.cloned.1.call-update) | async-done | bytes 1843216 | tf_op jit(solution)/shard_map/all_gather | solution.py:128
  106.2 3.5 %gather_fusion = bf16[4,720,320]{1,2,0:T(8,128)(2,1)} fusion(bf16[4,720,320]{1,2,0:T(8,128)(2,1)} %all-gather.7.cloned.1.call-done, s32[1024]{0:T(1024)S(1)} %pad_clamp_fusion.1), kind=kCustom, calls=%fused_computation.clone | custom fusion | bytes 3686416 | tf_op jit(solution)/shard_map/jit(_take)/gather | solution.py:84
  109.7 1.8 broadcast_select_fusion.1
  111.5 2.8 copy.39
  114.3 4.6 %reshape.193 = bf16[2880,320]{0,1:T(8,128)(2,1)} reshape(bf16[4,720,320]{1,0,2:T(4,128)(2,1)} %copy.39) | data formatting | bytes 3686400 | tf_op jit(solution)/shard_map/reshape | solution.py:84
  118.9 2.3 convolution_bitcast_fusion
  121.3 1.6 copy.42
  122.9 3.1 %reshape.195 = f32[8,16,9,320]{3,2,1,0:T(8,128)} reshape(f32[128,2880]{1,0:T(8,128)} %copy.42) | data formatting | bytes 2949120 | tf_op jit(solution)/shard_map/reshape | solution.py:39
  126.0 7.0 %fusion.13 = f32[8,16,1,320]{3,2,1,0:T(1,128)S(1)} fusion(f32[8,16,9,320]{3,2,1,0:T(8,128)} %reshape.195), kind=kLoop, calls=%fused_computation.57 | loop fusion | flops 327680 | bytes 3506176 | tf_op jit(solution)/shard_map/add | solution.py:44
  135.4 2.9 convolution_convert_fusion.1
  138.3 5.8 %reshape.197 = bf16[4,720,320]{1,0,2:T(4,128)(2,1)} reshape(bf16[2880,320]{0,1:T(8,128)(2,1)} %convolution_convert_fusion.1) | data formatting | bytes 3686400 | tf_op jit(solution)/shard_map/reshape | solution.py:94
  144.1 3.1 %copy.43 = bf16[4,720,320]{1,2,0:T(8,128)(2,1)} copy(bf16[4,720,320]{1,0,2:T(4,128)(2,1)} %reshape.197) | data formatting | bytes 3686400 | tf_op jit(solution)/shard_map/reshape | solution.py:94
  147.2 3.5 %gather_fusion.1 = bf16[4,720,320]{1,2,0:T(8,128)(2,1)} fusion(bf16[4,720,320]{1,2,0:T(8,128)(2,1)} %copy.43, s32[1024]{0:T(1024)S(1)} %pad_clamp_fusion), kind=kCustom, calls=%fused_computation.1.clone | custom fusion | bytes 3686416 | tf_op jit(solution)/shard_map/jit(_take)/gather | solution.py:94
  150.7 3.1 %broadcast_select_fusion = bf16[4,720,320]{1,2,0:T(8,128)(2,1)} fusion(bf16[4,720,320]{1,2,0:T(8,128)(2,1)} %gather_fusion.1, pred[4]{0:T(512)(128)(4,1)S(1)} %compare_and_fusion), kind=kLoop, calls=%fused_computation.28 | loop fusion | flops 921600 | bytes 3686404 | tf_op jit(solution)/shard_map/jit(_take)/select_n | solution.py:94
  153.7 4.6 %all-to-all-start = ((bf16[4,720,320]{1,2,0:T(8,128)(2,1)}), bf16[4,720,320]{1,2,0:T(8,128)(2,1)}, u32[]{:S(2)}, u32[]{:S(2)}) async-start(bf16[4,720,320]{1,2,0:T(8,128)(2,1)} %broadcast_select_fusion), calls=%async_computation | async-start | bytes 3932160 | tf_op jit(solution)/shard_map/all_to_all | solution.py:95
  158.4 55.2 %all_gather.15 = bf16[4,8,16,320]{3,2,1,0:T(8,128)(2,1)} all-gather(bf16[1,8,16,320]{3,2,1,0:T(8,128)(2,1)S(1)} %bitcast.104), channel_id=1, replica_groups=mesh['rep'=8,'dom'=4] {'dom'}, dimensions={0}, use_global_device_ids=true | all-gather | bytes 409600 | tf_op jit(solution)/shard_map/all_gather | solution.py:151
  213.6 12.2 %while.26 = (s32[]{:T(128)}, f32[720,320]{0,1:T(8,128)S(1)}, bf16[4,8,16,320]{3,2,1,0:T(8,128)(2,1)}, s32[]{:T(128)}, s32[]{:T(128)}, /*index=5*/s32[]{:T(128)},...) while((s32[]{:T(128)}, f32[720,320]{0,1:T(8,128)S(1)}, ...), condition=%wide.region_16.18_spmd.clone, body=%wide.region_15.17_spmd.clone.sunk | while | flops 59904000 | bytes 4452547 | solution.py:163
  225.9 3.2 %convert_reduce_fusion = f32[720,320]{0,1:T(8,128)} fusion(bf16[4,720,320]{1,2,0:T(8,128)(2,1)} %all-to-all-done), kind=kLoop, calls=%fused_computation.26 | loop fusion | flops 1612800 | bytes 2764800 | tf_op jit(solution)/shard_map/reduce_sum | solution.py:96
  229.2 2.2 fusion.6
  232.2 58.7 %all-reduce.7.cloned.1.call-done = (f32[720,320]{0,1:T(8,128)}, f32[720,320]{0,1:T(8,128)}) async-done(((f32[720,320]{0,1:T(8,128)}, f32[720,320]{0,1:T(8,128)}), (f32[720,320]{0,1:T(8,128)}, f32[720,320]{0,1:T(8,128)})) %all-reduce.7.cloned.1.call-update) | async-done | bytes 1843216 | tf_op jit(solution)/shard_map/psum | solution.py:166
  290.8 2.3 broadcast_multiply_fusion
  293.1 1.0 broadcast_multiply_fusion.1
  (112 shorter events, 28.4 us)
Async XLA Ops:
  7.2 34.3 %copy-start = (bf16[1280,320]{0,1:T(8,128)(2,1)S(1)}, bf16[1280,320]{0,1:T(8,128)(2,1)}, u32[]{:S(2)}) copy-start(bf16[1280,320]{0,1:T(8,128)(2,1)} %param.17) | copy-start | bytes 2457604
  7.2 55.0 %all-gather.5.cloned.1.call-start = ((), (), s32[]{:S(2)}) async-start(), calls=%async_computation.1 | async-start | bytes 2457600 | tf_op jit(solution)/shard_map/all_gather | solution.py:112
  7.9 98.3 %all-gather.7.cloned.1.call-start = ((), (), s32[]{:S(2)}) async-start(), calls=%async_computation.2 | async-start | bytes 2457600 | tf_op jit(solution)/shard_map/all_gather | solution.py:128
  8.0 11.6 %copy-start.2 = (bf16[1,8,16,320]{3,2,1,0:T(8,128)(2,1)S(1)}, bf16[1,8,16,320]{3,2,1,0:T(8,128)(2,1)}, u32[]{:S(2)}) copy-start(bf16[1,8,16,320]{3,2,1,0:T(8,128)(2,1)} %param.13) | copy-start | bytes 245764
  16.8 25.0 %copy-start.6 = (s32[4]{0:T(128)S(1)}, s32[4]{0:T(128)}, u32[]{:S(2)}) copy-start(s32[4]{0:T(128)} %param.16) | copy-start | bytes 52
  153.7 4.6 %copy-start.5 = (bf16[128,320]{1,0:T(8,128)(2,1)S(1)}, bf16[128,320]{1,0:T(8,128)(2,1)}, u32[]{:S(2)}) copy-start(bf16[128,320]{1,0:T(8,128)(2,1)} %get-tuple-element.565) | copy-start | bytes 245764
  153.7 72.1 %all-to-all-start = ((bf16[4,720,320]{1,2,0:T(8,128)(2,1)}), bf16[4,720,320]{1,2,0:T(8,128)(2,1)}, u32[]{:S(2)}, u32[]{:S(2)}) async-start(bf16[4,720,320]{1,2,0:T(8,128)(2,1)} %broadcast_select_fusion), calls=%async_computation | async-start | bytes 3932160 | tf_op jit(solution)/shard_map/all_to_all | solution.py:95
  158.3 132.5 %all-reduce.7.cloned.1.call-start = ((), (), s32[]{:S(2)}) async-start(), calls=%async_computation.3 | async-start | bytes 3932160 | tf_op jit(solution)/shard_map/psum | solution.py:166
  225.8 3.2 %copy-start.1 = (f32[720,320]{0,1:T(8,128)}, f32[720,320]{0,1:T(8,128)S(1)}, u32[]{:S(2)}) copy-start(f32[720,320]{0,1:T(8,128)S(1)} %get-tuple-element.434) | copy-start | bytes 2764804
  225.8 3.3 %copy-start.3 = (bf16[1,8,16,320]{3,2,1,0:T(8,128)(2,1)S(1)}, bf16[1,8,16,320]{3,2,1,0:T(8,128)(2,1)}, u32[]{:S(2)}) copy-start(bf16[1,8,16,320]{3,2,1,0:T(8,128)(2,1)} %param.13) | copy-start | bytes 245764
  290.8 2.3 copy-start.4
Sparse Core Ops, SparseCore 0:
  9.6 52.5 all-gather.4
  63.8 42.3 all-gather.6
  229.2 61.5 all-reduce.6
where the time goes:
time: 302 us; the launch traced here: 301 us
  waiting for transfers between devices  102 us (34%)
  blocking collectives  77 us (25%)
  local copies, waits for them, and re-layouts  47.8 us (16%)
  other arithmetic  27.3 us (9%)
  between operations  15.6 us (5%)
  matrix products  15.1 us (5%)
  loops' own time  10.7 us (4%)
  starting transfers between devices  4.68 us (2%)
    psum x1, waiting for transfers between devices, body(): second_total, first_total = lax.psum((second_owned, total), 'rep')  58.7 us
    all_gather x1, blocking collectives, body(): lax.all_gather(conv_grad.reshape(1, HEIGHT, WIDTH, C), 'dom', axis=0, til...  55.2 us
    all_gather x1, waiting for transfers between devices, body(): second_stored = lax.all_gather(second_weight, 'dom', axis=0, tiled=True)  22 us
    all_gather x1, blocking collectives, body(): lax.all_gather(first_act.reshape(1, HEIGHT, WIDTH, C), 'dom', axis=0, til...  21.8 us
    all_gather x1, waiting for transfers between devices, body(): weight_piece = lax.all_gather(first_weight, 'dom', axis=0, tiled=True)  20.4 us
    another operation x1, loops' own time, body(): lax.scan(add_block, jnp.zeros((pixels, C), jnp.float32), (jnp.arange(coun...  10.5 us
    reshape x2, local copies, waits for them, and re-layouts, second_owner_sum(): term_rounded.reshape(group_size, block_rows, C)  8.9 us
    add x1, other arithmetic, spread_back(): result + framed[2 - row_tap:2 - row_tap + HEIGHT, 2 - col_tap:2 - col_tap...  7.03 us
  transfers between devices with their start and end apart: 4, of which 3 were waited for; matrix products, arithmetic and copies ran while one was open for 12% of the time, Pallas kernels for 0%

commit v1 on v0

v1 whole, which is shorter than its diff:
```python
import functools
import math

import jax
import jax.numpy as jnp
from jax import lax
from jax.experimental import pallas as pl
from jax.experimental.pallas import tpu as pltpu
from jax.sharding import PartitionSpec as P

GROUPS = 32
NORM_EPS = 1e-05
F32 = jnp.float32
BF16 = jnp.bfloat16
HIGHEST = lax.Precision.HIGHEST


def round_up(value, unit):
    return -(-value // unit) * unit


def nn(a, b, precision=None):
    return lax.dot_general(
        a, b, (((1,), (0,)), ((), ())), precision=precision, preferred_element_type=F32
    )


def nt(a, b):
    return lax.dot_general(a, b, (((1,), (1,)), ((), ())), preferred_element_type=F32)


def tn(a, b):
    return lax.dot_general(a, b, (((0,), (0,)), ((), ())), preferred_element_type=F32)


def iota(shape, axis):
    return lax.broadcasted_iota(jnp.int32, shape, axis)


def quotient(value, unit):
    return jnp.floor((value.astype(F32) + 0.5) * (1.0 / unit)).astype(jnp.int32)


def one_hot(hit):
    return jnp.where(hit, 1.0, 0.0).astype(BF16)


def silu(value):
    return value / (1.0 + jnp.exp(-value))


class Plan:
    def __init__(self, n_rep, n_dom, height, width, channels, embed, block_rows):
        self.n_rep, self.n_dom = n_rep, n_dom
        self.height, self.width, self.channels = height, width, channels
        self.embed, self.block_rows = embed, block_rows
        self.pixels = height * width
        self.per_group = channels // GROUPS
        team = 1
        while (
            n_rep % (2 * team) == 0
            and GROUPS % (2 * team) == 0
            and block_rows % (2 * team * self.per_group) == 0
        ):
            team *= 2
        self.team = team
        self.local = channels // team
        self.stretch = self.per_group * team
        self.stretches = block_rows // self.stretch
        self.quarters = channels // self.stretch
        self.piece = self.stretches * self.per_group
        self.piece_pad = round_up(self.piece, 16)
        self.wide = round_up(3 * self.local, 128)
        self.act_rows = self.pixels + 16

    def dom_peer(self, here, step):
        if self.n_dom & (self.n_dom - 1) == 0:
            return here ^ step
        return lax.rem(here + step, self.n_dom)

    def dom_source(self, here, step):
        if self.n_dom & (self.n_dom - 1) == 0:
            return here ^ step
        return lax.rem(here - step + self.n_dom, self.n_dom)


def logical_of(plan, owner_ref, holder):
    total = 0
    for block in range(plan.n_dom):
        total = total + jnp.where(owner_ref[block] == holder, block, 0)
    return total


def group_matrix(plan, lanes, channels):
    row, col = iota((lanes, lanes), 0), iota((lanes, lanes), 1)
    same = quotient(row, plan.per_group) == quotient(col, plan.per_group)
    return jnp.where(same & (row < channels) & (col < channels), 1.0, 0.0)


def prep_kernel(plan, place_ref, steps_ref, x_ref, tw_ref, w1_ref, w2_ref, act_ref, s1_ref, s2_ref):
    c, pix = plan.channels, plan.pixels
    spot = place_ref[0]
    row, col = iota((plan.local, c), 0), iota((plan.local, c), 1)
    band = quotient(row, plan.per_group)
    wanted = band * plan.stretch + spot * plan.per_group + row - band * plan.per_group
    s1_ref[...] = nn(one_hot(col == wanted), w1_ref[...]).astype(BF16)
    row, col = iota((plan.piece_pad, plan.block_rows), 0), iota((plan.piece_pad, plan.block_rows), 1)
    band = quotient(row, plan.per_group)
    wanted = band * plan.stretch + spot * plan.per_group + row - band * plan.per_group
    s2_ref[...] = nt(one_hot((col == wanted) & (row < plan.piece)), w2_ref[...]).astype(BF16)
    x = x_ref[...].astype(F32)
    same = group_matrix(plan, c, c)
    count = pix * plan.per_group
    center = nn(jnp.broadcast_to(jnp.sum(x, 0, keepdims=True), (8, c)), same, HIGHEST)[0:1] / count
    off = x - center
    spread = nn(jnp.broadcast_to(jnp.sum(off * off, 0, keepdims=True), (8, c)), same, HIGHEST)[0:1] / count
    act_ref[0:pix, :] = silu(off * lax.rsqrt(spread + NORM_EPS)).astype(BF16)
    half = plan.embed // 2
    lane = iota((8, plan.embed), 1)
    k = jnp.where(lane < half, lane, lane - half).astype(F32)
    angle = steps_ref[0].astype(F32) * jnp.exp(-math.log(10000.0) * k / half)
    wave = jnp.where(lane < half, jnp.cos(angle), jnp.sin(angle))
    bias = nt(silu(wave).astype(BF16), tw_ref[...])
    high = bias.astype(BF16)
    rest = bias - high.astype(F32)
    mid = rest.astype(BF16)
    low = (rest - mid.astype(F32)).astype(BF16)
    which = iota((16, c), 0)
    high, mid, low = (jnp.concatenate([v.astype(F32)] * 2, axis=0) for v in (high, mid, low))
    tail = jnp.where(which == 0, high, jnp.where(which == 1, mid, jnp.where(which == 2, low, 0.0)))
    act_ref[pix:, :] = tail.astype(BF16)


def roll_rows(value, shift, width, plan):
    rows = value.shape[0]
    moved = pltpu.roll(value, shift % rows, 0)
    x = iota(value.shape, 0) & (width - 1) if width & (width - 1) == 0 else lax.rem(iota(value.shape, 0), width)
    return jnp.where(x == (0 if shift == 1 else width - 1), 0.0, moved)


def roll_lanes(value, shift):
    lanes = value.shape[1]
    return value if shift % lanes == 0 else pltpu.roll(value, shift % lanes, 1)


def gather_taps(wide, plan, sign):
    left = roll_rows(wide, sign, plan.width, plan)
    right = roll_rows(roll_lanes(wide, -2 * plan.local), -sign, plan.width, plan)
    return left + roll_lanes(wide, -plan.local) + right


def spread_taps(value, plan, sign):
    left = roll_rows(value, sign, plan.width, plan)
    right = roll_rows(value, -sign, plan.width, plan)
    return left + roll_lanes(value, plan.local) + roll_lanes(right, 2 * plan.local)


def main_kernel(plan, n_team, *refs):
    d, c, pix, local, wide = plan.n_dom, plan.channels, plan.pixels, plan.local, plan.wide
    place_ref, owner_ref = refs[0:2]
    acts = refs[2 : 2 + n_team]
    cots = refs[2 + n_team : 2 + 2 * n_team]
    w1s = refs[2 + 2 * n_team : 2 + 2 * n_team + d]
    w2s = refs[2 + 2 * n_team + d : 2 + 2 * n_team + 2 * d]
    rest = refs[2 + 2 * n_team + 2 * d :]
    part_ref = rest[0]
    g1s = rest[1 : 1 + d]
    g2s = rest[1 + d : 1 + 2 * d]
    actp, cotp, act2p, w1st, w2st, g1st = rest[1 + 2 * d :]
    spot, here = place_ref[0], place_ref[1]
    rows = n_team * pix
    width = plan.width

    for pad in (actp, cotp):
        pad[:, 0:width, :] = jnp.zeros((n_team, width, c), BF16)
        pad[:, width + pix :, :] = jnp.zeros((n_team, width, c), BF16)
    act2p[:, 0:width, :] = jnp.zeros((n_team, width, wide), BF16)
    act2p[:, width + pix :, :] = jnp.zeros((n_team, width, wide), BF16)
    for slot in range(n_team):
        actp[slot, width : width + pix, :] = acts[slot][0:pix, :]
        cotp[slot, width : width + pix, :] = cots[slot][...]

    def window(pad, tap):
        return pad[:, tap * width : tap * width + pix, :].reshape(rows, pad.shape[2])

    for slot in range(d):
        block = logical_of(plan, owner_ref, plan.dom_source(here, slot))
        w1st[block] = w1s[slot][...].astype(F32)
        w2st[slot] = w2s[slot][...]
    flat = jnp.concatenate([w1st[b] for b in range(d)], axis=1)
    zeros = [jnp.zeros((wide - 3 * local, c), F32)] if wide > 3 * local else []
    w1k = [
        jnp.concatenate(
            [flat[:, (3 * ky + kx) * c : (3 * ky + kx + 1) * c] for kx in range(3)] + zeros, axis=0
        ).astype(BF16)
        for ky in range(3)
    ]
    row, col = iota((3 * wide, plan.piece_pad), 0), iota((3 * wide, plan.piece_pad), 1)
    band = quotient(row, wide)
    within = row - band * wide
    compact = jnp.where(within < 3 * local, band * 3 * local + within, -1)
    w2all = jnp.zeros((3 * wide, c), F32)
    for slot in range(d):
        block = logical_of(plan, owner_ref, plan.dom_source(here, slot))
        hit = (col < plan.piece) & (compact == block * plan.piece + col)
        w2all = w2all + nn(one_hot(hit), w2st[slot])
    w2k = [w2all[ky * wide : (ky + 1) * wide].astype(BF16) for ky in range(3)]

    total = jnp.zeros((rows, wide), F32)
    for ky in range(3):
        total = total + nt(window(actp, ky), w1k[ky])
    conv = gather_taps(total, plan, 1)
    row, col = iota((c, wide), 0), iota((c, wide), 1)
    band = quotient(col, plan.per_group)
    wanted = band * plan.stretch + spot * plan.per_group + col - band * plan.per_group
    pick = one_hot((col < local) & (row == wanted))
    lane_ok = iota((1, wide), 1) < local
    same = group_matrix(plan, wide, local)
    count = pix * plan.per_group

    def group_mean(value):
        sums = jnp.sum(value.reshape(n_team, pix, wide), axis=1)
        if n_team < 8:
            sums = jnp.concatenate([sums, jnp.zeros((8 - n_team, wide), F32)], axis=0)
        return nn(sums, same, HIGHEST)[0:n_team].reshape(n_team, 1, wide) / count

    biases = []
    for slot in range(n_team):
        split = nn(acts[slot][pix:, :], pick)
        biases.append(split[0:1] + split[1:2] + split[2:3])
    bias = jnp.concatenate(biases, axis=0).reshape(n_team, 1, wide)
    conv = jnp.where(lane_ok, conv, 0.0).reshape(n_team, pix, wide) + bias
    off = conv - group_mean(conv.reshape(rows, wide))
    inverse = lax.rsqrt(group_mean((off * off).reshape(rows, wide)) + NORM_EPS)
    norm = off * inverse
    gate = 1.0 / (1.0 + jnp.exp(-norm))
    act2 = norm * gate
    act2x = spread_taps(act2.reshape(rows, wide), plan, 1)
    act2p[:, width : width + pix, :] = act2x.astype(BF16).reshape(n_team, pix, wide)

    out = jnp.zeros((rows, c), F32)
    for ky in range(3):
        out = out + nn(window(act2p, ky), w2k[ky])
    part_ref[...] = out.astype(BF16).reshape(n_team, pix, c)

    act2t = act2x.T.astype(BF16)
    second = jnp.concatenate([nn(act2t, window(cotp, 2 - ky)) for ky in range(3)], axis=0).astype(BF16)
    row, col = iota((plan.piece_pad, 3 * wide), 0), iota((plan.piece_pad, 3 * wide), 1)
    band = quotient(col, wide)
    within = col - band * wide
    compact = jnp.where(within < 3 * local, band * 3 * local + within, -1)
    for slot in range(d):
        block = logical_of(plan, owner_ref, plan.dom_peer(here, slot))
        hit = (row < plan.piece) & (compact == block * plan.piece + row)
        g2s[slot][...] = nn(one_hot(hit), second).astype(BF16)

    back = jnp.zeros((rows, wide), F32)
    for ky in range(3):
        back = back + nt(window(cotp, 2 - ky), w2k[ky])
    back = jnp.where(lane_ok, gather_taps(back, plan, -1), 0.0).reshape(n_team, pix, wide)
    grad = back * gate * (1.0 + norm * (1.0 - gate))
    grad_mean = group_mean(grad.reshape(rows, wide))
    prod_mean = group_mean((grad * norm).reshape(rows, wide))
    grad = inverse * (grad - grad_mean - norm * prod_mean)
    grad = jnp.where(lane_ok, grad, 0.0).reshape(rows, wide)

    gradt = spread_taps(grad.astype(BF16).astype(F32), plan, -1).T.astype(BF16)
    parts = [nn(gradt, window(actp, ky)) for ky in range(3)]
    flat = jnp.concatenate(
        [parts[t // 3][(t % 3) * local : (t % 3 + 1) * local] for t in range(9)], axis=1
    )
    for block in range(d):
        g1st[block] = flat[:, block * plan.block_rows : (block + 1) * plan.block_rows]
    for slot in range(d):
        block = logical_of(plan, owner_ref, plan.dom_peer(here, slot))
        g1s[slot][...] = g1st[block].astype(BF16)


def sum_kernel(n, *refs):
    outs = refs[-len(refs) // (n + 1) :]
    for i, out in enumerate(outs):
        total = refs[i][...].astype(F32)
        for k in range(1, n):
            total = total + refs[i + k * len(outs)][...].astype(F32)
        out[...] = total.astype(out.dtype)


def pair_kernel(n, part_ref, came_ref, out_ref):
    for k in range(n):
        out_ref[k] = (part_ref[2 * k].astype(F32) + came_ref[k].astype(F32)).astype(BF16)


def out_kernel(n, *refs):
    total = refs[0][...].astype(F32)
    for k in range(1, n + 1):
        total = total + refs[k][...].astype(F32)
    refs[n + 1][...] = total.astype(BF16)


def last_kernel(plan, n_team, scale, place_ref, *refs):
    local, c, r = plan.local, plan.channels, plan.block_rows
    firsts, seconds = refs[0:n_team], refs[n_team : 2 * n_team]
    out1, out2, st1, st2 = refs[2 * n_team :]
    spot = place_ref[0]
    for slot in range(n_team):
        st1[spot ^ slot] = firsts[slot][...].astype(F32)
        st2[spot ^ slot] = seconds[slot][...]
    row, col = iota((c, n_team * local), 0), iota((c, n_team * local), 1)
    who = quotient(col, local)
    inner = col - who * local
    band = quotient(inner, plan.per_group)
    wanted = band * plan.stretch + who * plan.per_group + inner - band * plan.per_group
    stacked = st1[...].reshape(n_team * local, r).astype(BF16)
    out1[...] = nn(one_hot(row == wanted), stacked) * scale
    row, col = iota((n_team * plan.piece_pad, r), 0), iota((n_team * plan.piece_pad, r), 1)
    who = quotient(row, plan.piece_pad)
    inner = row - who * plan.piece_pad
    band = quotient(inner, plan.per_group)
    wanted = band * plan.stretch + who * plan.per_group + inner - band * plan.per_group
    stacked = st2[...].reshape(n_team * plan.piece_pad, c)
    out2[...] = tn(stacked, one_hot((inner < plan.piece) & (col == wanted))) * scale


VMEM = pl.BlockSpec(memory_space=pltpu.VMEM)
SMEM = pl.BlockSpec(memory_space=pltpu.SMEM)


def call(kernel, name, out_shape, operands, n_smem=0, scratch=()):
    n = len(operands)
    return pl.pallas_call(
        kernel,
        name=name,
        out_shape=out_shape,
        in_specs=[SMEM] * n_smem + [VMEM] * (n - n_smem),
        out_specs=jax.tree.map(lambda _: VMEM, out_shape),
        scratch_shapes=list(scratch),
        compiler_params=pltpu.CompilerParams(vmem_limit_bytes=48 * 1024 * 1024),
    )(*operands)


def shape(dims, dtype):
    return jax.ShapeDtypeStruct(dims, dtype)


def body(block_input, cotangent, timesteps, owner_map, time_weight, first_weight, second_weight):
    n_rep, n_dom = lax.axis_size("rep"), lax.axis_size("dom")
    height, width, c = block_input.shape[1:]
    plan = Plan(n_rep, n_dom, height, width, c, time_weight.shape[0], first_weight.shape[0])
    team, d, pix = plan.team, n_dom, plan.pixels
    r, local = plan.block_rows, plan.local
    here = lax.axis_index("dom")
    spot = lax.axis_index("rep") % team
    place = jnp.stack([spot, here]).astype(jnp.int32)

    def to_rep(value, step):
        return lax.ppermute(value, "rep", [(i, i ^ step) for i in range(n_rep)])

    def to_dom(value, step):
        if d & (d - 1) == 0:
            return lax.ppermute(value, "dom", [(i, i ^ step) for i in range(d)])
        return lax.ppermute(value, "dom", [(i, (i + step) % d) for i in range(d)])

    def team_gather(value):
        slots = [value] + [None] * (team - 1)
        for step in reversed(range(2, team, 2)):
            slots[step] = to_rep(value, step)
        if team > 1:
            for step in range(0, team, 2):
                slots[step + 1] = to_rep(slots[step], 1)
        return slots

    def dom_gather(value):
        return [value] + [to_dom(value, step) for step in range(1, d)]

    x = block_input.reshape(pix, c)
    cot = cotangent.reshape(pix, c)
    act, s1, s2 = call(
        functools.partial(prep_kernel, plan),
        "prep",
        (
            shape((plan.act_rows, c), BF16),
            shape((local, r), BF16),
            shape((plan.piece_pad, c), BF16),
        ),
        (place, timesteps, x, time_weight.T, first_weight.T, second_weight.T),
        n_smem=2,
    )
    w1s, w2s = dom_gather(s1), dom_gather(s2)
    acts, cots = team_gather(act), team_gather(cot)
    rows = (height + 2) * width
    outs = call(
        functools.partial(main_kernel, plan, team),
        "main",
        (
            shape((team, pix, c), BF16),
            *[shape((local, r), BF16)] * d,
            *[shape((plan.piece_pad, c), BF16)] * d,
        ),
        (place, owner_map, *acts, *cots, *w1s, *w2s),
        n_smem=2,
        scratch=(
            pltpu.VMEM((team, rows, c), BF16),
            pltpu.VMEM((team, rows, c), BF16),
            pltpu.VMEM((team, rows, plan.wide), BF16),
            pltpu.VMEM((d, local, r), F32),
            pltpu.VMEM((d, plan.piece_pad, c), BF16),
            pltpu.VMEM((d, local, r), F32),
        ),
    )
    part, g1s, g2s = outs[0], outs[1 : 1 + d], outs[1 + d :]

    got1 = [g1s[0]] + [to_dom(g1s[k], k) for k in range(1, d)]
    got2 = [g2s[0]] + [to_dom(g2s[k], k) for k in range(1, d)]
    mine = BF16 if n_rep == team else F32
    sum1, sum2 = call(
        functools.partial(sum_kernel, d),
        "owner_sum",
        (shape((local, r), mine), shape((plan.piece_pad, c), mine)),
        tuple(v for pair in zip(got1, got2) for v in pair),
    )
    if n_rep > team:
        same_spot = [[i * team + k for i in range(n_rep // team)] for k in range(team)]
        sum1, sum2 = lax.psum((sum1, sum2), "rep", axis_index_groups=same_spot)
        sum1, sum2 = sum1.astype(BF16), sum2.astype(BF16)
    firsts, seconds = team_gather(sum1), team_gather(sum2)
    first, second = call(
        functools.partial(last_kernel, plan, team, 1.0 / (n_rep * n_dom)),
        "assemble",
        (shape((c, r), F32), shape((c, r), F32)),
        (place, *firsts, *seconds),
        n_smem=1,
        scratch=(
            pltpu.VMEM((team, local, r), F32),
            pltpu.VMEM((team, plan.piece_pad, c), BF16),
        ),
    )

    if team > 1:
        away = part.reshape(team // 2, 2, pix, c)[:, 1]
        half = call(
            functools.partial(pair_kernel, team // 2),
            "pair_sum",
            shape((team // 2, pix, c), BF16),
            (part, to_rep(away, 1)),
        )
        shares = [half[0]] + [to_rep(half[k], 2 * k) for k in range(1, team // 2)]
    else:
        shares = [part[0]]
    output = call(
        functools.partial(out_kernel, len(shares)), "output", shape((pix, c), BF16), (x, *shares)
    )
    return output.reshape(1, height, width, c), first.T, second.T


def solution(mesh):
    placed = (
        P(("rep", "dom"), None, None, None),
        P(("rep", "dom"), None, None, None),
        P(("rep", "dom")),
        P(),
        P(),
        P("dom", None),
        P("dom", None),
    )
    return jax.shard_map(
        body,
        mesh=mesh,
        in_specs=placed,
        out_specs=(P(("rep", "dom"), None, None, None), P("dom", None), P("dom", None)),
        check_vma=False,
    )
```

time: 302 us -> 80.3 us (0.27)
  waiting for transfers between devices: 102 us -> 19.8 us
  blocking collectives: 77 us -> 0 us
  local copies, waits for them, and re-layouts: 47.8 us -> 4.19 us
  starting transfers between devices: 4.68 us -> 42.9 us
  other arithmetic: 27.3 us -> 0.08 us
  matrix products: 15.1 us -> 0 us
  between operations: 15.6 us -> 1.43 us
  Pallas kernels: 0 us -> 11.6 us
  loops' own time: 10.7 us -> 0 us
    all_gather x2 -> x0, blocking collectives: 77 us -> none  [the longest x1 55.2 us: body(): lax.all_gather(conv_grad.reshape(1, HEIGHT, WIDTH, C), 'dom', axis=0, til...]
    psum x1 -> x0, waiting for transfers between devices: 58.7 us -> none  [body(): second_total, first_total = lax.psum((second_owned, total), 'rep')]
    ppermute x0 -> x44, starting transfers between devices: none -> 42.9 us  [the longest x32 22.9 us: to_rep(): return lax.ppermute(value, 'rep', [(i, i ^ step) for i in range(n_rep)])]
    all_gather x2 -> x0, waiting for transfers between devices: 42.4 us -> none  [the longest x1 22 us: body(): second_stored = lax.all_gather(second_weight, 'dom', axis=0, tiled=True)]
    ppermute x0 -> x44, waiting for transfers between devices: none -> 19.8 us  [the longest x12 10.4 us: to_dom(): return lax.ppermute(value, 'dom', [(i, i ^ step) for i in range(d)])]
    reshape x4 -> x0, local copies, waits for them, and re-layouts: 16.6 us -> none  [the longest x2 8.9 us: second_owner_sum(): term_rounded.reshape(group_size, block_rows, C)]
    dot_general x12 -> x0, matrix products: 15.1 us -> none  [the longest x4 5.68 us: add_block(): jnp.dot(columns_taken, block, preferred_element_type=jnp.float32)]
    pallas_call x0 -> x6, Pallas kernels: none -> 11.6 us  [call(): pl.pallas_call(kernel, name=name, out_shape=out_shape, in_specs=[SMEM] *...]
  transfers between devices with their start and end apart: 4 -> 44, of which waited for: 3 -> 13; matrix products, arithmetic and copies ran while one was open for 12% -> 0% of each run, Pallas kernels for 0% -> 4%
where the time goes in v1:
time: 80.3 us; the launch traced here: 80 us
  starting transfers between devices  42.9 us (53%)
  waiting for transfers between devices  19.8 us (25%)
  Pallas kernels  11.6 us (14%)
  local copies, waits for them, and re-layouts  4.19 us (5%)
  between operations  1.43 us (2%)
    ppermute x32, starting transfers between devices, to_rep(): return lax.ppermute(value, 'rep', [(i, i ^ step) for i in range(n_rep)])  22.9 us
    ppermute x12, starting transfers between devices, to_dom(): return lax.ppermute(value, 'dom', [(i, i ^ step) for i in range(d)])  20 us
    pallas_call x6, Pallas kernels, call(): pl.pallas_call(kernel, name=name, out_shape=out_shape, in_specs=[SMEM] *...  11.6 us
    ppermute x12, waiting for transfers between devices, to_dom(): return lax.ppermute(value, 'dom', [(i, i ^ step) for i in range(d)])  10.4 us
    ppermute x32, waiting for transfers between devices, to_rep(): return lax.ppermute(value, 'rep', [(i, i ^ step) for i in range(n_rep)])  9.36 us
    unnamed x14, local copies, waits for them, and re-layouts  4.11 us
  transfers between devices with their start and end apart: 44, of which 13 were waited for; matrix products, arithmetic and copies ran while one was open for 0% of the time, Pallas kernels for 4%

profile of v1, /device:TPU:0, one launch (start us, length us, event | category | flops | bytes accessed | tf_op | source)
XLA Modules:
  0.0 80.0 jit_solution(3064360890085848999)
XLA Ops:
  1.4 1.1 %copy-done = bf16[1280,320]{0,1:T(8,128)(2,1)S(1)} copy-done((bf16[1280,320]{0,1:T(8,128)(2,1)S(1)}, bf16[1280,320]{0,1:T(8,128)(2,1)}, u32[]{:S(2)}) %copy-start) | copy-done | bytes 819224
  2.5 1.0 %copy-done.1 = bf16[720,320]{0,1:T(8,128)(2,1)S(1)} copy-done((bf16[720,320]{0,1:T(8,128)(2,1)S(1)}, bf16[720,320]{0,1:T(8,128)(2,1)}, u32[]{:S(2)}) %copy-start.1) | copy-done | bytes 460824
  3.5 1.0 %copy-done.2 = bf16[720,320]{0,1:T(8,128)(2,1)S(1)} copy-done((bf16[720,320]{0,1:T(8,128)(2,1)S(1)}, bf16[720,320]{0,1:T(8,128)(2,1)}, u32[]{:S(2)}) %copy-start.2) | copy-done | bytes 460824
  4.6 0.9 %copy-done.3 = bf16[1,8,16,320]{3,2,1,0:T(8,128)(2,1)S(1)} copy-done((bf16[1,8,16,320]{3,2,1,0:T(8,128)(2,1)S(1)}, bf16[1,8,16,320]{3,2,1,0:T(8,128)(2,1)}, u32[]{:S(2)}) %copy-start.3) | copy-done | bytes 81944
  5.5 1.7 %prep.1 = (bf16[144,320]{1,0:T(8,128)(2,1)S(1)}, bf16[40,720]{1,0:T(8,128)(2,1)S(1)}, bf16[96,320]{1,0:T(8,128)(2,1)S(1)}) custom-call(s32[2]{0:T(128)S(1)} %pad_add_fusion.place_ref.refs_0_, s32[1]{0:T(128)S(6)} %copy.15.steps_ref, bf16[128,320]{1,0:T(8,128)(2,1)S(1)} %bitcast.27, bf16[320,1280]{1,0:T(8,128)(2,1)S(1)} %bitcast.24, ...), custom_call_target="tpu_custom_call" | custom-call | tf_op jit(solution)/shard_map/prep/pallas_call | solution.py:330
  7.2 5.1 %collective-permute-start.16 = (bf16[40,720]{1,0:T(8,128)(2,1)S(1)}, bf16[40,720]{1,0:T(8,128)(2,1)S(1)}, u32[]{:S(2)}, u32[]{:S(2)}) collective-permute-start(bf16[40,720]{1,0:T(8,128)(2,1)S(1)} %get-tuple-element.20.refs_18_), channel_id=1, source_target_pairs={{0,3},{1,2},{2,1},{3,0},{4,7},{5,6},{6,5},{7,4},{8,11},{9,10},{10,... | collective-permute-start | bytes 172808 | tf_op jit(solution)/shard_map/ppermute | solution.py:360
  12.9 3.7 %collective-permute-start.19 = (bf16[96,320]{1,0:T(8,128)(2,1)S(1)}, bf16[96,320]{1,0:T(8,128)(2,1)S(1)}, u32[]{:S(2)}, u32[]{:S(2)}) collective-permute-start(bf16[96,320]{1,0:T(8,128)(2,1)S(1)} %get-tuple-element.21.refs_22_), channel_id=1, source_target_pairs={{0,3},{1,2},{2,1},{3,0},{4,7},{5,6},{6,5},{7,4},{8,11},{9,10},{10,... | collective-permute-start | bytes 184328 | tf_op jit(solution)/shard_map/ppermute | solution.py:360
  16.7 2.5 %collective-permute-start.12 = (bf16[128,320]{1,0:T(8,128)(2,1)S(1)}, bf16[128,320]{1,0:T(8,128)(2,1)S(1)}, u32[]{:S(2)}, u32[]{:S(2)}) collective-permute-start(bf16[128,320]{1,0:T(8,128)(2,1)S(1)} %bitcast.29), channel_id=1, source_target_pairs={{0,24},{4,28},{8,16},{12,20},{16,8},{20,12},{24,0},{28,4},{1,25},{... | collective-permute-start | bytes 245768 | tf_op jit(solution)/shard_map/ppermute | solution.py:356
  19.2 2.1 %collective-permute-done.15.refs_20_ = bf16[40,720]{1,0:T(8,128)(2,1)S(1)} collective-permute-done((bf16[40,720]{1,0:T(8,128)(2,1)S(1)}, bf16[40,720]{1,0:T(8,128)(2,1)S(1)}, u32[]{:S(2)}, u32[]{:S(2)}) %collective-permute-start.15) | collective-permute-done | bytes 57632 | tf_op jit(solution)/shard_map/ppermute | solution.py:360
  21.3 1.5 %collective-permute-start.10 = (bf16[128,320]{1,0:T(8,128)(2,1)S(1)}, bf16[128,320]{1,0:T(8,128)(2,1)S(1)}, u32[]{:S(2)}, u32[]{:S(2)}) collective-permute-start(bf16[128,320]{1,0:T(8,128)(2,1)S(1)} %bitcast.30), channel_id=1, source_target_pairs={{0,16},{4,20},{8,24},{12,28},{16,0},{20,4},{24,8},{28,12},{1,17},{... | collective-permute-start | bytes 245768 | tf_op jit(solution)/shard_map/ppermute | solution.py:356
  22.8 1.5 %collective-permute-start.8 = (bf16[128,320]{1,0:T(8,128)(2,1)S(1)}, bf16[128,320]{1,0:T(8,128)(2,1)S(1)}, u32[]{:S(2)}, u32[]{:S(2)}) collective-permute-start(bf16[128,320]{1,0:T(8,128)(2,1)S(1)} %bitcast.31), channel_id=1, source_target_pairs={{0,8},{4,12},{8,0},{12,4},{16,24},{20,28},{24,16},{28,20},{1,9},{5... | collective-permute-start | bytes 245768 | tf_op jit(solution)/shard_map/ppermute | solution.py:356
  24.4 4.3 %collective-permute-done.17.refs_23_ = bf16[96,320]{1,0:T(8,128)(2,1)S(1)} collective-permute-done((bf16[96,320]{1,0:T(8,128)(2,1)S(1)}, bf16[96,320]{1,0:T(8,128)(2,1)S(1)}, u32[]{:S(2)}, u32[]{:S(2)}) %collective-permute-start.17) | collective-permute-done | bytes 61472 | tf_op jit(solution)/shard_map/ppermute | solution.py:360
  29.1 1.5 %collective-permute-start.3 = (bf16[144,320]{1,0:T(8,128)(2,1)S(1)}, bf16[144,320]{1,0:T(8,128)(2,1)S(1)}, u32[]{:S(2)}, u32[]{:S(2)}) collective-permute-start(bf16[144,320]{1,0:T(8,128)(2,1)S(1)} %get-tuple-element.19.refs_2_), channel_id=1, source_target_pairs={{0,16},{4,20},{8,24},{12,28},{16,0},{20,4},{24,8},{28,12},{1,17},{... | collective-permute-start | bytes 276488 | tf_op jit(solution)/shard_map/ppermute | solution.py:356
  30.6 1.5 %collective-permute-start.1 = (bf16[144,320]{1,0:T(8,128)(2,1)S(1)}, bf16[144,320]{1,0:T(8,128)(2,1)S(1)}, u32[]{:S(2)}, u32[]{:S(2)}) collective-permute-start(bf16[144,320]{1,0:T(8,128)(2,1)S(1)} %get-tuple-element.19.refs_2_), channel_id=1, source_target_pairs={{0,8},{4,12},{8,0},{12,4},{16,24},{20,28},{24,16},{28,20},{1,9},{5... | collective-permute-start | bytes 276488 | tf_op jit(solution)/shard_map/ppermute | solution.py:356
  32.6 1.7 %collective-permute-done.5.refs_8_ = bf16[144,320]{1,0:T(8,128)(2,1)S(1)} collective-permute-done((bf16[144,320]{1,0:T(8,128)(2,1)S(1)}, bf16[144,320]{1,0:T(8,128)(2,1)S(1)}, u32[]{:S(2)}, u32[]{:S(2)}) %collective-permute-start.5) | collective-permute-done | bytes 92192 | tf_op jit(solution)/shard_map/ppermute | solution.py:356
  36.1 0.8 collective-permute-done.11.refs_15_
  37.2 6.4 %main.1 = (bf16[8,128,320]{2,1,0:T(8,128)(2,1)S(1)}, bf16[40,720]{1,0:T(8,128)(2,1)S(1)}, bf16[40,720]{1,0:T(8,128)(2,1)S(1)}, bf16[40,720]{1,0:T(8,128)(2,1)S(1...) custom-call(s32[2]{0:T(128)S(1)} %pad_add_fusion.place_ref.refs_0_, ...), custom_call_target="tpu_custom_call" | custom-call | tf_op jit(solution)/shard_map/main/pallas_call | solution.py:330
  44.3 3.0 %collective-permute-start.26 = (bf16[40,720]{1,0:T(8,128)(2,1)S(1)}, bf16[40,720]{1,0:T(8,128)(2,1)S(1)}, u32[]{:S(2)}, u32[]{:S(2)}) collective-permute-start(bf16[40,720]{1,0:T(8,128)(2,1)S(1)} %get-tuple-element.27), channel_id=1, source_target_pairs={{0,2},{1,3},{2,0},{3,1},{4,6},{5,7},{6,4},{7,5},{8,10},{9,11},{10,... | collective-permute-start | bytes 172808 | tf_op jit(solution)/shard_map/ppermute | solution.py:360
  47.8 1.1 %collective-permute-start.27 = (bf16[96,320]{1,0:T(8,128)(2,1)S(1)}, bf16[96,320]{1,0:T(8,128)(2,1)S(1)}, u32[]{:S(2)}, u32[]{:S(2)}) collective-permute-start(bf16[96,320]{1,0:T(8,128)(2,1)S(1)} %get-tuple-element.28), channel_id=1, source_target_pairs={{0,2},{1,3},{2,0},{3,1},{4,6},{5,7},{6,4},{7,5},{8,10},{9,11},{10,... | collective-permute-start | bytes 184328 | tf_op jit(solution)/shard_map/ppermute | solution.py:360
  48.9 3.4 %collective-permute-start.29 = (bf16[96,320]{1,0:T(8,128)(2,1)S(1)}, bf16[96,320]{1,0:T(8,128)(2,1)S(1)}, u32[]{:S(2)}, u32[]{:S(2)}) collective-permute-start(bf16[96,320]{1,0:T(8,128)(2,1)S(1)} %get-tuple-element.30), channel_id=1, source_target_pairs={{0,3},{1,2},{2,1},{3,0},{4,7},{5,6},{6,5},{7,4},{8,11},{9,10},{10,... | collective-permute-start | bytes 184328 | tf_op jit(solution)/shard_map/ppermute | solution.py:360
  52.3 2.1 %collective-permute-start.28 = (bf16[40,720]{1,0:T(8,128)(2,1)S(1)}, bf16[40,720]{1,0:T(8,128)(2,1)S(1)}, u32[]{:S(2)}, u32[]{:S(2)}) collective-permute-start(bf16[40,720]{1,0:T(8,128)(2,1)S(1)} %get-tuple-element.29), channel_id=1, source_target_pairs={{0,3},{1,2},{2,1},{3,0},{4,7},{5,6},{6,5},{7,4},{8,11},{9,10},{10,... | collective-permute-start | bytes 172808 | tf_op jit(solution)/shard_map/ppermute | solution.py:360
  54.4 4.1 %collective-permute-done.28.refs_6_ = bf16[40,720]{1,0:T(8,128)(2,1)S(1)} collective-permute-done((bf16[40,720]{1,0:T(8,128)(2,1)S(1)}, bf16[40,720]{1,0:T(8,128)(2,1)S(1)}, u32[]{:S(2)}, u32[]{:S(2)}) %collective-permute-start.28) | collective-permute-done | bytes 57632 | tf_op jit(solution)/shard_map/ppermute | solution.py:360
  58.5 1.3 %collective-permute-start.35 = (bf16[40,720]{1,0:T(8,128)(2,1)S(1)}, bf16[40,720]{1,0:T(8,128)(2,1)S(1)}, u32[]{:S(2)}, u32[]{:S(2)}) collective-permute-start(bf16[40,720]{1,0:T(8,128)(2,1)S(1)} %get-tuple-element.31.refs_0_), channel_id=1, source_target_pairs={{0,24},{4,28},{8,16},{12,20},{16,8},{20,12},{24,0},{28,4},{1,25},{... | collective-permute-start | bytes 172808 | tf_op jit(solution)/shard_map/ppermute | solution.py:356
  59.8 2.1 %collective-permute-start.33 = (bf16[40,720]{1,0:T(8,128)(2,1)S(1)}, bf16[40,720]{1,0:T(8,128)(2,1)S(1)}, u32[]{:S(2)}, u32[]{:S(2)}) collective-permute-start(bf16[40,720]{1,0:T(8,128)(2,1)S(1)} %get-tuple-element.31.refs_0_), channel_id=1, source_target_pairs={{0,16},{4,20},{8,24},{12,28},{16,0},{20,4},{24,8},{28,12},{1,17},{... | collective-permute-start | bytes 172808 | tf_op jit(solution)/shard_map/ppermute | solution.py:356
  62.4 1.2 %collective-permute-start.40 = (bf16[96,320]{1,0:T(8,128)(2,1)S(1)}, bf16[96,320]{1,0:T(8,128)(2,1)S(1)}, u32[]{:S(2)}, u32[]{:S(2)}) collective-permute-start(bf16[96,320]{1,0:T(8,128)(2,1)S(1)} %get-tuple-element.32.refs_8_), channel_id=1, source_target_pairs={{0,16},{4,20},{8,24},{12,28},{16,0},{20,4},{24,8},{28,12},{1,17},{... | collective-permute-start | bytes 184328 | tf_op jit(solution)/shard_map/ppermute | solution.py:356
  63.9 2.2 %collective-permute-start.38 = (bf16[96,320]{1,0:T(8,128)(2,1)S(1)}, bf16[96,320]{1,0:T(8,128)(2,1)S(1)}, u32[]{:S(2)}, u32[]{:S(2)}) collective-permute-start(bf16[96,320]{1,0:T(8,128)(2,1)S(1)} %get-tuple-element.32.refs_8_), channel_id=1, source_target_pairs={{0,8},{4,12},{8,0},{12,4},{16,24},{20,28},{24,16},{28,20},{1,9},{5... | collective-permute-start | bytes 184328 | tf_op jit(solution)/shard_map/ppermute | solution.py:356
  66.3 4.0 %collective-permute-done.31.refs_2_ = bf16[40,720]{1,0:T(8,128)(2,1)S(1)} collective-permute-done((bf16[40,720]{1,0:T(8,128)(2,1)S(1)}, bf16[40,720]{1,0:T(8,128)(2,1)S(1)}, u32[]{:S(2)}, u32[]{:S(2)}) %collective-permute-start.31) | collective-permute-done | bytes 57632 | tf_op jit(solution)/shard_map/ppermute | solution.py:356
  71.9 2.0 %collective-permute-start.22 = (bf16[128,320]{1,0:T(8,128)(2,1)S(1)}, bf16[128,320]{1,0:T(8,128)(2,1)S(1)}, u32[]{:S(2)}, u32[]{:S(2)}) collective-permute-start(bf16[128,320]{1,0:T(8,128)(2,1)S(1)} %get-tuple-element.36), channel_id=1, source_target_pairs={{0,16},{4,20},{8,24},{12,28},{16,0},{20,4},{24,8},{28,12},{1,17},{... | collective-permute-start | bytes 245768 | tf_op jit(solution)/shard_map/ppermute | solution.py:356
  73.9 1.2 %collective-permute-start.21 = (bf16[128,320]{1,0:T(8,128)(2,1)S(1)}, bf16[128,320]{1,0:T(8,128)(2,1)S(1)}, u32[]{:S(2)}, u32[]{:S(2)}) collective-permute-start(bf16[128,320]{1,0:T(8,128)(2,1)S(1)} %get-tuple-element.37), channel_id=1, source_target_pairs={{0,8},{4,12},{8,0},{12,4},{16,24},{20,28},{24,16},{28,20},{1,9},{5... | collective-permute-start | bytes 245768 | tf_op jit(solution)/shard_map/ppermute | solution.py:356
  75.6 0.8 collective-permute-done.41.refs_13_
  76.5 2.7 %assemble.1 = (f32[320,720]{1,0:T(8,128)}, f32[320,720]{1,0:T(8,128)}) custom-call(s32[2]{0:T(128)S(1)} %pad_add_fusion.place_ref.refs_0_, bf16[40,720]{1,0:T(8,128)(2,1)S(1)} %get-tuple-element.31.refs_0_, bf16[40,720]{1,0:T(8,128)(2,1)S(1)} %collective-permute-done.30.refs_1_, bf16[40,720]{1,0:T(8,128)(2,1)S(1)} %collective-permute-done.31.refs_2_, ...), custom_call_target="tpu_custom_call" | custom-call | tf_op jit(solution)/shard_map/assemble/pallas_call | solution.py:330
  79.2 0.7 output.1
  (79 shorter events, 8.3 us)
Async XLA Ops:
  7.2 9.5 %collective-permute-start.16 = (bf16[40,720]{1,0:T(8,128)(2,1)S(1)}, bf16[40,720]{1,0:T(8,128)(2,1)S(1)}, u32[]{:S(2)}, u32[]{:S(2)}) collective-permute-start(bf16[40,720]{1,0:T(8,128)(2,1)S(1)} %get-tuple-element.20.refs_18_), channel_id=1, source_target_pairs={{0,3},{1,2},{2,1},{3,0},{4,7},{5,6},{6,5},{7,4},{8,11},{9,10},{10,... | collective-permute-start | bytes 172808 | tf_op jit(solution)/shard_map/ppermute | solution.py:360
  12.3 9.0 %collective-permute-start.15 = (bf16[40,720]{1,0:T(8,128)(2,1)S(1)}, bf16[40,720]{1,0:T(8,128)(2,1)S(1)}, u32[]{:S(2)}, u32[]{:S(2)}) collective-permute-start(bf16[40,720]{1,0:T(8,128)(2,1)S(1)} %get-tuple-element.20.refs_18_), channel_id=1, source_target_pairs={{0,2},{1,3},{2,0},{3,1},{4,6},{5,7},{6,4},{7,5},{8,10},{9,11},{10,... | collective-permute-start | bytes 172808 | tf_op jit(solution)/shard_map/ppermute | solution.py:360
  12.3 10.5 %collective-permute-start.14 = (bf16[40,720]{1,0:T(8,128)(2,1)S(1)}, bf16[40,720]{1,0:T(8,128)(2,1)S(1)}, u32[]{:S(2)}, u32[]{:S(2)}) collective-permute-start(bf16[40,720]{1,0:T(8,128)(2,1)S(1)} %get-tuple-element.20.refs_18_), channel_id=1, source_target_pairs={{0,1},{1,0},{2,3},{3,2},{4,5},{5,4},{6,7},{7,6},{8,9},{9,8},{10,11... | collective-permute-start | bytes 172808 | tf_op jit(solution)/shard_map/ppermute | solution.py:360
  12.9 11.4 %collective-permute-start.19 = (bf16[96,320]{1,0:T(8,128)(2,1)S(1)}, bf16[96,320]{1,0:T(8,128)(2,1)S(1)}, u32[]{:S(2)}, u32[]{:S(2)}) collective-permute-start(bf16[96,320]{1,0:T(8,128)(2,1)S(1)} %get-tuple-element.21.refs_22_), channel_id=1, source_target_pairs={{0,3},{1,2},{2,1},{3,0},{4,7},{5,6},{6,5},{7,4},{8,11},{9,10},{10,... | collective-permute-start | bytes 184328 | tf_op jit(solution)/shard_map/ppermute | solution.py:360
  16.7 7.6 %collective-permute-start.18 = (bf16[96,320]{1,0:T(8,128)(2,1)S(1)}, bf16[96,320]{1,0:T(8,128)(2,1)S(1)}, u32[]{:S(2)}, u32[]{:S(2)}) collective-permute-start(bf16[96,320]{1,0:T(8,128)(2,1)S(1)} %get-tuple-element.21.refs_22_), channel_id=1, source_target_pairs={{0,2},{1,3},{2,0},{3,1},{4,6},{5,7},{6,4},{7,5},{8,10},{9,11},{10,... | collective-permute-start | bytes 184328 | tf_op jit(solution)/shard_map/ppermute | solution.py:360
  16.7 12.4 %collective-permute-start.12 = (bf16[128,320]{1,0:T(8,128)(2,1)S(1)}, bf16[128,320]{1,0:T(8,128)(2,1)S(1)}, u32[]{:S(2)}, u32[]{:S(2)}) collective-permute-start(bf16[128,320]{1,0:T(8,128)(2,1)S(1)} %bitcast.29), channel_id=1, source_target_pairs={{0,24},{4,28},{8,16},{12,20},{16,8},{20,12},{24,0},{28,4},{1,25},{... | collective-permute-start | bytes 245768 | tf_op jit(solution)/shard_map/ppermute | solution.py:356
  21.3 9.4 %collective-permute-start.10 = (bf16[128,320]{1,0:T(8,128)(2,1)S(1)}, bf16[128,320]{1,0:T(8,128)(2,1)S(1)}, u32[]{:S(2)}, u32[]{:S(2)}) collective-permute-start(bf16[128,320]{1,0:T(8,128)(2,1)S(1)} %bitcast.30), channel_id=1, source_target_pairs={{0,16},{4,20},{8,24},{12,28},{16,0},{20,4},{24,8},{28,12},{1,17},{... | collective-permute-start | bytes 245768 | tf_op jit(solution)/shard_map/ppermute | solution.py:356
  22.8 9.3 %collective-permute-start.8 = (bf16[128,320]{1,0:T(8,128)(2,1)S(1)}, bf16[128,320]{1,0:T(8,128)(2,1)S(1)}, u32[]{:S(2)}, u32[]{:S(2)}) collective-permute-start(bf16[128,320]{1,0:T(8,128)(2,1)S(1)} %bitcast.31), channel_id=1, source_target_pairs={{0,8},{4,12},{8,0},{12,4},{16,24},{20,28},{24,16},{28,20},{1,9},{5... | collective-permute-start | bytes 245768 | tf_op jit(solution)/shard_map/ppermute | solution.py:356
  24.3 4.4 %collective-permute-start.17 = (bf16[96,320]{1,0:T(8,128)(2,1)S(1)}, bf16[96,320]{1,0:T(8,128)(2,1)S(1)}, u32[]{:S(2)}, u32[]{:S(2)}) collective-permute-start(bf16[96,320]{1,0:T(8,128)(2,1)S(1)} %get-tuple-element.21.refs_22_), channel_id=1, source_target_pairs={{0,1},{1,0},{2,3},{3,2},{4,5},{5,4},{6,7},{7,6},{8,9},{9,8},{10,11... | collective-permute-start | bytes 184328 | tf_op jit(solution)/shard_map/ppermute | solution.py:360
  24.3 7.9 %collective-permute-start.7 = (bf16[128,320]{1,0:T(8,128)(2,1)S(1)}, bf16[128,320]{1,0:T(8,128)(2,1)S(1)}, u32[]{:S(2)}, u32[]{:S(2)}) collective-permute-start(bf16[128,320]{1,0:T(8,128)(2,1)S(1)} %bitcast.32), channel_id=1, source_target_pairs={{0,4},{4,0},{8,12},{12,8},{16,20},{20,16},{24,28},{28,24},{1,5},{5... | collective-permute-start | bytes 245768 | tf_op jit(solution)/shard_map/ppermute | solution.py:356
  28.6 5.8 %collective-permute-start.5 = (bf16[144,320]{1,0:T(8,128)(2,1)S(1)}, bf16[144,320]{1,0:T(8,128)(2,1)S(1)}, u32[]{:S(2)}, u32[]{:S(2)}) collective-permute-start(bf16[144,320]{1,0:T(8,128)(2,1)S(1)} %get-tuple-element.19.refs_2_), channel_id=1, source_target_pairs={{0,24},{4,28},{8,16},{12,20},{16,8},{20,12},{24,0},{28,4},{1,25},{... | collective-permute-start | bytes 276488 | tf_op jit(solution)/shard_map/ppermute | solution.py:356
  29.1 5.9 %collective-permute-start.3 = (bf16[144,320]{1,0:T(8,128)(2,1)S(1)}, bf16[144,320]{1,0:T(8,128)(2,1)S(1)}, u32[]{:S(2)}, u32[]{:S(2)}) collective-permute-start(bf16[144,320]{1,0:T(8,128)(2,1)S(1)} %get-tuple-element.19.refs_2_), channel_id=1, source_target_pairs={{0,16},{4,20},{8,24},{12,28},{16,0},{20,4},{24,8},{28,12},{1,17},{... | collective-permute-start | bytes 276488 | tf_op jit(solution)/shard_map/ppermute | solution.py:356
  30.6 4.7 %collective-permute-start.1 = (bf16[144,320]{1,0:T(8,128)(2,1)S(1)}, bf16[144,320]{1,0:T(8,128)(2,1)S(1)}, u32[]{:S(2)}, u32[]{:S(2)}) collective-permute-start(bf16[144,320]{1,0:T(8,128)(2,1)S(1)} %get-tuple-element.19.refs_2_), channel_id=1, source_target_pairs={{0,8},{4,12},{8,0},{12,4},{16,24},{20,28},{24,16},{28,20},{1,9},{5... | collective-permute-start | bytes 276488 | tf_op jit(solution)/shard_map/ppermute | solution.py:356
  32.1 3.8 %collective-permute-start.13 = (bf16[128,320]{1,0:T(8,128)(2,1)S(1)}, bf16[128,320]{1,0:T(8,128)(2,1)S(1)}, u32[]{:S(2)}, u32[]{:S(2)}) collective-permute-start(bf16[128,320]{1,0:T(8,128)(2,1)S(1)} %collective-permute-done.12.refs_16_), channel_id=1, source_target_pairs={{0,4},{4,0},{8,12},{12,8},{16,20},{20,16},{24,28},{28,24},{1,5},{5... | collective-permute-start | bytes 245768 | tf_op jit(solution)/shard_map/ppermute | solution.py:356
  43.7 22.5 %collective-permute-start.20 = (bf16[4,128,320]{2,1,0:T(8,128)(2,1)S(1)}, bf16[4,128,320]{2,1,0:T(8,128)(2,1)S(1)}, u32[]{:S(2)}, u32[]{:S(2)}) collective-permute-start(bf16[4,128,320]{2,1,0:T(8,128)(2,1)S(1)} %slice_bitcast_fusion), channel_id=1, source_target_pairs={{0,4},{4,0},{8,12},{12,8},{16,20},{20,16},{24,28},{28,24},{1,5},{5... | collective-permute-start | bytes 983048 | tf_op jit(solution)/shard_map/ppermute | solution.py:356
  43.9 5.0 %collective-permute-start.24 = (bf16[40,720]{1,0:T(8,128)(2,1)S(1)}, bf16[40,720]{1,0:T(8,128)(2,1)S(1)}, u32[]{:S(2)}, u32[]{:S(2)}) collective-permute-start(bf16[40,720]{1,0:T(8,128)(2,1)S(1)} %get-tuple-element.25), channel_id=1, source_target_pairs={{0,1},{1,0},{2,3},{3,2},{4,5},{5,4},{6,7},{7,6},{8,9},{9,8},{10,11... | collective-permute-start | bytes 172808 | tf_op jit(solution)/shard_map/ppermute | solution.py:360
  44.3 8.0 %collective-permute-start.26 = (bf16[40,720]{1,0:T(8,128)(2,1)S(1)}, bf16[40,720]{1,0:T(8,128)(2,1)S(1)}, u32[]{:S(2)}, u32[]{:S(2)}) collective-permute-start(bf16[40,720]{1,0:T(8,128)(2,1)S(1)} %get-tuple-element.27), channel_id=1, source_target_pairs={{0,2},{1,3},{2,0},{3,1},{4,6},{5,7},{6,4},{7,5},{8,10},{9,11},{10,... | collective-permute-start | bytes 172808 | tf_op jit(solution)/shard_map/ppermute | solution.py:360
  47.3 11.1 %collective-permute-start.25 = (bf16[96,320]{1,0:T(8,128)(2,1)S(1)}, bf16[96,320]{1,0:T(8,128)(2,1)S(1)}, u32[]{:S(2)}, u32[]{:S(2)}) collective-permute-start(bf16[96,320]{1,0:T(8,128)(2,1)S(1)} %get-tuple-element.26), channel_id=1, source_target_pairs={{0,1},{1,0},{2,3},{3,2},{4,5},{5,4},{6,7},{7,6},{8,9},{9,8},{10,11... | collective-permute-start | bytes 184328 | tf_op jit(solution)/shard_map/ppermute | solution.py:360
  47.8 10.7 %collective-permute-start.27 = (bf16[96,320]{1,0:T(8,128)(2,1)S(1)}, bf16[96,320]{1,0:T(8,128)(2,1)S(1)}, u32[]{:S(2)}, u32[]{:S(2)}) collective-permute-start(bf16[96,320]{1,0:T(8,128)(2,1)S(1)} %get-tuple-element.28), channel_id=1, source_target_pairs={{0,2},{1,3},{2,0},{3,1},{4,6},{5,7},{6,4},{7,5},{8,10},{9,11},{10,... | collective-permute-start | bytes 184328 | tf_op jit(solution)/shard_map/ppermute | solution.py:360
  48.9 9.6 %collective-permute-start.29 = (bf16[96,320]{1,0:T(8,128)(2,1)S(1)}, bf16[96,320]{1,0:T(8,128)(2,1)S(1)}, u32[]{:S(2)}, u32[]{:S(2)}) collective-permute-start(bf16[96,320]{1,0:T(8,128)(2,1)S(1)} %get-tuple-element.30), channel_id=1, source_target_pairs={{0,3},{1,2},{2,1},{3,0},{4,7},{5,6},{6,5},{7,4},{8,11},{9,10},{10,... | collective-permute-start | bytes 184328 | tf_op jit(solution)/shard_map/ppermute | solution.py:360
  52.3 6.1 %collective-permute-start.28 = (bf16[40,720]{1,0:T(8,128)(2,1)S(1)}, bf16[40,720]{1,0:T(8,128)(2,1)S(1)}, u32[]{:S(2)}, u32[]{:S(2)}) collective-permute-start(bf16[40,720]{1,0:T(8,128)(2,1)S(1)} %get-tuple-element.29), channel_id=1, source_target_pairs={{0,3},{1,2},{2,1},{3,0},{4,7},{5,6},{6,5},{7,4},{8,11},{9,10},{10,... | collective-permute-start | bytes 172808 | tf_op jit(solution)/shard_map/ppermute | solution.py:360
  58.5 5.4 %collective-permute-start.35 = (bf16[40,720]{1,0:T(8,128)(2,1)S(1)}, bf16[40,720]{1,0:T(8,128)(2,1)S(1)}, u32[]{:S(2)}, u32[]{:S(2)}) collective-permute-start(bf16[40,720]{1,0:T(8,128)(2,1)S(1)} %get-tuple-element.31.refs_0_), channel_id=1, source_target_pairs={{0,24},{4,28},{8,16},{12,20},{16,8},{20,12},{24,0},{28,4},{1,25},{... | collective-permute-start | bytes 172808 | tf_op jit(solution)/shard_map/ppermute | solution.py:356
  59.8 6.3 %collective-permute-start.33 = (bf16[40,720]{1,0:T(8,128)(2,1)S(1)}, bf16[40,720]{1,0:T(8,128)(2,1)S(1)}, u32[]{:S(2)}, u32[]{:S(2)}) collective-permute-start(bf16[40,720]{1,0:T(8,128)(2,1)S(1)} %get-tuple-element.31.refs_0_), channel_id=1, source_target_pairs={{0,16},{4,20},{8,24},{12,28},{16,0},{20,4},{24,8},{28,12},{1,17},{... | collective-permute-start | bytes 172808 | tf_op jit(solution)/shard_map/ppermute | solution.py:356
  61.9 9.0 %collective-permute-start.42 = (bf16[96,320]{1,0:T(8,128)(2,1)S(1)}, bf16[96,320]{1,0:T(8,128)(2,1)S(1)}, u32[]{:S(2)}, u32[]{:S(2)}) collective-permute-start(bf16[96,320]{1,0:T(8,128)(2,1)S(1)} %get-tuple-element.32.refs_8_), channel_id=1, source_target_pairs={{0,24},{4,28},{8,16},{12,20},{16,8},{20,12},{24,0},{28,4},{1,25},{... | collective-permute-start | bytes 184328 | tf_op jit(solution)/shard_map/ppermute | solution.py:356
  62.4 8.6 %collective-permute-start.40 = (bf16[96,320]{1,0:T(8,128)(2,1)S(1)}, bf16[96,320]{1,0:T(8,128)(2,1)S(1)}, u32[]{:S(2)}, u32[]{:S(2)}) collective-permute-start(bf16[96,320]{1,0:T(8,128)(2,1)S(1)} %get-tuple-element.32.refs_8_), channel_id=1, source_target_pairs={{0,16},{4,20},{8,24},{12,28},{16,0},{20,4},{24,8},{28,12},{1,17},{... | collective-permute-start | bytes 184328 | tf_op jit(solution)/shard_map/ppermute | solution.py:356
  63.9 7.5 %collective-permute-start.38 = (bf16[96,320]{1,0:T(8,128)(2,1)S(1)}, bf16[96,320]{1,0:T(8,128)(2,1)S(1)}, u32[]{:S(2)}, u32[]{:S(2)}) collective-permute-start(bf16[96,320]{1,0:T(8,128)(2,1)S(1)} %get-tuple-element.32.refs_8_), channel_id=1, source_target_pairs={{0,8},{4,12},{8,0},{12,4},{16,24},{20,28},{24,16},{28,20},{1,9},{5... | collective-permute-start | bytes 184328 | tf_op jit(solution)/shard_map/ppermute | solution.py:356
  66.1 4.2 %collective-permute-start.31 = (bf16[40,720]{1,0:T(8,128)(2,1)S(1)}, bf16[40,720]{1,0:T(8,128)(2,1)S(1)}, u32[]{:S(2)}, u32[]{:S(2)}) collective-permute-start(bf16[40,720]{1,0:T(8,128)(2,1)S(1)} %get-tuple-element.31.refs_0_), channel_id=1, source_target_pairs={{0,8},{4,12},{8,0},{12,4},{16,24},{20,28},{24,16},{28,20},{1,9},{5... | collective-permute-start | bytes 172808 | tf_op jit(solution)/shard_map/ppermute | solution.py:356
  66.2 4.2 %collective-permute-start.30 = (bf16[40,720]{1,0:T(8,128)(2,1)S(1)}, bf16[40,720]{1,0:T(8,128)(2,1)S(1)}, u32[]{:S(2)}, u32[]{:S(2)}) collective-permute-start(bf16[40,720]{1,0:T(8,128)(2,1)S(1)} %get-tuple-element.31.refs_0_), channel_id=1, source_target_pairs={{0,4},{4,0},{8,12},{12,8},{16,20},{20,16},{24,28},{28,24},{1,5},{5... | collective-permute-start | bytes 172808 | tf_op jit(solution)/shard_map/ppermute | solution.py:356
  70.9 4.2 %collective-permute-start.32 = (bf16[40,720]{1,0:T(8,128)(2,1)S(1)}, bf16[40,720]{1,0:T(8,128)(2,1)S(1)}, u32[]{:S(2)}, u32[]{:S(2)}) collective-permute-start(bf16[40,720]{1,0:T(8,128)(2,1)S(1)} %collective-permute-done.31.refs_2_), channel_id=1, source_target_pairs={{0,4},{4,0},{8,12},{12,8},{16,20},{20,16},{24,28},{28,24},{1,5},{5... | collective-permute-start | bytes 172808 | tf_op jit(solution)/shard_map/ppermute | solution.py:356
  71.6 7.6 %collective-permute-start.23 = (bf16[128,320]{1,0:T(8,128)(2,1)S(1)}, bf16[128,320]{1,0:T(8,128)(2,1)S(1)}, u32[]{:S(2)}, u32[]{:S(2)}) collective-permute-start(bf16[128,320]{1,0:T(8,128)(2,1)S(1)} %get-tuple-element.35), channel_id=1, source_target_pairs={{0,24},{4,28},{8,16},{12,20},{16,8},{20,12},{24,0},{28,4},{1,25},{... | collective-permute-start | bytes 245768 | tf_op jit(solution)/shard_map/ppermute | solution.py:356
  71.9 7.3 %collective-permute-start.22 = (bf16[128,320]{1,0:T(8,128)(2,1)S(1)}, bf16[128,320]{1,0:T(8,128)(2,1)S(1)}, u32[]{:S(2)}, u32[]{:S(2)}) collective-permute-start(bf16[128,320]{1,0:T(8,128)(2,1)S(1)} %get-tuple-element.36), channel_id=1, source_target_pairs={{0,16},{4,20},{8,24},{12,28},{16,0},{20,4},{24,8},{28,12},{1,17},{... | collective-permute-start | bytes 245768 | tf_op jit(solution)/shard_map/ppermute | solution.py:356
  73.9 5.4 %collective-permute-start.21 = (bf16[128,320]{1,0:T(8,128)(2,1)S(1)}, bf16[128,320]{1,0:T(8,128)(2,1)S(1)}, u32[]{:S(2)}, u32[]{:S(2)}) collective-permute-start(bf16[128,320]{1,0:T(8,128)(2,1)S(1)} %get-tuple-element.37), channel_id=1, source_target_pairs={{0,8},{4,12},{8,0},{12,4},{16,24},{20,28},{24,16},{28,20},{1,9},{5... | collective-permute-start | bytes 245768 | tf_op jit(solution)/shard_map/ppermute | solution.py:356
  (19 other events, 66.3 us)

commit v2 on v1

v2 whole, which is shorter than its diff:
```python
import functools
import math

import jax
import jax.numpy as jnp
from jax import lax
from jax.experimental import pallas as pl
from jax.experimental.pallas import tpu as pltpu
from jax.sharding import PartitionSpec as P

GROUPS = 32
NORM_EPS = 1e-05
F32 = jnp.float32
BF16 = jnp.bfloat16
HIGHEST = lax.Precision.HIGHEST


def round_up(value, unit):
    return -(-value // unit) * unit


def nn(a, b, precision=None):
    return lax.dot_general(
        a, b, (((1,), (0,)), ((), ())), precision=precision, preferred_element_type=F32
    )


def nt(a, b):
    return lax.dot_general(a, b, (((1,), (1,)), ((), ())), preferred_element_type=F32)


def tn(a, b):
    return lax.dot_general(a, b, (((0,), (0,)), ((), ())), preferred_element_type=F32)


def iota(shape, axis):
    return lax.broadcasted_iota(jnp.int32, shape, axis)


def quotient(value, unit):
    return jnp.floor((value.astype(F32) + 0.5) * (1.0 / unit)).astype(jnp.int32)


def one_hot(hit):
    return jnp.where(hit, 1.0, 0.0).astype(BF16)


def silu(value):
    return value / (1.0 + jnp.exp(-value))


class Plan:
    def __init__(self, n_rep, n_dom, height, width, channels, embed, block_rows):
        if n_dom < 2 or n_dom & (n_dom - 1):
            raise ValueError("dom size")
        self.n_rep, self.n_dom = n_rep, n_dom
        self.height, self.width, self.channels = height, width, channels
        self.embed, self.block_rows = embed, block_rows
        self.pixels = height * width
        self.per_group = channels // GROUPS
        team = 1
        while (
            n_rep % (2 * team) == 0
            and GROUPS % (2 * team) == 0
            and block_rows % (2 * team * self.per_group) == 0
        ):
            team *= 2
        self.team = team
        self.local = channels // team
        self.stretch = self.per_group * team
        self.stretches = block_rows // self.stretch
        self.quarters = channels // self.stretch
        self.piece = self.stretches * self.per_group
        self.piece_pad = round_up(self.piece, 16)
        self.wide = round_up(3 * self.local, 128)
        self.act_rows = self.pixels + 16
        self.head = channels // 128 * 128
        self.packed = 2 * channels
        more = block_rows - self.packed
        if more > 0:
            self.first_rows = self.local + folded_rows(self, self.local, more)
        else:
            self.first_rows = folded_rows(self, self.local, block_rows)
        self.first_rows = round_up(self.first_rows, 16)
        self.second_rows = round_up(folded_rows(self, self.piece_pad, channels), 16)


def own_spot(plan):
    return lax.rem(lax.axis_index("rep"), plan.team)


def logical_of(plan, owner_ref, holder):
    total = 0
    for block in range(plan.n_dom):
        total = total + jnp.where(owner_ref[block] == holder, block, 0)
    return total


def group_matrix(plan, lanes, channels):
    row, col = iota((lanes, lanes), 0), iota((lanes, lanes), 1)
    same = quotient(row, plan.per_group) == quotient(col, plan.per_group)
    return jnp.where(same & (row < channels) & (col < channels), 1.0, 0.0)


def fold(plan, value):
    rows, lanes = value.shape
    fits = plan.packed // lanes
    chunk = round_up(-(-rows // fits), 8)
    if chunk * fits > rows:
        value = jnp.concatenate([value, jnp.zeros((chunk * fits - rows, lanes), F32)], axis=0)
    parts = [value[i * chunk : (i + 1) * chunk] for i in range(fits)]
    if fits * lanes < plan.packed:
        parts.append(jnp.zeros((chunk, plan.packed - fits * lanes), F32))
    return parts[0] if len(parts) == 1 else jnp.concatenate(parts, axis=1)


def unfold(plan, value, rows, lanes):
    fits = plan.packed // lanes
    parts = [value[:, i * lanes : (i + 1) * lanes] for i in range(fits)]
    return jnp.concatenate(parts, axis=0)[0:rows]


def folded_rows(plan, rows, lanes):
    return round_up(-(-rows // (plan.packed // lanes)), 8)


def pack_first(plan, value):
    if plan.block_rows > plan.packed:
        parts = [value[:, 0 : plan.packed], fold(plan, value[:, plan.packed :])]
    else:
        parts = [fold(plan, value)]
    have = sum(part.shape[0] for part in parts)
    if have < plan.first_rows:
        parts.append(jnp.zeros((plan.first_rows - have, plan.packed), F32))
    return jnp.concatenate(parts, axis=0) if len(parts) > 1 else parts[0]


def unpack_first(plan, value):
    local, r = plan.local, plan.block_rows
    if r > plan.packed:
        more = r - plan.packed
        tail = unfold(plan, value[local : local + folded_rows(plan, local, more)], local, more)
        return jnp.concatenate([value[0:local], tail], axis=1)
    return unfold(plan, value[0 : folded_rows(plan, local, r)], local, r)


def pack_second(plan, value):
    value = fold(plan, value)
    if value.shape[0] < plan.second_rows:
        rest = jnp.zeros((plan.second_rows - value.shape[0], plan.packed), F32)
        value = jnp.concatenate([value, rest], axis=0)
    return value


def unpack_second(plan, value):
    rows = folded_rows(plan, plan.piece_pad, plan.channels)
    return unfold(plan, value[0:rows], plan.piece_pad, plan.channels)


def local_to_global(plan, index, spot):
    band = quotient(index, plan.per_group)
    return band * plan.stretch + spot * plan.per_group + index - band * plan.per_group


def slice_kernel(plan, w1_any, w2_any, pay_ref, w1_ref, w2_ref, sems):
    copies = [
        pltpu.make_async_copy(src, dst, sems.at[i])
        for i, (src, dst) in enumerate(((w1_any, w1_ref), (w2_any, w2_ref)))
    ]
    for copy in copies:
        copy.start()
    spot = own_spot(plan)
    row, col = iota((plan.local, plan.channels), 0), iota((plan.local, plan.channels), 1)
    pick1 = one_hot(col == local_to_global(plan, row, spot))
    row, col = iota((plan.piece_pad, plan.block_rows), 0), iota((plan.piece_pad, plan.block_rows), 1)
    pick2 = one_hot((col == local_to_global(plan, row, spot)) & (row < plan.piece))
    copies[0].wait()
    pay_ref[0 : plan.first_rows, :] = pack_first(plan, nn(pick1, w1_ref[...])).astype(BF16)
    copies[1].wait()
    pay_ref[plan.first_rows :, :] = pack_second(plan, nt(pick2, w2_ref[...])).astype(BF16)


def act_kernel(plan, steps_ref, x_any, cot_any, after_ref, act_ref, x_ref, cot_ref, sems):
    del after_ref
    copies = [
        pltpu.make_async_copy(x_any, x_ref, sems.at[0]),
        pltpu.make_async_copy(cot_any, cot_ref, sems.at[1]),
    ]
    for copy in copies:
        copy.start()
    c, pix, head = plan.channels, plan.pixels, plan.head
    half = plan.embed // 2
    k = iota((16, c), 0) * c + iota((16, c), 1)
    angle = jnp.where(k < half, k, k - half).astype(F32)
    angle = steps_ref[0].astype(F32) * jnp.exp(-math.log(10000.0) * angle / half)
    wave = silu(jnp.where(k < half, jnp.cos(angle), jnp.sin(angle)))
    wave = jnp.where(iota((16, c), 0) < plan.embed // c, wave, 0.0)
    act_ref[pix:, :] = jnp.concatenate([wave, jnp.zeros((16, c), F32)], axis=1).astype(BF16)
    same = group_matrix(plan, c, c)
    count = pix * plan.per_group
    copies[0].wait()
    x = x_ref[...].astype(F32)
    center = nn(jnp.broadcast_to(jnp.sum(x, 0, keepdims=True), (8, c)), same, HIGHEST)[0:1] / count
    off = x - center
    spread = nn(jnp.broadcast_to(jnp.sum(off * off, 0, keepdims=True), (8, c)), same, HIGHEST)[0:1] / count
    act = silu(off * lax.rsqrt(spread + NORM_EPS)).astype(BF16)
    copies[1].wait()
    act_ref[0:pix, 0:head] = act[:, 0:head]
    act_ref[0:pix, head : 2 * head] = cot_ref[:, 0:head]
    act_ref[0:pix, 2 * head :] = jnp.concatenate(
        [act[:, head:].astype(F32), cot_ref[:, head:].astype(F32)], axis=1
    ).astype(BF16)


def relay_kernel(pass_ref, *refs):
    refs[-1][...] = pass_ref[...]


def time_kernel(plan, tw_ref, out_ref, table1_ref, table2_ref):
    team = plan.team
    c = plan.channels
    row, col = iota((plan.wide, c), 0), iota((plan.wide, c), 1)
    pick = one_hot((row < plan.local) & (col == local_to_global(plan, row, own_spot(plan))))
    own = nn(pick, tw_ref[...])
    for part in range(plan.embed // c):
        out_ref[part] = own[:, part * c : (part + 1) * c].astype(BF16)
    row, col = iota((c, team * plan.local), 0), iota((c, team * plan.local), 1)
    who = quotient(col, plan.local)
    table1_ref[...] = one_hot(row == local_to_global(plan, col - who * plan.local, who))
    row, col = iota(table2_ref.shape, 0), iota(table2_ref.shape, 1)
    who = quotient(row, plan.piece_pad)
    inner = row - who * plan.piece_pad
    table2_ref[...] = one_hot((inner < plan.piece) & (col == local_to_global(plan, inner, who)))


def roll_rows(value, shift, width, plan):
    rows = value.shape[0]
    moved = pltpu.roll(value, shift % rows, 0)
    x = iota(value.shape, 0) & (width - 1) if width & (width - 1) == 0 else lax.rem(iota(value.shape, 0), width)
    return jnp.where(x == (0 if shift == 1 else width - 1), 0.0, moved)


def roll_lanes(value, shift):
    lanes = value.shape[1]
    return value if shift % lanes == 0 else pltpu.roll(value, shift % lanes, 1)


def gather_taps(wide, plan, sign):
    left = roll_rows(wide, sign, plan.width, plan)
    right = roll_rows(roll_lanes(wide, -2 * plan.local), -sign, plan.width, plan)
    return left + roll_lanes(wide, -plan.local) + right


def spread_taps(value, plan, sign):
    left = roll_rows(value, sign, plan.width, plan)
    right = roll_rows(value, -sign, plan.width, plan)
    return left + roll_lanes(value, plan.local) + roll_lanes(right, 2 * plan.local)


def window(plan, pad, tap):
    value = pad[:, tap * plan.width : tap * plan.width + plan.pixels, :]
    return value.reshape(value.shape[0] * plan.pixels, value.shape[2])


def fill_pad(plan, pad):
    pad[:, 0 : plan.width, :] = jnp.zeros((pad.shape[0], plan.width, pad.shape[2]), BF16)
    pad[:, plan.width + plan.pixels :, :] = jnp.zeros((pad.shape[0], plan.width, pad.shape[2]), BF16)


def group_mean(plan, value, same):
    team, wide = plan.team, plan.wide
    sums = jnp.sum(value.reshape(team, plan.pixels, wide), axis=1)
    if team < 8:
        sums = jnp.concatenate([sums, jnp.zeros((8 - team, wide), F32)], axis=0)
    return nn(sums, same, HIGHEST)[0:team].reshape(team, 1, wide) / (plan.pixels * plan.per_group)


def main_kernel(plan, owner_ref, *refs):
    team, d, c, pix, local, wide = plan.team, plan.n_dom, plan.channels, plan.pixels, plan.local, plan.wide
    pays, slices, tw_ref = refs[0:team], refs[team : team + d], refs[team + d]
    refs = refs[1:]
    act2p, w2_ref = refs[team + d : team + d + 2]
    pieces = refs[team + d + 2 : team + 2 * d + 2]
    actp, cotp, w1st, w2st, held = refs[team + 2 * d + 2 :]
    here = lax.axis_index("dom")
    rows, width, head = team * pix, plan.width, plan.head

    for pad in (actp, cotp, act2p):
        fill_pad(plan, pad)
    for slot in range(team):
        actp[slot, width : width + pix, 0:head] = pays[slot][0:pix, 0:head]
        cotp[slot, width : width + pix, 0:head] = pays[slot][0:pix, head : 2 * head]
        tails = pays[slot][0:pix, 2 * head :].astype(F32)
        actp[slot, width : width + pix, head:] = tails[:, 0 : c - head].astype(BF16)
        cotp[slot, width : width + pix, head:] = tails[:, c - head :].astype(BF16)

    for slot in range(d):
        block = logical_of(plan, owner_ref, here ^ slot)
        w1st[block] = unpack_first(plan, slices[slot][0 : plan.first_rows, :].astype(F32))
    flat = jnp.concatenate([w1st[b] for b in range(d)], axis=1)
    zeros = [jnp.zeros((wide - 3 * local, c), F32)] if wide > 3 * local else []
    total = jnp.zeros((rows, wide), F32)
    for ky in range(3):
        taps = [flat[:, (3 * ky + kx) * c : (3 * ky + kx + 1) * c] for kx in range(3)]
        total = total + nt(window(plan, actp, ky), jnp.concatenate(taps + zeros, axis=0).astype(BF16))
    conv = gather_taps(total, plan, 1)
    lane_ok = iota((1, wide), 1) < local
    same = group_matrix(plan, wide, local)
    tails = jnp.concatenate([pays[slot][pix:, 0:c] for slot in range(team)], axis=0)
    row = iota((16, wide), 0)
    bias = jnp.zeros((team, 16, wide), F32)
    for part in range(plan.embed // c):
        product = nt(tails, tw_ref[part]).reshape(team, 16, wide)
        bias = bias + jnp.where(row == part, product, 0.0)
    bias = jnp.sum(bias, axis=1, keepdims=True)
    conv = jnp.where(lane_ok, conv, 0.0).reshape(team, pix, wide) + bias
    off = conv - group_mean(plan, conv.reshape(rows, wide), same)
    inverse = lax.rsqrt(group_mean(plan, (off * off).reshape(rows, wide), same) + NORM_EPS)
    norm = off * inverse
    norm = norm.reshape(rows, wide)
    gate = 1.0 / (1.0 + jnp.exp(-norm))
    act2x = spread_taps(norm * gate, plan, 1)
    act2p[:, width : width + pix, :] = act2x.astype(BF16).reshape(team, pix, wide)

    for slot in range(d):
        block = logical_of(plan, owner_ref, here ^ slot)
        w2st[block] = unpack_second(plan, slices[slot][plan.first_rows :, :].astype(F32))
    flat = jnp.concatenate([w2st[b][0 : plan.piece] for b in range(d)], axis=0)
    for ky in range(3):
        value = flat[3 * local * ky : 3 * local * (ky + 1)]
        if 3 * local < wide:
            value = jnp.concatenate([value, jnp.zeros((wide - 3 * local, c), F32)], axis=0)
        w2_ref[ky * wide : (ky + 1) * wide, :] = value.astype(BF16)

    back = jnp.zeros((rows, wide), F32)
    for ky in range(3):
        back = back + nt(window(plan, cotp, 2 - ky), w2_ref[ky * wide : (ky + 1) * wide, :])
    back = jnp.where(lane_ok, gather_taps(back, plan, -1), 0.0)
    grad = back * gate * (1.0 + norm * (1.0 - gate))
    grad_mean = group_mean(plan, grad, same)
    prod_mean = group_mean(plan, grad * norm, same)
    shaped = (team, pix, wide)
    grad = inverse * (grad.reshape(shaped) - grad_mean - norm.reshape(shaped) * prod_mean)
    grad = jnp.where(lane_ok, grad, 0.0).reshape(rows, wide).astype(BF16).astype(F32)

    gradt = spread_taps(grad, plan, -1).T.astype(BF16)
    parts = [nn(gradt, window(plan, actp, ky)) for ky in range(3)]
    flat = [parts[t // 3][(t % 3) * local : (t % 3 + 1) * local] for t in range(9)]
    flat = jnp.concatenate(flat, axis=1)
    for block in range(d):
        value = flat[:, block * plan.block_rows : (block + 1) * plan.block_rows]
        held[block, 0 : plan.first_rows, :] = pack_first(plan, value)

    act2t = act2x.T.astype(BF16)
    flat = [nn(act2t, window(plan, cotp, 2 - ky))[0 : 3 * local] for ky in range(3)]
    rest = jnp.zeros((plan.piece_pad - plan.piece, c), F32)
    flat = jnp.concatenate([*flat, rest] if rest.shape[0] else flat, axis=0)
    for block in range(d):
        value = flat[block * plan.piece : block * plan.piece + plan.piece_pad]
        held[block, plan.first_rows :, :] = pack_second(plan, value)
    for slot in range(d):
        piece = held[logical_of(plan, owner_ref, here ^ slot)]
        pieces[slot][...] = piece.astype(pieces[slot].dtype)


def share_kernel(plan, act2p, w2_ref, after_ref, keep_ref, away_ref):
    del after_ref
    team, c, pix, wide = plan.team, plan.channels, plan.pixels, plan.wide
    out = jnp.zeros((team * pix, c), F32)
    for ky in range(3):
        out = out + nn(window(plan, act2p, ky), w2_ref[ky * wide : (ky + 1) * wide, :])
    out = out.reshape(team, pix, c)
    for slot in range(team):
        if slot % 2:
            away_ref[slot // 2] = out[slot].astype(BF16)
        else:
            keep_ref[slot // 2] = out[slot]


def pair_kernel(keep_ref, came_ref, *outs):
    for k, out in enumerate(outs):
        out[...] = (keep_ref[k] + came_ref[k].astype(F32)).astype(out.dtype)


def total_kernel(n, *refs):
    total = refs[0][...].astype(F32)
    for ref in refs[1:n]:
        total = total + ref[...].astype(F32)
    refs[-1][...] = total.astype(refs[-1].dtype)


def stack_kernel(*refs):
    for k, ref in enumerate(refs[:-1]):
        refs[-1][k] = ref[...]


def last_kernel(plan, scale, n_stacks, *refs):
    team, local, c, r = plan.team, plan.local, plan.channels, plan.block_rows
    stacks = refs[0:n_stacks]
    table1_ref, table2_ref, x_ref = refs[n_stacks : n_stacks + 3]
    shares = refs[n_stacks + 3 : -8]
    first_any, second_any, output_ref, held1, held2, first_ref, second_ref, sems = refs[-8:]
    spot = own_spot(plan)
    for slot in range(team):
        piece = stacks[slot % n_stacks][slot // n_stacks, plan.first_rows :, :].astype(F32)
        held2[spot ^ slot] = unpack_second(plan, piece).astype(BF16)
    second_ref[...] = tn(held2[...].reshape(team * plan.piece_pad, c), table2_ref[...]) * scale
    copy2 = pltpu.make_async_copy(second_ref, second_any, sems.at[0])
    copy2.start()
    for slot in range(team):
        piece = stacks[slot % n_stacks][slot // n_stacks, 0 : plan.first_rows, :].astype(F32)
        held1[spot ^ slot] = unpack_first(plan, piece)
    stacked = held1[...].reshape(team * local, r).astype(BF16)
    first_ref[...] = nn(table1_ref[...], stacked) * scale
    copy1 = pltpu.make_async_copy(first_ref, first_any, sems.at[1])
    copy1.start()
    total = x_ref[...].astype(F32)
    for ref in shares:
        total = total + ref[...].reshape(total.shape).astype(F32)
    output_ref[...] = total.astype(BF16)
    copy2.wait()
    copy1.wait()


VMEM = pl.BlockSpec(memory_space=pltpu.VMEM)
SMEM = pl.BlockSpec(memory_space=pltpu.SMEM)


HBM = pl.BlockSpec(memory_space=pltpu.HBM)


def call(kernel, name, out_shape, operands, cost, n_smem=0, n_hbm=0, scratch=(), limit=48 * 1024 * 1024, out_hbm=0):
    n = len(operands)
    return pl.pallas_call(
        kernel,
        name=name,
        out_shape=out_shape,
        in_specs=[SMEM] * n_smem + [HBM] * n_hbm + [VMEM] * (n - n_smem - n_hbm),
        out_specs=[HBM] * out_hbm + [VMEM] * (len(out_shape) - out_hbm) if isinstance(out_shape, tuple) else VMEM,
        scratch_shapes=list(scratch),
        compiler_params=pltpu.CompilerParams(vmem_limit_bytes=limit),
        cost_estimate=pl.CostEstimate(
            flops=int(cost * 1e9), bytes_accessed=int(cost * 3e6), transcendentals=0
        ),
    )(*operands)


def shape(dims, dtype):
    return jax.ShapeDtypeStruct(dims, dtype)


def body(block_input, cotangent, timesteps, owner_map, time_weight, first_weight, second_weight):
    n_rep, n_dom = lax.axis_size("rep"), lax.axis_size("dom")
    height, width, c = block_input.shape[1:]
    plan = Plan(n_rep, n_dom, height, width, c, time_weight.shape[0], first_weight.shape[0])
    team, d, pix = plan.team, n_dom, plan.pixels
    r, local = plan.block_rows, plan.local
    def to_rep(value, step):
        return lax.ppermute(value, "rep", [(i, i ^ step) for i in range(n_rep)])

    def to_dom(value, step):
        return lax.ppermute(value, "dom", [(i, i ^ step) for i in range(d)])

    def team_gather(value):
        slots = [value] + [None] * (team - 1)
        for step in range(2, team, 2):
            slots[step] = to_rep(value, step)
        if team > 1:
            for step in range(0, team, 2):
                slots[step + 1] = to_rep(slots[step], 1)
        return slots

    x = block_input.reshape(pix, c)
    cot = cotangent.reshape(pix, c)
    pay = call(
        functools.partial(slice_kernel, plan),
        "slices",
        shape((plan.first_rows + plan.second_rows, plan.packed), BF16),
        (first_weight.T, second_weight.T),
        2,
        n_hbm=2,
        scratch=(
            pltpu.VMEM((c, r), BF16),
            pltpu.VMEM((c, r), BF16),
            pltpu.SemaphoreType.DMA((2,)),
        ),
        limit=56_000_000,
    )
    act = call(
        functools.partial(act_kernel, plan),
        "act",
        shape((plan.act_rows, 2 * c), BF16),
        (timesteps, x, cot, pay),
        2,
        n_smem=1,
        n_hbm=2,
        scratch=(
            pltpu.VMEM((pix, c), BF16),
            pltpu.VMEM((pix, c), BF16),
            pltpu.SemaphoreType.DMA((2,)),
        ),
        limit=56_000_000,
    )
    pays = team_gather(act)
    slots = {0: pay, d // 2: to_dom(pay, d // 2)}
    if d > 2:
        slots[d // 4] = to_dom(pay, d // 4)
    slots[d // 2] = call(
        relay_kernel,
        "relay",
        shape(pay.shape, BF16),
        (slots[d // 2], *([slots[d // 4]] if d > 2 else [])),
        20,
    )
    time_own, table1, table2 = call(
        functools.partial(time_kernel, plan),
        "time_own",
        (
            shape((plan.embed // c, plan.wide, c), BF16),
            shape((c, team * local), BF16),
            shape((team * plan.piece_pad, r), BF16),
        ),
        (time_weight.T,),
        0.001,
    )
    bit = d // 4
    while bit:
        for slot, value in list(slots.items()):
            if slot + bit not in slots:
                slots[slot + bit] = to_dom(value, bit)
        bit //= 2
    slices = [slots[slot] for slot in range(d)]
    rows = (height + 2) * width
    both = (plan.first_rows + plan.second_rows, plan.packed)
    act2p, w2, *pieces = call(
        functools.partial(main_kernel, plan),
        "main",
        (
            shape((team, rows, plan.wide), BF16),
            shape((3 * plan.wide, c), BF16),
            *[shape(both, BF16 if slot else F32) for slot in range(d)],
        ),
        (owner_map, *pays, *slices, time_own),
        6,
        n_smem=1,
        scratch=(
            pltpu.VMEM((team, rows, c), BF16),
            pltpu.VMEM((team, rows, c), BF16),
            pltpu.VMEM((d, local, r), F32),
            pltpu.VMEM((d, plan.piece_pad, c), F32),
            pltpu.VMEM((d, *both), F32),
        ),
    )

    half = -(-team // 2)
    keep, away = call(
        functools.partial(share_kernel, plan),
        "share",
        (shape((half, pix, c), F32), shape((half, pix, c), BF16)),
        (act2p, w2, pieces[0]),
        0.001,
    )
    shares = [keep]
    if team > 1:
        pairs = call(
            pair_kernel,
            "pair",
            tuple(shape((pix, c), BF16 if k else F32) for k in range(half)),
            (keep, to_rep(away, 1)),
            0.001,
        )
        shares = [pairs[0]] + [to_rep(pairs[k], 2 * k) for k in range(1, half)]

    parts = [pieces[0]] + [to_dom(pieces[step], step) for step in range(1, d)]
    total = call(
        functools.partial(total_kernel, d),
        "total",
        shape(both, BF16 if n_rep == team else F32),
        (*parts, *shares[1:]),
        0.001,
    )

    scale = 1.0 / (n_rep * n_dom)
    same_spot = [[i * team + k for i in range(n_rep // team)] for k in range(team)]
    if n_rep > team:
        total = lax.psum(total, "rep", axis_index_groups=same_spot).astype(BF16)
    stacks = [total[None]]
    if team > 1:
        slots = [total] + [to_rep(total, step) for step in range(2, team, 2)]
        stack = call(stack_kernel, "stack", shape((len(slots), *both), BF16), slots, 0.001)
        stacks = [stack, to_rep(stack, 1)]
    first, second, output = call(
        functools.partial(last_kernel, plan, scale, len(stacks)),
        "last",
        (shape((c, r), F32), shape((c, r), F32), shape((pix, c), BF16)),
        (*stacks, table1, table2, x, *shares),
        0.1,
        scratch=(
            pltpu.VMEM((team, local, r), F32),
            pltpu.VMEM((team, plan.piece_pad, c), BF16),
            pltpu.VMEM((c, r), F32),
            pltpu.VMEM((c, r), F32),
            pltpu.SemaphoreType.DMA((2,)),
        ),
        out_hbm=2,
    )
    return output.reshape(1, height, width, c), first.T, second.T


def solution(mesh):
    placed = (
        P(("rep", "dom"), None, None, None),
        P(("rep", "dom"), None, None, None),
        P(("rep", "dom")),
        P(),
        P(),
        P("dom", None),
        P("dom", None),
    )
    return jax.shard_map(
        body,
        mesh=mesh,
        in_specs=placed,
        out_specs=(P(("rep", "dom"), None, None, None), P("dom", None), P("dom", None)),
        check_vma=False,
    )
```

time: 80.3 us -> 56.8 us (0.71)
  starting transfers between devices: 42.9 us -> 25 us
  local copies, waits for them, and re-layouts: 4.19 us -> 0.02 us
  waiting for transfers between devices: 19.8 us -> 16.3 us
  Pallas kernels: 11.6 us -> 13.2 us
    ppermute x12 -> x6, starting transfers between devices: 20 us -> 10.1 us  [to_dom(): return lax.ppermute(value, 'dom', [(i, i ^ step) for i in range(d)])]
    ppermute x32 -> x15, starting transfers between devices: 22.9 us -> 14.9 us  [to_rep(): return lax.ppermute(value, 'rep', [(i, i ^ step) for i in range(n_rep)])]
    unnamed x14 -> x8, local copies, waits for them, and re-layouts: 4.11 us -> 0.02 us
    ppermute x32 -> x15, waiting for transfers between devices: 9.36 us -> 6.33 us  [to_rep(): return lax.ppermute(value, 'rep', [(i, i ^ step) for i in range(n_rep)])]
    pallas_call x6 -> x10, Pallas kernels: 11.6 us -> 13.2 us  [call(): pl.pallas_call(kernel, name=name, out_shape=out_shape, in_specs=[SMEM] *...]
    ppermute x12 -> x6, waiting for transfers between devices: 10.4 us -> 10 us  [to_dom(): return lax.ppermute(value, 'dom', [(i, i ^ step) for i in range(d)])]
  transfers between devices with their start and end apart: 44 -> 21, of which waited for: 13 -> 9; matrix products, arithmetic and copies ran while one was open for 0% -> 0% of each run, Pallas kernels for 4% -> 2%
where the time goes in v2:
time: 56.8 us; the launch traced here: 56 us
  starting transfers between devices  25 us (44%)
  waiting for transfers between devices  16.3 us (29%)
  Pallas kernels  13.2 us (23%)
  between operations  1.43 us (3%)
    ppermute x15, starting transfers between devices, to_rep(): return lax.ppermute(value, 'rep', [(i, i ^ step) for i in range(n_rep)])  14.9 us
    pallas_call x10, Pallas kernels, call(): pl.pallas_call(kernel, name=name, out_shape=out_shape, in_specs=[SMEM] *...  13.2 us
    ppermute x6, starting transfers between devices, to_dom(): return lax.ppermute(value, 'dom', [(i, i ^ step) for i in range(d)])  10.1 us
    ppermute x6, waiting for transfers between devices, to_dom(): return lax.ppermute(value, 'dom', [(i, i ^ step) for i in range(d)])  10 us
    ppermute x15, waiting for transfers between devices, to_rep(): return lax.ppermute(value, 'rep', [(i, i ^ step) for i in range(n_rep)])  6.33 us
  transfers between devices with their start and end apart: 21, of which 9 were waited for; matrix products, arithmetic and copies ran while one was open for 0% of the time, Pallas kernels for 2%

profile of v2, /device:TPU:0, one launch (start us, length us, event | category | flops | bytes accessed | tf_op | source)
XLA Modules:
  0.0 56.0 jit_solution(5828625618701072898)
XLA Ops:
  1.3 1.9 %slices.1.after_ref.refs_8_ = bf16[96,640]{1,0:T(8,128)(2,1)S(1)} custom-call(bf16[320,720]{1,0:T(8,128)(2,1)} %bitcast.14, bf16[320,720]{1,0:T(8,128)(2,1)} %bitcast.15), custom_call_target="tpu_custom_call" | custom-call | flops 2000000000 | bytes 6000000 | tf_op jit(solution)/shard_map/slices/pallas_call | solution.py:434
  3.2 1.3 %act.1.refs_0_ = bf16[144,640]{1,0:T(8,128)(2,1)S(1)} custom-call(s32[1]{0:T(128)S(6)} %copy.10.steps_ref, bf16[128,320]{1,0:T(8,128)(2,1)S(1)} %bitcast.9, bf16[128,320]{1,0:T(8,128)(2,1)S(1)} %bitcast.11, bf16[96,640]{1,0:T(8,128)(2,1)S(1)} %slices.1.after_ref.refs_8_), custom_call_target="tpu_custom_call" | custom-call | flops 2000000000 | bytes 6000000 | tf_op jit(solution)/shard_map/act/pallas_call | solution.py:434
  4.5 4.0 %collective-permute-start.5 = (bf16[144,640]{1,0:T(8,128)(2,1)S(1)}, bf16[144,640]{1,0:T(8,128)(2,1)S(1)}, u32[]{:S(2)}, u32[]{:S(2)}) collective-permute-start(bf16[144,640]{1,0:T(8,128)(2,1)S(1)} %act.1.refs_0_), channel_id=1, source_target_pairs={{0,24},{4,28},{8,16},{12,20},{16,8},{20,12},{24,0},{28,4},{1,25},{... | collective-permute-start | bytes 552968 | tf_op jit(solution)/shard_map/ppermute | solution.py:459
  8.5 0.5 collective-permute-start.3
  9.0 0.1 collective-permute-start.1
  9.1 3.0 %collective-permute-start.8 = (bf16[96,640]{1,0:T(8,128)(2,1)S(1)}, bf16[96,640]{1,0:T(8,128)(2,1)S(1)}, u32[]{:S(2)}, u32[]{:S(2)}) collective-permute-start(bf16[96,640]{1,0:T(8,128)(2,1)S(1)} %slices.1.after_ref.refs_8_), channel_id=1, source_target_pairs={{0,2},{1,3},{2,0},{3,1},{4,6},{5,7},{6,4},{7,5},{8,10},{9,11},{10,... | collective-permute-start | bytes 368648 | tf_op jit(solution)/shard_map/ppermute | solution.py:462
  12.1 1.6 %collective-permute-start.7 = (bf16[96,640]{1,0:T(8,128)(2,1)S(1)}, bf16[96,640]{1,0:T(8,128)(2,1)S(1)}, u32[]{:S(2)}, u32[]{:S(2)}) collective-permute-start(bf16[96,640]{1,0:T(8,128)(2,1)S(1)} %slices.1.after_ref.refs_8_), channel_id=1, source_target_pairs={{0,1},{1,0},{2,3},{3,2},{4,5},{5,4},{6,7},{7,6},{8,9},{9,8},{10,11... | collective-permute-start | bytes 368648 | tf_op jit(solution)/shard_map/ppermute | solution.py:462
  13.7 3.6 %collective-permute-done.8.pass_ref = bf16[96,640]{1,0:T(8,128)(2,1)S(1)} collective-permute-done((bf16[96,640]{1,0:T(8,128)(2,1)S(1)}, bf16[96,640]{1,0:T(8,128)(2,1)S(1)}, u32[]{:S(2)}, u32[]{:S(2)}) %collective-permute-start.8) | collective-permute-done | bytes 122912 | tf_op jit(solution)/shard_map/ppermute | solution.py:462
  17.3 0.5 collective-permute-start.6
  17.9 0.4 collective-permute-start.2
  18.4 1.1 %collective-permute-start.9 = (bf16[96,640]{1,0:T(8,128)(2,1)S(1)}, bf16[96,640]{1,0:T(8,128)(2,1)S(1)}, u32[]{:S(2)}, u32[]{:S(2)}) collective-permute-start(bf16[96,640]{1,0:T(8,128)(2,1)S(1)} %relay.1.refs_10_), channel_id=1, source_target_pairs={{0,1},{1,0},{2,3},{3,2},{4,5},{5,4},{6,7},{7,6},{8,9},{9,8},{10,11... | collective-permute-start | bytes 368648 | tf_op jit(solution)/shard_map/ppermute | solution.py:462
  19.4 1.3 %time_own.1 = (bf16[4,128,320]{2,1,0:T(8,128)(2,1)S(1)}, bf16[320,320]{1,0:T(8,128)(2,1)S(1)}, bf16[768,720]{1,0:T(8,128)(2,1)S(1)}) custom-call(bf16[320,1280]{1,0:T(8,128)(2,1)S(1)} %bitcast.8), custom_call_target="tpu_custom_call" | custom-call | flops 1000000 | bytes 3000 | tf_op jit(solution)/shard_map/time_own/pallas_call | solution.py:434
  20.7 3.0 %collective-permute-done.9.refs_11_ = bf16[96,640]{1,0:T(8,128)(2,1)S(1)} collective-permute-done((bf16[96,640]{1,0:T(8,128)(2,1)S(1)}, bf16[96,640]{1,0:T(8,128)(2,1)S(1)}, u32[]{:S(2)}, u32[]{:S(2)}) %collective-permute-start.9) | collective-permute-done | bytes 122912 | tf_op jit(solution)/shard_map/ppermute | solution.py:462
  23.8 5.1 %main.1 = (bf16[8,160,128]{2,1,0:T(8,128)(2,1)S(1)}, bf16[384,320]{1,0:T(8,128)(2,1)S(1)}, f32[96,640]{1,0:T(8,128)S(1)}, bf16[96,640]{1,0:T(8,128)(2,1)S(1)}, b...) custom-call(s32[4]{0:T(128)S(1)} %copy-done.3, bf16[144,640]{1,0:T(8,128)(2,1)S(1)} %act.1.refs_0_, ...), custom_call_target="tpu_custom_call" | custom-call | flops 6000000000 | bytes 18000000 | tf_op jit(solution)/shard_map/main/pallas_call | solution.py:434
  28.9 0.8 %share.1 = (f32[4,128,320]{2,1,0:T(8,128)S(1)}, bf16[4,128,320]{2,1,0:T(8,128)(2,1)S(1)}) custom-call(bf16[8,160,128]{2,1,0:T(8,128)(2,1)S(1)} %get-tuple-element.26.act2p, bf16[384,320]{1,0:T(8,128)(2,1)S(1)} %get-tuple-element.27.w2_ref, f32[96,640]{1,0:T(8,128)S(1)} %get-tuple-element.22.after_ref.refs_0_), custom_call_target="tpu_custom_call" | custom-call | flops 1000000 | bytes 3000 | tf_op jit(solution)/shard_map/share/pallas_call | solution.py:434
  29.6 0.1 collective-permute-start.13
  29.7 1.1 %collective-permute-start.10 = (bf16[96,640]{1,0:T(8,128)(2,1)S(1)}, bf16[96,640]{1,0:T(8,128)(2,1)S(1)}, u32[]{:S(2)}, u32[]{:S(2)}) collective-permute-start(bf16[96,640]{1,0:T(8,128)(2,1)S(1)} %get-tuple-element.23), channel_id=1, source_target_pairs={{0,1},{1,0},{2,3},{3,2},{4,5},{5,4},{6,7},{7,6},{8,9},{9,8},{10,11... | collective-permute-start | bytes 368648 | tf_op jit(solution)/shard_map/ppermute | solution.py:462
  30.8 3.0 %collective-permute-start.11 = (bf16[96,640]{1,0:T(8,128)(2,1)S(1)}, bf16[96,640]{1,0:T(8,128)(2,1)S(1)}, u32[]{:S(2)}, u32[]{:S(2)}) collective-permute-start(bf16[96,640]{1,0:T(8,128)(2,1)S(1)} %get-tuple-element.24), channel_id=1, source_target_pairs={{0,2},{1,3},{2,0},{3,1},{4,6},{5,7},{6,4},{7,5},{8,10},{9,11},{10,... | collective-permute-start | bytes 368648 | tf_op jit(solution)/shard_map/ppermute | solution.py:462
  33.8 0.4 collective-permute-start.12
  34.2 1.6 %collective-permute-start.14 = (bf16[128,320]{1,0:T(8,128)(2,1)S(1)}, bf16[128,320]{1,0:T(8,128)(2,1)S(1)}, u32[]{:S(2)}, u32[]{:S(2)}) collective-permute-start(bf16[128,320]{1,0:T(8,128)(2,1)S(1)} %get-tuple-element.30), channel_id=1, source_target_pairs={{0,8},{4,12},{8,0},{12,4},{16,24},{20,28},{24,16},{28,20},{1,9},{5... | collective-permute-start | bytes 245768 | tf_op jit(solution)/shard_map/ppermute | solution.py:459
  35.8 1.5 %collective-permute-start.15 = (bf16[128,320]{1,0:T(8,128)(2,1)S(1)}, bf16[128,320]{1,0:T(8,128)(2,1)S(1)}, u32[]{:S(2)}, u32[]{:S(2)}) collective-permute-start(bf16[128,320]{1,0:T(8,128)(2,1)S(1)} %get-tuple-element.31), channel_id=1, source_target_pairs={{0,16},{4,20},{8,24},{12,28},{16,0},{20,4},{24,8},{28,12},{1,17},{... | collective-permute-start | bytes 245768 | tf_op jit(solution)/shard_map/ppermute | solution.py:459
  37.4 0.4 collective-permute-done.10.refs_1_
  37.7 2.5 %collective-permute-start.16 = (bf16[128,320]{1,0:T(8,128)(2,1)S(1)}, bf16[128,320]{1,0:T(8,128)(2,1)S(1)}, u32[]{:S(2)}, u32[]{:S(2)}) collective-permute-start(bf16[128,320]{1,0:T(8,128)(2,1)S(1)} %get-tuple-element.32), channel_id=1, source_target_pairs={{0,24},{4,28},{8,16},{12,20},{16,8},{20,12},{24,0},{28,4},{1,25},{... | collective-permute-start | bytes 245768 | tf_op jit(solution)/shard_map/ppermute | solution.py:459
  40.2 2.9 %collective-permute-done.11.refs_2_ = bf16[96,640]{1,0:T(8,128)(2,1)S(1)} collective-permute-done((bf16[96,640]{1,0:T(8,128)(2,1)S(1)}, bf16[96,640]{1,0:T(8,128)(2,1)S(1)}, u32[]{:S(2)}, u32[]{:S(2)}) %collective-permute-start.11) | collective-permute-done | bytes 122912 | tf_op jit(solution)/shard_map/ppermute | solution.py:462
  43.3 2.6 %collective-permute-start.19 = (bf16[96,640]{1,0:T(8,128)(2,1)S(1)}, bf16[96,640]{1,0:T(8,128)(2,1)S(1)}, u32[]{:S(2)}, u32[]{:S(2)}) collective-permute-start(bf16[96,640]{1,0:T(8,128)(2,1)S(1)} %total.1.refs_0_), channel_id=1, source_target_pairs={{0,24},{4,28},{8,16},{12,20},{16,8},{20,12},{24,0},{28,4},{1,25},{... | collective-permute-start | bytes 368648 | tf_op jit(solution)/shard_map/ppermute | solution.py:459
  45.9 0.5 collective-permute-start.18
  46.4 0.5 collective-permute-start.17
  46.9 3.3 %collective-permute-done.19.refs_3_ = bf16[96,640]{1,0:T(8,128)(2,1)S(1)} collective-permute-done((bf16[96,640]{1,0:T(8,128)(2,1)S(1)}, bf16[96,640]{1,0:T(8,128)(2,1)S(1)}, u32[]{:S(2)}, u32[]{:S(2)}) %collective-permute-start.19) | collective-permute-done | bytes 122912 | tf_op jit(solution)/shard_map/ppermute | solution.py:459
  50.2 0.9 %collective-permute-done.18.refs_2_ = bf16[96,640]{1,0:T(8,128)(2,1)S(1)} collective-permute-done((bf16[96,640]{1,0:T(8,128)(2,1)S(1)}, bf16[96,640]{1,0:T(8,128)(2,1)S(1)}, u32[]{:S(2)}, u32[]{:S(2)}) %collective-permute-start.18) | collective-permute-done | bytes 122912 | tf_op jit(solution)/shard_map/ppermute | solution.py:459
  51.2 0.1 collective-permute-done.17.refs_1_
  51.4 1.9 %collective-permute-done.20.refs_1_ = bf16[4,96,640]{2,1,0:T(8,128)(2,1)S(1)} collective-permute-done((bf16[4,96,640]{2,1,0:T(8,128)(2,1)S(1)}, bf16[4,96,640]{2,1,0:T(8,128)(2,1)S(1)}, u32[]{:S(2)}, u32[]{:S(2)}) %collective-permute-start.20) | collective-permute-done | bytes 491552 | tf_op jit(solution)/shard_map/ppermute | solution.py:459
  53.3 2.8 %last.1 = (f32[320,720]{1,0:T(8,128)}, f32[320,720]{1,0:T(8,128)}, bf16[128,320]{1,0:T(8,128)(2,1)}) custom-call(bf16[4,96,640]{2,1,0:T(8,128)(2,1)S(1)} %stack.1.refs_0_, bf16[4,96,640]{2,1,0:T(8,128)(2,1)S(1)} %collective-permute-done.20.refs_1_, bf16[320,320]{1,0:T(8,128)(2,1)S(1)} %get-tuple-element.33.refs_2_, ...), custom_call_target="tpu_custom_call" | custom-call | flops 100000000 | bytes 300000 | tf_op jit(solution)/shard_map/last/pallas_call | solution.py:434
  (28 shorter events, 0.4 us)
Async XLA Ops:
  1.3 1.9 %copy-start.1 = (bf16[1,8,16,320]{3,2,1,0:T(8,128)(2,1)S(1)}, bf16[1,8,16,320]{3,2,1,0:T(8,128)(2,1)}, u32[]{:S(2)}) copy-start(bf16[1,8,16,320]{3,2,1,0:T(8,128)(2,1)} %param.7) | copy-start | bytes 245764
  1.3 1.9 %copy-start.2 = (bf16[1,8,16,320]{3,2,1,0:T(8,128)(2,1)S(1)}, bf16[1,8,16,320]{3,2,1,0:T(8,128)(2,1)}, u32[]{:S(2)}) copy-start(bf16[1,8,16,320]{3,2,1,0:T(8,128)(2,1)} %param.8) | copy-start | bytes 245764
  4.5 14.9 %copy-start = (bf16[1280,320]{0,1:T(8,128)(2,1)S(1)}, bf16[1280,320]{0,1:T(8,128)(2,1)}, u32[]{:S(2)}) copy-start(bf16[1280,320]{0,1:T(8,128)(2,1)} %param.11) | copy-start | bytes 2457604
  4.5 19.3 %copy-start.3 = (s32[4]{0:T(128)S(1)}, s32[4]{0:T(128)}, u32[]{:S(2)}) copy-start(s32[4]{0:T(128)} %owner_ref.1) | copy-start | bytes 52
  4.5 12.8 %collective-permute-start.5 = (bf16[144,640]{1,0:T(8,128)(2,1)S(1)}, bf16[144,640]{1,0:T(8,128)(2,1)S(1)}, u32[]{:S(2)}, u32[]{:S(2)}) collective-permute-start(bf16[144,640]{1,0:T(8,128)(2,1)S(1)} %act.1.refs_0_), channel_id=1, source_target_pairs={{0,24},{4,28},{8,16},{12,20},{16,8},{20,12},{24,0},{28,4},{1,25},{... | collective-permute-start | bytes 552968 | tf_op jit(solution)/shard_map/ppermute | solution.py:459
  8.5 9.4 %collective-permute-start.3 = (bf16[144,640]{1,0:T(8,128)(2,1)S(1)}, bf16[144,640]{1,0:T(8,128)(2,1)S(1)}, u32[]{:S(2)}, u32[]{:S(2)}) collective-permute-start(bf16[144,640]{1,0:T(8,128)(2,1)S(1)} %act.1.refs_0_), channel_id=1, source_target_pairs={{0,16},{4,20},{8,24},{12,28},{16,0},{20,4},{24,8},{28,12},{1,17},{... | collective-permute-start | bytes 552968 | tf_op jit(solution)/shard_map/ppermute | solution.py:459
  9.0 8.9 %collective-permute-start.1 = (bf16[144,640]{1,0:T(8,128)(2,1)S(1)}, bf16[144,640]{1,0:T(8,128)(2,1)S(1)}, u32[]{:S(2)}, u32[]{:S(2)}) collective-permute-start(bf16[144,640]{1,0:T(8,128)(2,1)S(1)} %act.1.refs_0_), channel_id=1, source_target_pairs={{0,8},{4,12},{8,0},{12,4},{16,24},{20,28},{24,16},{28,20},{1,9},{5... | collective-permute-start | bytes 552968 | tf_op jit(solution)/shard_map/ppermute | solution.py:459
  9.1 8.2 %collective-permute-start.8 = (bf16[96,640]{1,0:T(8,128)(2,1)S(1)}, bf16[96,640]{1,0:T(8,128)(2,1)S(1)}, u32[]{:S(2)}, u32[]{:S(2)}) collective-permute-start(bf16[96,640]{1,0:T(8,128)(2,1)S(1)} %slices.1.after_ref.refs_8_), channel_id=1, source_target_pairs={{0,2},{1,3},{2,0},{3,1},{4,6},{5,7},{6,4},{7,5},{8,10},{9,11},{10,... | collective-permute-start | bytes 368648 | tf_op jit(solution)/shard_map/ppermute | solution.py:462
  12.1 6.3 %collective-permute-start.7 = (bf16[96,640]{1,0:T(8,128)(2,1)S(1)}, bf16[96,640]{1,0:T(8,128)(2,1)S(1)}, u32[]{:S(2)}, u32[]{:S(2)}) collective-permute-start(bf16[96,640]{1,0:T(8,128)(2,1)S(1)} %slices.1.after_ref.refs_8_), channel_id=1, source_target_pairs={{0,1},{1,0},{2,3},{3,2},{4,5},{5,4},{6,7},{7,6},{8,9},{9,8},{10,11... | collective-permute-start | bytes 368648 | tf_op jit(solution)/shard_map/ppermute | solution.py:462
  17.3 3.4 %collective-permute-start = (bf16[144,640]{1,0:T(8,128)(2,1)S(1)}, bf16[144,640]{1,0:T(8,128)(2,1)S(1)}, u32[]{:S(2)}, u32[]{:S(2)}) collective-permute-start(bf16[144,640]{1,0:T(8,128)(2,1)S(1)} %act.1.refs_0_), channel_id=1, source_target_pairs={{0,4},{4,0},{8,12},{12,8},{16,20},{20,16},{24,28},{28,24},{1,5},{5... | collective-permute-start | bytes 552968 | tf_op jit(solution)/shard_map/ppermute | solution.py:459
  17.3 6.4 %collective-permute-start.6 = (bf16[144,640]{1,0:T(8,128)(2,1)S(1)}, bf16[144,640]{1,0:T(8,128)(2,1)S(1)}, u32[]{:S(2)}, u32[]{:S(2)}) collective-permute-start(bf16[144,640]{1,0:T(8,128)(2,1)S(1)} %collective-permute-done.5.refs_6_), channel_id=1, source_target_pairs={{0,4},{4,0},{8,12},{12,8},{16,20},{20,16},{24,28},{28,24},{1,5},{5... | collective-permute-start | bytes 552968 | tf_op jit(solution)/shard_map/ppermute | solution.py:459
  17.9 5.9 %collective-permute-start.4 = (bf16[144,640]{1,0:T(8,128)(2,1)S(1)}, bf16[144,640]{1,0:T(8,128)(2,1)S(1)}, u32[]{:S(2)}, u32[]{:S(2)}) collective-permute-start(bf16[144,640]{1,0:T(8,128)(2,1)S(1)} %collective-permute-done.3.refs_4_), channel_id=1, source_target_pairs={{0,4},{4,0},{8,12},{12,8},{16,20},{20,16},{24,28},{28,24},{1,5},{5... | collective-permute-start | bytes 552968 | tf_op jit(solution)/shard_map/ppermute | solution.py:459
  17.9 5.8 %collective-permute-start.2 = (bf16[144,640]{1,0:T(8,128)(2,1)S(1)}, bf16[144,640]{1,0:T(8,128)(2,1)S(1)}, u32[]{:S(2)}, u32[]{:S(2)}) collective-permute-start(bf16[144,640]{1,0:T(8,128)(2,1)S(1)} %collective-permute-done.1.refs_2_), channel_id=1, source_target_pairs={{0,4},{4,0},{8,12},{12,8},{16,20},{20,16},{24,28},{28,24},{1,5},{5... | collective-permute-start | bytes 552968 | tf_op jit(solution)/shard_map/ppermute | solution.py:459
  18.4 5.4 %collective-permute-start.9 = (bf16[96,640]{1,0:T(8,128)(2,1)S(1)}, bf16[96,640]{1,0:T(8,128)(2,1)S(1)}, u32[]{:S(2)}, u32[]{:S(2)}) collective-permute-start(bf16[96,640]{1,0:T(8,128)(2,1)S(1)} %relay.1.refs_10_), channel_id=1, source_target_pairs={{0,1},{1,0},{2,3},{3,2},{4,5},{5,4},{6,7},{7,6},{8,9},{9,8},{10,11... | collective-permute-start | bytes 368648 | tf_op jit(solution)/shard_map/ppermute | solution.py:462
  29.6 4.5 %collective-permute-start.13 = (bf16[4,128,320]{2,1,0:T(8,128)(2,1)S(1)}, bf16[4,128,320]{2,1,0:T(8,128)(2,1)S(1)}, u32[]{:S(2)}, u32[]{:S(2)}) collective-permute-start(bf16[4,128,320]{2,1,0:T(8,128)(2,1)S(1)} %get-tuple-element.29), channel_id=1, source_target_pairs={{0,4},{4,0},{8,12},{12,8},{16,20},{20,16},{24,28},{28,24},{1,5},{5... | collective-permute-start | bytes 983048 | tf_op jit(solution)/shard_map/ppermute | solution.py:459
  29.7 8.0 %collective-permute-start.10 = (bf16[96,640]{1,0:T(8,128)(2,1)S(1)}, bf16[96,640]{1,0:T(8,128)(2,1)S(1)}, u32[]{:S(2)}, u32[]{:S(2)}) collective-permute-start(bf16[96,640]{1,0:T(8,128)(2,1)S(1)} %get-tuple-element.23), channel_id=1, source_target_pairs={{0,1},{1,0},{2,3},{3,2},{4,5},{5,4},{6,7},{7,6},{8,9},{9,8},{10,11... | collective-permute-start | bytes 368648 | tf_op jit(solution)/shard_map/ppermute | solution.py:462
  30.8 12.4 %collective-permute-start.11 = (bf16[96,640]{1,0:T(8,128)(2,1)S(1)}, bf16[96,640]{1,0:T(8,128)(2,1)S(1)}, u32[]{:S(2)}, u32[]{:S(2)}) collective-permute-start(bf16[96,640]{1,0:T(8,128)(2,1)S(1)} %get-tuple-element.24), channel_id=1, source_target_pairs={{0,2},{1,3},{2,0},{3,1},{4,6},{5,7},{6,4},{7,5},{8,10},{9,11},{10,... | collective-permute-start | bytes 368648 | tf_op jit(solution)/shard_map/ppermute | solution.py:462
  33.8 9.4 %collective-permute-start.12 = (bf16[96,640]{1,0:T(8,128)(2,1)S(1)}, bf16[96,640]{1,0:T(8,128)(2,1)S(1)}, u32[]{:S(2)}, u32[]{:S(2)}) collective-permute-start(bf16[96,640]{1,0:T(8,128)(2,1)S(1)} %get-tuple-element.25), channel_id=1, source_target_pairs={{0,3},{1,2},{2,1},{3,0},{4,7},{5,6},{6,5},{7,4},{8,11},{9,10},{10,... | collective-permute-start | bytes 368648 | tf_op jit(solution)/shard_map/ppermute | solution.py:462
  34.2 9.0 %collective-permute-start.14 = (bf16[128,320]{1,0:T(8,128)(2,1)S(1)}, bf16[128,320]{1,0:T(8,128)(2,1)S(1)}, u32[]{:S(2)}, u32[]{:S(2)}) collective-permute-start(bf16[128,320]{1,0:T(8,128)(2,1)S(1)} %get-tuple-element.30), channel_id=1, source_target_pairs={{0,8},{4,12},{8,0},{12,4},{16,24},{20,28},{24,16},{28,20},{1,9},{5... | collective-permute-start | bytes 245768 | tf_op jit(solution)/shard_map/ppermute | solution.py:459
  35.8 7.3 %collective-permute-start.15 = (bf16[128,320]{1,0:T(8,128)(2,1)S(1)}, bf16[128,320]{1,0:T(8,128)(2,1)S(1)}, u32[]{:S(2)}, u32[]{:S(2)}) collective-permute-start(bf16[128,320]{1,0:T(8,128)(2,1)S(1)} %get-tuple-element.31), channel_id=1, source_target_pairs={{0,16},{4,20},{8,24},{12,28},{16,0},{20,4},{24,8},{28,12},{1,17},{... | collective-permute-start | bytes 245768 | tf_op jit(solution)/shard_map/ppermute | solution.py:459
  37.7 5.5 %collective-permute-start.16 = (bf16[128,320]{1,0:T(8,128)(2,1)S(1)}, bf16[128,320]{1,0:T(8,128)(2,1)S(1)}, u32[]{:S(2)}, u32[]{:S(2)}) collective-permute-start(bf16[128,320]{1,0:T(8,128)(2,1)S(1)} %get-tuple-element.32), channel_id=1, source_target_pairs={{0,24},{4,28},{8,16},{12,20},{16,8},{20,12},{24,0},{28,4},{1,25},{... | collective-permute-start | bytes 245768 | tf_op jit(solution)/shard_map/ppermute | solution.py:459
  43.3 6.9 %collective-permute-start.19 = (bf16[96,640]{1,0:T(8,128)(2,1)S(1)}, bf16[96,640]{1,0:T(8,128)(2,1)S(1)}, u32[]{:S(2)}, u32[]{:S(2)}) collective-permute-start(bf16[96,640]{1,0:T(8,128)(2,1)S(1)} %total.1.refs_0_), channel_id=1, source_target_pairs={{0,24},{4,28},{8,16},{12,20},{16,8},{20,12},{24,0},{28,4},{1,25},{... | collective-permute-start | bytes 368648 | tf_op jit(solution)/shard_map/ppermute | solution.py:459
  45.9 5.3 %collective-permute-start.18 = (bf16[96,640]{1,0:T(8,128)(2,1)S(1)}, bf16[96,640]{1,0:T(8,128)(2,1)S(1)}, u32[]{:S(2)}, u32[]{:S(2)}) collective-permute-start(bf16[96,640]{1,0:T(8,128)(2,1)S(1)} %total.1.refs_0_), channel_id=1, source_target_pairs={{0,16},{4,20},{8,24},{12,28},{16,0},{20,4},{24,8},{28,12},{1,17},{... | collective-permute-start | bytes 368648 | tf_op jit(solution)/shard_map/ppermute | solution.py:459
  46.4 4.9 %collective-permute-start.17 = (bf16[96,640]{1,0:T(8,128)(2,1)S(1)}, bf16[96,640]{1,0:T(8,128)(2,1)S(1)}, u32[]{:S(2)}, u32[]{:S(2)}) collective-permute-start(bf16[96,640]{1,0:T(8,128)(2,1)S(1)} %total.1.refs_0_), channel_id=1, source_target_pairs={{0,8},{4,12},{8,0},{12,4},{16,24},{20,28},{24,16},{28,20},{1,9},{5... | collective-permute-start | bytes 368648 | tf_op jit(solution)/shard_map/ppermute | solution.py:459
  51.3 1.9 %collective-permute-start.20 = (bf16[4,96,640]{2,1,0:T(8,128)(2,1)S(1)}, bf16[4,96,640]{2,1,0:T(8,128)(2,1)S(1)}, u32[]{:S(2)}, u32[]{:S(2)}) collective-permute-start(bf16[4,96,640]{2,1,0:T(8,128)(2,1)S(1)} %stack.1.refs_0_), channel_id=1, source_target_pairs={{0,4},{4,0},{8,12},{12,8},{16,20},{20,16},{24,28},{28,24},{1,5},{5... | collective-permute-start | bytes 1474568 | tf_op jit(solution)/shard_map/ppermute | solution.py:459

commit v3 on v2

--- a/solution.py
+++ b/solution.py
@@ -12,17 +12,14 @@
 NORM_EPS = 1e-05
 F32 = jnp.float32
 BF16 = jnp.bfloat16
-HIGHEST = lax.Precision.HIGHEST
 
 
 def round_up(value, unit):
     return -(-value // unit) * unit
 
 
-def nn(a, b, precision=None):
-    return lax.dot_general(
-        a, b, (((1,), (0,)), ((), ())), precision=precision, preferred_element_type=F32
-    )
+def nn(a, b):
+    return lax.dot_general(a, b, (((1,), (0,)), ((), ())), preferred_element_type=F32)
 
 
 def nt(a, b):
@@ -99,7 +96,18 @@
 def group_matrix(plan, lanes, channels):
     row, col = iota((lanes, lanes), 0), iota((lanes, lanes), 1)
     same = quotient(row, plan.per_group) == quotient(col, plan.per_group)
-    return jnp.where(same & (row < channels) & (col < channels), 1.0, 0.0)
+    return one_hot(same & (row < channels) & (col < channels))
+
+
+def group_sum(sums, same):
+    rows = sums.shape[0]
+    if rows < 8:
+        sums = jnp.concatenate([sums, jnp.zeros((8 - rows, sums.shape[1]), F32)], axis=0)
+    high = sums.astype(BF16).astype(F32)
+    mid = (sums - high).astype(BF16).astype(F32)
+    parts = jnp.concatenate([high, mid, sums - high - mid, jnp.zeros_like(high)], axis=0)
+    total = nn(parts.astype(BF16), same)
+    return (total[0:8] + total[8:16] + total[16:24])[0:rows]
 
 
 def fold(plan, value):
@@ -172,37 +180,30 @@
     spot = own_spot(plan)
     row, col = iota((plan.local, plan.channels), 0), iota((plan.local, plan.channels), 1)
     pick1 = one_hot(col == local_to_global(plan, row, spot))
-    row, col = iota((plan.piece_pad, plan.block_rows), 0), iota((plan.piece_pad, plan.block_rows), 1)
-    pick2 = one_hot((col == local_to_global(plan, row, spot)) & (row < plan.piece))
+    lanes = round_up(plan.piece_pad, 128)
+    row, col = iota((plan.block_rows, lanes), 0), iota((plan.block_rows, lanes), 1)
+    pick2 = one_hot((row == local_to_global(plan, col, spot)) & (col < plan.piece))
     copies[0].wait()
     pay_ref[0 : plan.first_rows, :] = pack_first(plan, nn(pick1, w1_ref[...])).astype(BF16)
     copies[1].wait()
-    pay_ref[plan.first_rows :, :] = pack_second(plan, nt(pick2, w2_ref[...])).astype(BF16)
-
-
-def act_kernel(plan, steps_ref, x_any, cot_any, after_ref, act_ref, x_ref, cot_ref, sems):
+    pay_ref[plan.first_rows :, :] = pack_second(plan, nn(w2_ref[...], pick2).T[0 : plan.piece_pad]).astype(BF16)
+
+
+def act_kernel(plan, x_any, cot_any, steps_ref, after_ref, act_ref, x_ref, cot_ref, sems):
     del after_ref
     copies = [
-        pltpu.make_async_copy(x_any, x_ref, sems.at[0]),
-        pltpu.make_async_copy(cot_any, cot_ref, sems.at[1]),
+        pltpu.make_async_copy(src, dst, sems.at[i])
+        for i, (src, dst) in enumerate(((x_any, x_ref), (cot_any, cot_ref)))
     ]
     for copy in copies:
         copy.start()
     c, pix, head = plan.channels, plan.pixels, plan.head
-    half = plan.embed // 2
-    k = iota((16, c), 0) * c + iota((16, c), 1)
-    angle = jnp.where(k < half, k, k - half).astype(F32)
-    angle = steps_ref[0].astype(F32) * jnp.exp(-math.log(10000.0) * angle / half)
-    wave = silu(jnp.where(k < half, jnp.cos(angle), jnp.sin(angle)))
-    wave = jnp.where(iota((16, c), 0) < plan.embed // c, wave, 0.0)
-    act_ref[pix:, :] = jnp.concatenate([wave, jnp.zeros((16, c), F32)], axis=1).astype(BF16)
     same = group_matrix(plan, c, c)
     count = pix * plan.per_group
     copies[0].wait()
     x = x_ref[...].astype(F32)
-    center = nn(jnp.broadcast_to(jnp.sum(x, 0, keepdims=True), (8, c)), same, HIGHEST)[0:1] / count
-    off = x - center
-    spread = nn(jnp.broadcast_to(jnp.sum(off * off, 0, keepdims=True), (8, c)), same, HIGHEST)[0:1] / count
+    off = x - group_sum(jnp.sum(x, 0, keepdims=True), same) / count
+    spread = group_sum(jnp.sum(off * off, 0, keepdims=True), same) / count
     act = silu(off * lax.rsqrt(spread + NORM_EPS)).astype(BF16)
     copies[1].wait()
     act_ref[0:pix, 0:head] = act[:, 0:head]
@@ -210,27 +211,54 @@
     act_ref[0:pix, 2 * head :] = jnp.concatenate(
         [act[:, head:].astype(F32), cot_ref[:, head:].astype(F32)], axis=1
     ).astype(BF16)
+    half = plan.embed // 2
+    k = iota((16, c), 0) * c + iota((16, c), 1)
+    angle = jnp.where(k < half, k, k - half).astype(F32)
+    angle = steps_ref[...].astype(F32) * jnp.exp(-math.log(10000.0) * angle / half)
+    wave = silu(jnp.where(k < half, jnp.cos(angle), jnp.sin(angle)))
+    wave = jnp.where(iota((16, c), 0) < plan.embed // c, wave, 0.0)
+    act_ref[pix:, :] = jnp.concatenate([wave, jnp.zeros((16, c), F32)], axis=1).astype(BF16)
 
 
 def relay_kernel(pass_ref, *refs):
     refs[-1][...] = pass_ref[...]
 
 
-def time_kernel(plan, tw_ref, out_ref, table1_ref, table2_ref):
-    team = plan.team
+def time_kernel(plan, tw_ref, out_ref, main_ref, fold_ref, second_ref):
     c = plan.channels
+    spot = own_spot(plan)
     row, col = iota((plan.wide, c), 0), iota((plan.wide, c), 1)
-    pick = one_hot((row < plan.local) & (col == local_to_global(plan, row, own_spot(plan))))
+    pick = one_hot((row < plan.local) & (col == local_to_global(plan, row, spot)))
     own = nn(pick, tw_ref[...])
     for part in range(plan.embed // c):
         out_ref[part] = own[:, part * c : (part + 1) * c].astype(BF16)
-    row, col = iota((c, team * plan.local), 0), iota((c, team * plan.local), 1)
-    who = quotient(col, plan.local)
-    table1_ref[...] = one_hot(row == local_to_global(plan, col - who * plan.local, who))
-    row, col = iota(table2_ref.shape, 0), iota(table2_ref.shape, 1)
-    who = quotient(row, plan.piece_pad)
-    inner = row - who * plan.piece_pad
-    table2_ref[...] = one_hot((inner < plan.piece) & (col == local_to_global(plan, inner, who)))
+
+    n = -(-plan.team // 2)
+    base, chunk, used, _ = fold_layout(plan)
+    for kind in range(main_ref.shape[0]):
+
+        def holder(place):
+            return (2 * place + kind) ^ spot
+
+        row, col = iota(main_ref.shape[1:], 0), iota(main_ref.shape[1:], 1)
+        place = quotient(col, plan.first_rows)
+        inner = col - place * plan.first_rows
+        hit = (inner < plan.local) & (row == local_to_global(plan, inner, holder(place)))
+        main_ref[kind] = one_hot(hit)
+        row, col = iota(fold_ref.shape[1:], 0), iota(fold_ref.shape[1:], 1)
+        piece = quotient(col, n * chunk)
+        place = quotient(col - piece * (n * chunk), chunk)
+        inner = col - (piece * n + place - piece) * chunk
+        hit = (inner < plan.local) & (row == local_to_global(plan, inner, holder(place)))
+        fold_ref[kind] = one_hot(hit)
+        row, col = iota(second_ref.shape[1:], 0), iota(second_ref.shape[1:], 1)
+        piece = quotient(row, n * plan.second_rows)
+        place = quotient(row - piece * (n * plan.second_rows), plan.second_rows)
+        inner = row - (piece * n + place) * plan.second_rows
+        rows = folded_rows(plan, plan.piece_pad, c)
+        hit = (inner < rows) & (inner + piece * rows < plan.piece)
+        hit = hit & (col == local_to_global(plan, inner + piece * rows, holder(place)))
+        second_ref[kind] = one_hot(hit)
 
 
 def roll_rows(value, shift, width, plan):
@@ -270,42 +298,70 @@
 def group_mean(plan, value, same):
     team, wide = plan.team, plan.wide
     sums = jnp.sum(value.reshape(team, plan.pixels, wide), axis=1)
-    if team < 8:
-        sums = jnp.concatenate([sums, jnp.zeros((8 - team, wide), F32)], axis=0)
-    return nn(sums, same, HIGHEST)[0:team].reshape(team, 1, wide) / (plan.pixels * plan.per_group)
+    sums = [group_sum(sums[k : k + 8], same) for k in range(0, team, 8)]
+    sums = sums[0] if len(sums) == 1 else jnp.concatenate(sums, axis=0)
+    return sums.reshape(team, 1, wide) * (1.0 / (plan.pixels * plan.per_group))
+
+
+def row_taps(plan, value, sign):
+    team, pix, wide, width = plan.team, plan.pixels, plan.wide, plan.width
+    value = value.reshape(team, pix, 3 * wide)
+    edge = jnp.zeros((team, width, wide), F32)
+    low, mid, high = (value[:, :, k * wide : (k + 1) * wide] for k in range(3))
+    if sign < 0:
+        low, high = high, low
+    low = jnp.concatenate([edge, low[:, : pix - width]], axis=1)
+    high = jnp.concatenate([high[:, width:], edge], axis=1)
+    return (low + mid + high).reshape(team * pix, wide)
+
+
+def stack_rows(plan, value, sign):
+    width, pix = plan.width, plan.pixels
+    lanes = value.shape[1]
+    inside = lax.rem(iota(value.shape, 1), pix)
+    above = jnp.where(inside < width, 0.0, pltpu.roll(value, width, 1))
+    below = jnp.where(inside >= pix - width, 0.0, pltpu.roll(value, lanes - width, 1))
+    order = (above, value, below) if sign > 0 else (below, value, above)
+    return jnp.concatenate([part.astype(BF16) for part in order], axis=0)
 
 
 def main_kernel(plan, owner_ref, *refs):
     team, d, c, pix, local, wide = plan.team, plan.n_dom, plan.channels, plan.pixels, plan.local, plan.wide
     pays, slices, tw_ref = refs[0:team], refs[team : team + d], refs[team + d]
-    refs = refs[1:]
-    act2p, w2_ref = refs[team + d : team + d + 2]
-    pieces = refs[team + d + 2 : team + 2 * d + 2]
-    actp, cotp, w1st, w2st, held = refs[team + 2 * d + 2 :]
+    act2p, w2_ref = refs[team + d + 1 : team + d + 3]
+    pieces = refs[team + d + 3 : team + 2 * d + 3]
+    maps, w1st, w2st, held = refs[team + 2 * d + 3 :]
     here = lax.axis_index("dom")
     rows, width, head = team * pix, plan.width, plan.head
-
-    for pad in (actp, cotp, act2p):
-        fill_pad(plan, pad)
+    tail = c - head
+
     for slot in range(team):
-        actp[slot, width : width + pix, 0:head] = pays[slot][0:pix, 0:head]
-        cotp[slot, width : width + pix, 0:head] = pays[slot][0:pix, head : 2 * head]
-        tails = pays[slot][0:pix, 2 * head :].astype(F32)
-        actp[slot, width : width + pix, head:] = tails[:, 0 : c - head].astype(BF16)
-        cotp[slot, width : width + pix, head:] = tails[:, c - head :].astype(BF16)
+        maps[slot * pix : (slot + 1) * pix, :] = pays[slot][0:pix, :]
 
     for slot in range(d):
         block = logical_of(plan, owner_ref, here ^ slot)
         w1st[block] = unpack_first(plan, slices[slot][0 : plan.first_rows, :].astype(F32))
+        w2st[block] = unpack_second(plan, slices[slot][plan.first_rows :, :].astype(F32))
     flat = jnp.concatenate([w1st[b] for b in range(d)], axis=1)
     zeros = [jnp.zeros((wide - 3 * local, c), F32)] if wide > 3 * local else []
-    total = jnp.zeros((rows, wide), F32)
+    w1 = []
     for ky in range(3):
-        taps = [flat[:, (3 * ky + kx) * c : (3 * ky + kx + 1) * c] for kx in range(3)]
-        total = total + nt(window(plan, actp, ky), jnp.concatenate(taps + zeros, axis=0).astype(BF16))
-    conv = gather_taps(total, plan, 1)
+        w1 += [flat[:, t * c : (t + 1) * c] for t in range(3 * ky, 3 * ky + 3)] + zeros
+    w1 = jnp.concatenate(w1, axis=0)
+    flat = jnp.concatenate([w2st[b][0 : plan.piece] for b in range(d)], axis=0)
+    w2 = []
+    for ky in range(3):
+        w2 += [flat[3 * local * ky : 3 * local * (ky + 1)]] + zeros
+    w2 = jnp.concatenate(w2, axis=0)
+    w2_ref[...] = w2.astype(BF16)
+
     lane_ok = iota((1, wide), 1) < local
     same = group_matrix(plan, wide, local)
+    none = jnp.zeros((3 * wide, tail), F32)
+    w1_tail = jnp.concatenate([w1[:, head:], none], axis=1).astype(BF16)
+    w2_tail = jnp.concatenate([none, w2[:, head:]], axis=1).astype(BF16)
+    conv = nt(maps[:, 0:head], w1[:, 0:head].astype(BF16)) + nt(maps[:, 2 * head :], w1_tail)
+    conv = gather_taps(row_taps(plan, conv, 1), plan, 1)
     tails = jnp.concatenate([pays[slot][pix:, 0:c] for slot in range(team)], axis=0)
     row = iota((16, wide), 0)
     bias = jnp.zeros((team, 16, wide), F32)
@@ -316,26 +372,14 @@
     conv = jnp.where(lane_ok, conv, 0.0).reshape(team, pix, wide) + bias
     off = conv - group_mean(plan, conv.reshape(rows, wide), same)
     inverse = lax.rsqrt(group_mean(plan, (off * off).reshape(rows, wide), same) + NORM_EPS)
-    norm = off * inverse
-    norm = norm.reshape(rows, wide)
+    norm = (off * inverse).reshape(rows, wide)
     gate = 1.0 / (1.0 + jnp.exp(-norm))
     act2x = spread_taps(norm * gate, plan, 1)
+    fill_pad(plan, act2p)
     act2p[:, width : width + pix, :] = act2x.astype(BF16).reshape(team, pix, wide)
 
-    for slot in range(d):
-        block = logical_of(plan, owner_ref, here ^ slot)
-        w2st[block] = unpack_second(plan, slices[slot][plan.first_rows :, :].astype(F32))
-    flat = jnp.concatenate([w2st[b][0 : plan.piece] for b in range(d)], axis=0)
-    for ky in range(3):
-        value = flat[3 * local * ky : 3 * local * (ky + 1)]
-        if 3 * local < wide:
-            value = jnp.concatenate([value, jnp.zeros((wide - 3 * local, c), F32)], axis=0)
-        w2_ref[ky * wide : (ky + 1) * wide, :] = value.astype(BF16)
-
-    back = jnp.zeros((rows, wide), F32)
-    for ky in range(3):
-        back = back + nt(window(plan, cotp, 2 - ky), w2_ref[ky * wide : (ky + 1) * wide, :])
-    back = jnp.where(lane_ok, gather_taps(back, plan, -1), 0.0)
+    back = nt(maps[:, head : 2 * head], w2[:, 0:head].astype(BF16)) + nt(maps[:, 2 * head :], w2_tail)
+    back = jnp.where(lane_ok, gather_taps(row_taps(plan, back, -1), plan, -1), 0.0)
     grad = back * gate * (1.0 + norm * (1.0 - gate))
     grad_mean = group_mean(plan, grad, same)
     prod_mean = group_mean(plan, grad * norm, same)
@@ -343,16 +387,20 @@
     grad = inverse * (grad.reshape(shaped) - grad_mean - norm.reshape(shaped) * prod_mean)
     grad = jnp.where(lane_ok, grad, 0.0).reshape(rows, wide).astype(BF16).astype(F32)
 
-    gradt = spread_taps(grad, plan, -1).T.astype(BF16)
-    parts = [nn(gradt, window(plan, actp, ky)) for ky in range(3)]
-    flat = [parts[t // 3][(t % 3) * local : (t % 3 + 1) * local] for t in range(9)]
+    act2t = stack_rows(plan, act2x.T, 1)
+    gradt = stack_rows(plan, spread_taps(grad, plan, -1).T, -1)
+    tails = nn(jnp.concatenate([gradt, act2t], axis=0), maps[:, 2 * head :])
+    first = jnp.concatenate([nn(gradt, maps[:, 0:head]), tails[0 : 3 * wide, 0:tail]], axis=1)
+    second = jnp.concatenate([nn(act2t, maps[:, head : 2 * head]), tails[3 * wide :, tail:]], axis=1)
+    flat = []
+    for t in range(9):
+        start = t // 3 * wide + t % 3 * local
+        flat.append(first[start : start + local])
     flat = jnp.concatenate(flat, axis=1)
     for block in range(d):
         value = flat[:, block * plan.block_rows : (block + 1) * plan.block_rows]
         held[block, 0 : plan.first_rows, :] = pack_first(plan, value)
-
-    act2t = act2x.T.astype(BF16)
-    flat = [nn(act2t, window(plan, cotp, 2 - ky))[0 : 3 * local] for ky in range(3)]
+    flat = [second[ky * wide : ky * wide + 3 * local] for ky in range(3)]
     rest = jnp.zeros((plan.piece_pad - plan.piece, c), F32)
     flat = jnp.concatenate([*flat, rest] if rest.shape[0] else flat, axis=0)
     for block in range(d):
@@ -394,32 +442,62 @@
         refs[-1][k] = ref[...]
 
 
-def last_kernel(plan, scale, n_stacks, *refs):
-    team, local, c, r = plan.team, plan.local, plan.channels, plan.block_rows
-    stacks = refs[0:n_stacks]
-    table1_ref, table2_ref, x_ref = refs[n_stacks : n_stacks + 3]
-    shares = refs[n_stacks + 3 : -8]
-    first_any, second_any, output_ref, held1, held2, first_ref, second_ref, sems = refs[-8:]
-    spot = own_spot(plan)
-    for slot in range(team):
-        piece = stacks[slot % n_stacks][slot // n_stacks, plan.first_rows :, :].astype(F32)
-        held2[spot ^ slot] = unpack_second(plan, piece).astype(BF16)
-    second_ref[...] = tn(held2[...].reshape(team * plan.piece_pad, c), table2_ref[...]) * scale
-    copy2 = pltpu.make_async_copy(second_ref, second_any, sems.at[0])
-    copy2.start()
-    for slot in range(team):
-        piece = stacks[slot % n_stacks][slot // n_stacks, 0 : plan.first_rows, :].astype(F32)
-        held1[spot ^ slot] = unpack_first(plan, piece)
-    stacked = held1[...].reshape(team * local, r).astype(BF16)
-    first_ref[...] = nn(table1_ref[...], stacked) * scale
-    copy1 = pltpu.make_async_copy(first_ref, first_any, sems.at[1])
-    copy1.start()
+def fold_layout(plan):
+    more = plan.block_rows - plan.packed
+    base, lanes = (plan.local, more) if more > 0 else (0, plan.block_rows)
+    chunk = folded_rows(plan, plan.local, lanes)
+    return base, chunk, -(-plan.local // chunk), lanes
+
+
+def first_in_place(plan, stack_ref, main_table, fold_table):
+    n = stack_ref.shape[0]
+    base, chunk, used, lanes = fold_layout(plan)
+    folded = stack_ref[:, base : base + chunk, :].astype(F32).reshape(n * chunk, plan.packed)
+    folded = [folded[:, k * lanes : (k + 1) * lanes] for k in range(used)]
+    first = nn(fold_table, jnp.concatenate(folded, axis=0).astype(BF16))
+    if not base:
+        return first
+    rows = stack_ref[:, 0 : plan.first_rows, :].reshape(n * plan.first_rows, plan.packed)
+    return jnp.concatenate([nn(main_table, rows), first], axis=1)
+
+
+def second_in_place(plan, stack_ref, table):
+    n, c = stack_ref.shape[0], plan.channels
+    rows = stack_ref[:, plan.first_rows :, :].reshape(n * plan.second_rows, plan.packed)
+    rows = [rows[:, k * c : (k + 1) * c] for k in range(plan.packed // c)]
+    return tn(jnp.concatenate(rows, axis=0), table)
+
+
+def part_kernel(plan, stack_ref, main_ref, fold_ref, second_ref, out1_ref, out2_ref):
+    out1_ref[...] = first_in_place(plan, stack_ref, main_ref[0], fold_ref[0])
+    out2_ref[...] = second_in_place(plan, stack_ref, second_ref[0])
+
+
+def last_kernel(plan, scale, n_came, *refs):
+    came, tables, part1_ref, part2_ref, x_ref = refs[0:n_came], refs[n_came : n_came + 3], *refs[n_came + 3 : n_came + 6]
+    shares = refs[n_came + 6 : -7]
+    first_any, second_any, output_any, first_ref, second_ref, output_ref, sems = refs[-7:]
     total = x_ref[...].astype(F32)
     for ref in shares:
         total = total + ref[...].reshape(total.shape).astype(F32)
     output_ref[...] = total.astype(BF16)
+    copy0 = pltpu.make_async_copy(output_ref, output_any, sems.at[2])
+    copy0.start()
+    first = part1_ref[...]
+    for ref in came:
+        first = first + first_in_place(plan, ref, tables[0][1], tables[1][1])
+    first_ref[...] = first * scale
+    copy1 = pltpu.make_async_copy(first_ref, first_any, sems.at[0])
+    copy1.start()
+    second = part2_ref[...]
+    for ref in came:
+        second = second + second_in_place(plan, ref, tables[2][1])
+    second_ref[...] = second * scale
+    copy2 = pltpu.make_async_copy(second_ref, second_any, sems.at[1])
+    copy2.start()
+    copy0.wait()
+    copy1.wait()
     copy2.wait()
-    copy1.wait()
 
 
 VMEM = pl.BlockSpec(memory_space=pltpu.VMEM)
@@ -490,9 +568,8 @@
         functools.partial(act_kernel, plan),
         "act",
         shape((plan.act_rows, 2 * c), BF16),
-        (timesteps, x, cot, pay),
+        (x, cot, timesteps.reshape(1, 1), pay),
         2,
-        n_smem=1,
         n_hbm=2,
         scratch=(
             pltpu.VMEM((pix, c), BF16),
@@ -512,13 +589,16 @@
         (slots[d // 2], *([slots[d // 4]] if d > 2 else [])),
         20,
     )
-    time_own, table1, table2 = call(
+    kinds, half = min(team, 2), -(-team // 2)
+    _, chunk, used, _ = fold_layout(plan)
+    time_own, *tables = call(
         functools.partial(time_kernel, plan),
         "time_own",
         (
             shape((plan.embed // c, plan.wide, c), BF16),
-            shape((c, team * local), BF16),
-            shape((team * plan.piece_pad, r), BF16),
+            shape((kinds, c, half * plan.first_rows), BF16),
+            shape((kinds, c, half * chunk * used), BF16),
+            shape((kinds, plan.packed // c * half * plan.second_rows, r), BF16),
         ),
         (time_weight.T,),
         0.001,
@@ -544,15 +624,13 @@
         6,
         n_smem=1,
         scratch=(
-            pltpu.VMEM((team, rows, c), BF16),
-            pltpu.VMEM((team, rows, c), BF16),
+            pltpu.VMEM((team * pix, 2 * c), BF16),
             pltpu.VMEM((d, local, r), F32),
             pltpu.VMEM((d, plan.piece_pad, c), F32),
             pltpu.VMEM((d, *both), F32),
         ),
     )
 
-    half = -(-team // 2)
     keep, away = call(
         functools.partial(share_kernel, plan),
         "share",
@@ -584,25 +662,31 @@
     same_spot = [[i * team + k for i in range(n_rep // team)] for k in range(team)]
     if n_rep > team:
         total = lax.psum(total, "rep", axis_index_groups=same_spot).astype(BF16)
-    stacks = [total[None]]
+    stack, came = total[None], []
     if team > 1:
         slots = [total] + [to_rep(total, step) for step in range(2, team, 2)]
-        stack = call(stack_kernel, "stack", shape((len(slots), *both), BF16), slots, 0.001)
-        stacks = [stack, to_rep(stack, 1)]
+        stack = call(stack_kernel, "stack", shape((half, *both), BF16), slots, 0.001)
+        came = [to_rep(stack, 1)]
+    part1, part2 = call(
+        functools.partial(part_kernel, plan),
+        "part",
+        (shape((c, r), F32), shape((c, r), F32)),
+        (stack, *tables),
+        0.001,
+    )
     first, second, output = call(
-        functools.partial(last_kernel, plan, scale, len(stacks)),
+        functools.partial(last_kernel, plan, scale, len(came)),
         "last",
         (shape((c, r), F32), shape((c, r), F32), shape((pix, c), BF16)),
-        (*stacks, table1, table2, x, *shares),
+        (*came, *tables, part1, part2, x, *shares),
         0.1,
         scratch=(
-            pltpu.VMEM((team, local, r), F32),
-            pltpu.VMEM((team, plan.piece_pad, c), BF16),
             pltpu.VMEM((c, r), F32),
             pltpu.VMEM((c, r), F32),
-            pltpu.SemaphoreType.DMA((2,)),
+            pltpu.VMEM((pix, c), BF16),
+            pltpu.SemaphoreType.DMA((3,)),
         ),
-        out_hbm=2,
+        out_hbm=3,
     )
     return output.reshape(1, height, width, c), first.T, second.T
 

time: 56.8 us -> 55.4 us (0.975)
  waiting for transfers between devices: 16.3 us -> 15.5 us
    ppermute x15, waiting for transfers between devices: 6.33 us -> 5.69 us  [to_rep(): return lax.ppermute(value, 'rep', [(i, i ^ step) for i in range(n_rep)])]
    pallas_call x10 -> x11, Pallas kernels: 13.2 us -> 12.7 us  [call(): pl.pallas_call(kernel, name=name, out_shape=out_shape, in_specs=[SMEM] *...]
  transfers between devices with their start and end apart: 21 -> 21, of which waited for: 9 -> 9; matrix products, arithmetic and copies ran while one was open for 0% -> 0% of each run, Pallas kernels for 2% -> 4%
where the time goes in v3:
time: 55.4 us; the launch traced here: 54.6 us
  starting transfers between devices  25 us (45%)
  waiting for transfers between devices  15.5 us (28%)
  Pallas kernels  12.7 us (23%)
  between operations  1.44 us (3%)
    ppermute x15, starting transfers between devices, to_rep(): return lax.ppermute(value, 'rep', [(i, i ^ step) for i in range(n_rep)])  14.9 us
    pallas_call x11, Pallas kernels, call(): pl.pallas_call(kernel, name=name, out_shape=out_shape, in_specs=[SMEM] *...  12.7 us
    ppermute x6, starting transfers between devices, to_dom(): return lax.ppermute(value, 'dom', [(i, i ^ step) for i in range(d)])  10.1 us
    ppermute x6, waiting for transfers between devices, to_dom(): return lax.ppermute(value, 'dom', [(i, i ^ step) for i in range(d)])  9.82 us
    ppermute x15, waiting for transfers between devices, to_rep(): return lax.ppermute(value, 'rep', [(i, i ^ step) for i in range(n_rep)])  5.69 us
  transfers between devices with their start and end apart: 21, of which 9 were waited for; matrix products, arithmetic and copies ran while one was open for 0% of the time, Pallas kernels for 4%

profile of v3, /device:TPU:0, one launch (start us, length us, event | category | flops | bytes accessed | tf_op | source)
XLA Modules:
  0.0 54.6 jit_solution(1623639456827738689)
XLA Ops:
  1.3 1.8 %slices.1.after_ref.refs_8_ = bf16[96,640]{1,0:T(8,128)(2,1)S(1)} custom-call(bf16[320,720]{1,0:T(8,128)(2,1)} %bitcast.16, bf16[320,720]{1,0:T(8,128)(2,1)} %bitcast.17), custom_call_target="tpu_custom_call" | custom-call | flops 2000000000 | bytes 6000000 | tf_op jit(solution)/shard_map/slices/pallas_call | solution.py:512
  3.2 0.9 %act.1.refs_0_ = bf16[144,640]{1,0:T(8,128)(2,1)S(1)} custom-call(bf16[128,320]{1,0:T(8,128)(2,1)S(1)} %bitcast.11, bf16[128,320]{1,0:T(8,128)(2,1)S(1)} %bitcast.13, s32[1,1]{1,0:T(1,128)} %bitcast.9.steps_ref, bf16[96,640]{1,0:T(8,128)(2,1)S(1)} %slices.1.after_ref.refs_8_), custom_call_target="tpu_custom_call" | custom-call | flops 2000000000 | bytes 6000000 | tf_op jit(solution)/shard_map/act/pallas_call | solution.py:512
  4.1 4.0 %collective-permute-start.5 = (bf16[144,640]{1,0:T(8,128)(2,1)S(1)}, bf16[144,640]{1,0:T(8,128)(2,1)S(1)}, u32[]{:S(2)}, u32[]{:S(2)}) collective-permute-start(bf16[144,640]{1,0:T(8,128)(2,1)S(1)} %act.1.refs_0_), channel_id=1, source_target_pairs={{0,24},{4,28},{8,16},{12,20},{16,8},{20,12},{24,0},{28,4},{1,25},{... | collective-permute-start | bytes 552968 | tf_op jit(solution)/shard_map/ppermute | solution.py:537
  8.1 0.5 collective-permute-start.3
  8.6 0.1 collective-permute-start.1
  8.7 3.0 %collective-permute-start.8 = (bf16[96,640]{1,0:T(8,128)(2,1)S(1)}, bf16[96,640]{1,0:T(8,128)(2,1)S(1)}, u32[]{:S(2)}, u32[]{:S(2)}) collective-permute-start(bf16[96,640]{1,0:T(8,128)(2,1)S(1)} %slices.1.after_ref.refs_8_), channel_id=1, source_target_pairs={{0,2},{1,3},{2,0},{3,1},{4,6},{5,7},{6,4},{7,5},{8,10},{9,11},{10,... | collective-permute-start | bytes 368648 | tf_op jit(solution)/shard_map/ppermute | solution.py:540
  11.7 1.6 %collective-permute-start.7 = (bf16[96,640]{1,0:T(8,128)(2,1)S(1)}, bf16[96,640]{1,0:T(8,128)(2,1)S(1)}, u32[]{:S(2)}, u32[]{:S(2)}) collective-permute-start(bf16[96,640]{1,0:T(8,128)(2,1)S(1)} %slices.1.after_ref.refs_8_), channel_id=1, source_target_pairs={{0,1},{1,0},{2,3},{3,2},{4,5},{5,4},{6,7},{7,6},{8,9},{9,8},{10,11... | collective-permute-start | bytes 368648 | tf_op jit(solution)/shard_map/ppermute | solution.py:540
  13.3 3.6 %collective-permute-done.8.pass_ref = bf16[96,640]{1,0:T(8,128)(2,1)S(1)} collective-permute-done((bf16[96,640]{1,0:T(8,128)(2,1)S(1)}, bf16[96,640]{1,0:T(8,128)(2,1)S(1)}, u32[]{:S(2)}, u32[]{:S(2)}) %collective-permute-start.8) | collective-permute-done | bytes 122912 | tf_op jit(solution)/shard_map/ppermute | solution.py:540
  16.9 0.5 collective-permute-start.6
  17.5 0.4 collective-permute-start.2
  17.9 1.1 %collective-permute-start.9 = (bf16[96,640]{1,0:T(8,128)(2,1)S(1)}, bf16[96,640]{1,0:T(8,128)(2,1)S(1)}, u32[]{:S(2)}, u32[]{:S(2)}) collective-permute-start(bf16[96,640]{1,0:T(8,128)(2,1)S(1)} %relay.1.refs_10_), channel_id=1, source_target_pairs={{0,1},{1,0},{2,3},{3,2},{4,5},{5,4},{6,7},{7,6},{8,9},{9,8},{10,11... | collective-permute-start | bytes 368648 | tf_op jit(solution)/shard_map/ppermute | solution.py:540
  19.0 1.4 %time_own.1 = (bf16[4,128,320]{2,1,0:T(8,128)(2,1)S(1)}, bf16[2,320,192]{2,1,0:T(8,128)(2,1)S(1)}, bf16[2,320,160]{2,1,0:T(8,128)(2,1)S(1)}, bf16[2,384,720]{2,1,0:T(8,128)(2,1)S(1)}) custom-call(bf16[320,1280]{1,0:T(8,128)(2,1)S(1)} %bitcast.10), custom_call_target="tpu_custom_call" | custom-call | flops 1000000 | bytes 3000 | tf_op jit(solution)/shard_map/time_own/pallas_call | solution.py:512
  20.5 2.9 %collective-permute-done.9.refs_11_ = bf16[96,640]{1,0:T(8,128)(2,1)S(1)} collective-permute-done((bf16[96,640]{1,0:T(8,128)(2,1)S(1)}, bf16[96,640]{1,0:T(8,128)(2,1)S(1)}, u32[]{:S(2)}, u32[]{:S(2)}) %collective-permute-start.9) | collective-permute-done | bytes 122912 | tf_op jit(solution)/shard_map/ppermute | solution.py:540
  23.3 4.9 %main.1 = (bf16[8,160,128]{2,1,0:T(8,128)(2,1)S(1)}, bf16[384,320]{1,0:T(8,128)(2,1)S(1)}, f32[96,640]{1,0:T(8,128)S(1)}, bf16[96,640]{1,0:T(8,128)(2,1)S(1)}, b...) custom-call(s32[4]{0:T(128)S(1)} %copy-done.3, bf16[144,640]{1,0:T(8,128)(2,1)S(1)} %act.1.refs_0_, ...), custom_call_target="tpu_custom_call" | custom-call | flops 6000000000 | bytes 18000000 | tf_op jit(solution)/shard_map/main/pallas_call | solution.py:512
  28.2 0.8 %share.1 = (f32[4,128,320]{2,1,0:T(8,128)S(1)}, bf16[4,128,320]{2,1,0:T(8,128)(2,1)S(1)}) custom-call(bf16[8,160,128]{2,1,0:T(8,128)(2,1)S(1)} %get-tuple-element.29.act2p, bf16[384,320]{1,0:T(8,128)(2,1)S(1)} %get-tuple-element.30.w2_ref, f32[96,640]{1,0:T(8,128)S(1)} %get-tuple-element.25.after_ref.refs_0_), custom_call_target="tpu_custom_call" | custom-call | flops 1000000 | bytes 3000 | tf_op jit(solution)/shard_map/share/pallas_call | solution.py:512
  29.1 1.1 %collective-permute-start.10 = (bf16[96,640]{1,0:T(8,128)(2,1)S(1)}, bf16[96,640]{1,0:T(8,128)(2,1)S(1)}, u32[]{:S(2)}, u32[]{:S(2)}) collective-permute-start(bf16[96,640]{1,0:T(8,128)(2,1)S(1)} %get-tuple-element.26), channel_id=1, source_target_pairs={{0,1},{1,0},{2,3},{3,2},{4,5},{5,4},{6,7},{7,6},{8,9},{9,8},{10,11... | collective-permute-start | bytes 368648 | tf_op jit(solution)/shard_map/ppermute | solution.py:540
  30.2 3.0 %collective-permute-start.11 = (bf16[96,640]{1,0:T(8,128)(2,1)S(1)}, bf16[96,640]{1,0:T(8,128)(2,1)S(1)}, u32[]{:S(2)}, u32[]{:S(2)}) collective-permute-start(bf16[96,640]{1,0:T(8,128)(2,1)S(1)} %get-tuple-element.27), channel_id=1, source_target_pairs={{0,2},{1,3},{2,0},{3,1},{4,6},{5,7},{6,4},{7,5},{8,10},{9,11},{10,... | collective-permute-start | bytes 368648 | tf_op jit(solution)/shard_map/ppermute | solution.py:540
  33.1 0.4 collective-permute-start.12
  33.6 1.6 %collective-permute-start.14 = (bf16[128,320]{1,0:T(8,128)(2,1)S(1)}, bf16[128,320]{1,0:T(8,128)(2,1)S(1)}, u32[]{:S(2)}, u32[]{:S(2)}) collective-permute-start(bf16[128,320]{1,0:T(8,128)(2,1)S(1)} %get-tuple-element.33), channel_id=1, source_target_pairs={{0,8},{4,12},{8,0},{12,4},{16,24},{20,28},{24,16},{28,20},{1,9},{5... | collective-permute-start | bytes 245768 | tf_op jit(solution)/shard_map/ppermute | solution.py:537
  35.2 1.5 %collective-permute-start.15 = (bf16[128,320]{1,0:T(8,128)(2,1)S(1)}, bf16[128,320]{1,0:T(8,128)(2,1)S(1)}, u32[]{:S(2)}, u32[]{:S(2)}) collective-permute-start(bf16[128,320]{1,0:T(8,128)(2,1)S(1)} %get-tuple-element.34), channel_id=1, source_target_pairs={{0,16},{4,20},{8,24},{12,28},{16,0},{20,4},{24,8},{28,12},{1,17},{... | collective-permute-start | bytes 245768 | tf_op jit(solution)/shard_map/ppermute | solution.py:537
  36.7 0.4 collective-permute-done.10.refs_1_
  37.1 2.5 %collective-permute-start.16 = (bf16[128,320]{1,0:T(8,128)(2,1)S(1)}, bf16[128,320]{1,0:T(8,128)(2,1)S(1)}, u32[]{:S(2)}, u32[]{:S(2)}) collective-permute-start(bf16[128,320]{1,0:T(8,128)(2,1)S(1)} %get-tuple-element.35), channel_id=1, source_target_pairs={{0,24},{4,28},{8,16},{12,20},{16,8},{20,12},{24,0},{28,4},{1,25},{... | collective-permute-start | bytes 245768 | tf_op jit(solution)/shard_map/ppermute | solution.py:537
  39.6 2.9 %collective-permute-done.11.refs_2_ = bf16[96,640]{1,0:T(8,128)(2,1)S(1)} collective-permute-done((bf16[96,640]{1,0:T(8,128)(2,1)S(1)}, bf16[96,640]{1,0:T(8,128)(2,1)S(1)}, u32[]{:S(2)}, u32[]{:S(2)}) %collective-permute-start.11) | collective-permute-done | bytes 122912 | tf_op jit(solution)/shard_map/ppermute | solution.py:540
  42.7 2.6 %collective-permute-start.19 = (bf16[96,640]{1,0:T(8,128)(2,1)S(1)}, bf16[96,640]{1,0:T(8,128)(2,1)S(1)}, u32[]{:S(2)}, u32[]{:S(2)}) collective-permute-start(bf16[96,640]{1,0:T(8,128)(2,1)S(1)} %total.1.refs_0_), channel_id=1, source_target_pairs={{0,24},{4,28},{8,16},{12,20},{16,8},{20,12},{24,0},{28,4},{1,25},{... | collective-permute-start | bytes 368648 | tf_op jit(solution)/shard_map/ppermute | solution.py:537
  45.3 0.5 collective-permute-start.18
  45.8 0.5 collective-permute-start.17
  46.3 3.3 %collective-permute-done.19.refs_3_ = bf16[96,640]{1,0:T(8,128)(2,1)S(1)} collective-permute-done((bf16[96,640]{1,0:T(8,128)(2,1)S(1)}, bf16[96,640]{1,0:T(8,128)(2,1)S(1)}, u32[]{:S(2)}, u32[]{:S(2)}) %collective-permute-start.19) | collective-permute-done | bytes 122912 | tf_op jit(solution)/shard_map/ppermute | solution.py:537
  49.5 1.0 %collective-permute-done.18.refs_2_ = bf16[96,640]{1,0:T(8,128)(2,1)S(1)} collective-permute-done((bf16[96,640]{1,0:T(8,128)(2,1)S(1)}, bf16[96,640]{1,0:T(8,128)(2,1)S(1)}, u32[]{:S(2)}, u32[]{:S(2)}) %collective-permute-start.18) | collective-permute-done | bytes 122912 | tf_op jit(solution)/shard_map/ppermute | solution.py:537
  50.5 0.2 collective-permute-done.17.refs_1_
  50.8 0.6 %part.1 = (f32[320,720]{1,0:T(8,128)S(1)}, f32[320,720]{1,0:T(8,128)S(1)}) custom-call(bf16[4,96,640]{2,1,0:T(8,128)(2,1)S(1)} %stack.1.stack_ref, bf16[2,320,192]{2,1,0:T(8,128)(2,1)S(1)} %get-tuple-element.36.main_ref.refs_1_, bf16[2,320,160]{2,1,0:T(8,128)(2,1)S(1)} %get-tuple-element.37.fold_ref.refs_2_, ...), custom_call_target="tpu_custom_call" | custom-call | flops 1000000 | bytes 3000 | tf_op jit(solution)/shard_map/part/pallas_call | solution.py:512
  51.4 1.2 %collective-permute-done.20.refs_0_ = bf16[4,96,640]{2,1,0:T(8,128)(2,1)S(1)} collective-permute-done((bf16[4,96,640]{2,1,0:T(8,128)(2,1)S(1)}, bf16[4,96,640]{2,1,0:T(8,128)(2,1)S(1)}, u32[]{:S(2)}, u32[]{:S(2)}) %collective-permute-start.20) | collective-permute-done | bytes 491552 | tf_op jit(solution)/shard_map/ppermute | solution.py:537
  52.6 2.0 %last.1 = (f32[320,720]{1,0:T(8,128)}, f32[320,720]{1,0:T(8,128)}, bf16[128,320]{1,0:T(8,128)(2,1)}) custom-call(bf16[4,96,640]{2,1,0:T(8,128)(2,1)S(1)} %collective-permute-done.20.refs_0_, bf16[2,320,192]{2,1,0:T(8,128)(2,1)S(1)} %get-tuple-element.36.main_ref.refs_1_, bf16[2,320,160]{2,1,0:T(8,128)(2,1)S(1)} %get-tuple-element.37.fold_ref.refs_2_, ...), custom_call_target="tpu_custom_call" | custom-call | flops 100000000 | bytes 300000 | tf_op jit(solution)/shard_map/last/pallas_call | solution.py:512
  (29 shorter events, 0.5 us)
Async XLA Ops:
  1.3 1.9 %copy-start.1 = (bf16[1,8,16,320]{3,2,1,0:T(8,128)(2,1)S(1)}, bf16[1,8,16,320]{3,2,1,0:T(8,128)(2,1)}, u32[]{:S(2)}) copy-start(bf16[1,8,16,320]{3,2,1,0:T(8,128)(2,1)} %param.7) | copy-start | bytes 245764
  1.3 1.9 %copy-start.2 = (bf16[1,8,16,320]{3,2,1,0:T(8,128)(2,1)S(1)}, bf16[1,8,16,320]{3,2,1,0:T(8,128)(2,1)}, u32[]{:S(2)}) copy-start(bf16[1,8,16,320]{3,2,1,0:T(8,128)(2,1)} %param.8) | copy-start | bytes 245764
  4.1 14.9 %copy-start = (bf16[1280,320]{0,1:T(8,128)(2,1)S(1)}, bf16[1280,320]{0,1:T(8,128)(2,1)}, u32[]{:S(2)}) copy-start(bf16[1280,320]{0,1:T(8,128)(2,1)} %param.11) | copy-start | bytes 2457604
  4.1 19.3 %copy-start.3 = (s32[4]{0:T(128)S(1)}, s32[4]{0:T(128)}, u32[]{:S(2)}) copy-start(s32[4]{0:T(128)} %owner_ref.1) | copy-start | bytes 52
  4.1 12.8 %collective-permute-start.5 = (bf16[144,640]{1,0:T(8,128)(2,1)S(1)}, bf16[144,640]{1,0:T(8,128)(2,1)S(1)}, u32[]{:S(2)}, u32[]{:S(2)}) collective-permute-start(bf16[144,640]{1,0:T(8,128)(2,1)S(1)} %act.1.refs_0_), channel_id=1, source_target_pairs={{0,24},{4,28},{8,16},{12,20},{16,8},{20,12},{24,0},{28,4},{1,25},{... | collective-permute-start | bytes 552968 | tf_op jit(solution)/shard_map/ppermute | solution.py:537
  8.1 9.4 %collective-permute-start.3 = (bf16[144,640]{1,0:T(8,128)(2,1)S(1)}, bf16[144,640]{1,0:T(8,128)(2,1)S(1)}, u32[]{:S(2)}, u32[]{:S(2)}) collective-permute-start(bf16[144,640]{1,0:T(8,128)(2,1)S(1)} %act.1.refs_0_), channel_id=1, source_target_pairs={{0,16},{4,20},{8,24},{12,28},{16,0},{20,4},{24,8},{28,12},{1,17},{... | collective-permute-start | bytes 552968 | tf_op jit(solution)/shard_map/ppermute | solution.py:537
  8.6 8.9 %collective-permute-start.1 = (bf16[144,640]{1,0:T(8,128)(2,1)S(1)}, bf16[144,640]{1,0:T(8,128)(2,1)S(1)}, u32[]{:S(2)}, u32[]{:S(2)}) collective-permute-start(bf16[144,640]{1,0:T(8,128)(2,1)S(1)} %act.1.refs_0_), channel_id=1, source_target_pairs={{0,8},{4,12},{8,0},{12,4},{16,24},{20,28},{24,16},{28,20},{1,9},{5... | collective-permute-start | bytes 552968 | tf_op jit(solution)/shard_map/ppermute | solution.py:537
  8.7 8.2 %collective-permute-start.8 = (bf16[96,640]{1,0:T(8,128)(2,1)S(1)}, bf16[96,640]{1,0:T(8,128)(2,1)S(1)}, u32[]{:S(2)}, u32[]{:S(2)}) collective-permute-start(bf16[96,640]{1,0:T(8,128)(2,1)S(1)} %slices.1.after_ref.refs_8_), channel_id=1, source_target_pairs={{0,2},{1,3},{2,0},{3,1},{4,6},{5,7},{6,4},{7,5},{8,10},{9,11},{10,... | collective-permute-start | bytes 368648 | tf_op jit(solution)/shard_map/ppermute | solution.py:540
  11.7 6.3 %collective-permute-start.7 = (bf16[96,640]{1,0:T(8,128)(2,1)S(1)}, bf16[96,640]{1,0:T(8,128)(2,1)S(1)}, u32[]{:S(2)}, u32[]{:S(2)}) collective-permute-start(bf16[96,640]{1,0:T(8,128)(2,1)S(1)} %slices.1.after_ref.refs_8_), channel_id=1, source_target_pairs={{0,1},{1,0},{2,3},{3,2},{4,5},{5,4},{6,7},{7,6},{8,9},{9,8},{10,11... | collective-permute-start | bytes 368648 | tf_op jit(solution)/shard_map/ppermute | solution.py:540
  16.9 3.5 %collective-permute-start = (bf16[144,640]{1,0:T(8,128)(2,1)S(1)}, bf16[144,640]{1,0:T(8,128)(2,1)S(1)}, u32[]{:S(2)}, u32[]{:S(2)}) collective-permute-start(bf16[144,640]{1,0:T(8,128)(2,1)S(1)} %act.1.refs_0_), channel_id=1, source_target_pairs={{0,4},{4,0},{8,12},{12,8},{16,20},{20,16},{24,28},{28,24},{1,5},{5... | collective-permute-start | bytes 552968 | tf_op jit(solution)/shard_map/ppermute | solution.py:537
  16.9 6.4 %collective-permute-start.6 = (bf16[144,640]{1,0:T(8,128)(2,1)S(1)}, bf16[144,640]{1,0:T(8,128)(2,1)S(1)}, u32[]{:S(2)}, u32[]{:S(2)}) collective-permute-start(bf16[144,640]{1,0:T(8,128)(2,1)S(1)} %collective-permute-done.5.refs_6_), channel_id=1, source_target_pairs={{0,4},{4,0},{8,12},{12,8},{16,20},{20,16},{24,28},{28,24},{1,5},{5... | collective-permute-start | bytes 552968 | tf_op jit(solution)/shard_map/ppermute | solution.py:537
  17.4 5.9 %collective-permute-start.4 = (bf16[144,640]{1,0:T(8,128)(2,1)S(1)}, bf16[144,640]{1,0:T(8,128)(2,1)S(1)}, u32[]{:S(2)}, u32[]{:S(2)}) collective-permute-start(bf16[144,640]{1,0:T(8,128)(2,1)S(1)} %collective-permute-done.3.refs_4_), channel_id=1, source_target_pairs={{0,4},{4,0},{8,12},{12,8},{16,20},{20,16},{24,28},{28,24},{1,5},{5... | collective-permute-start | bytes 552968 | tf_op jit(solution)/shard_map/ppermute | solution.py:537
  17.5 5.8 %collective-permute-start.2 = (bf16[144,640]{1,0:T(8,128)(2,1)S(1)}, bf16[144,640]{1,0:T(8,128)(2,1)S(1)}, u32[]{:S(2)}, u32[]{:S(2)}) collective-permute-start(bf16[144,640]{1,0:T(8,128)(2,1)S(1)} %collective-permute-done.1.refs_2_), channel_id=1, source_target_pairs={{0,4},{4,0},{8,12},{12,8},{16,20},{20,16},{24,28},{28,24},{1,5},{5... | collective-permute-start | bytes 552968 | tf_op jit(solution)/shard_map/ppermute | solution.py:537
  17.9 5.4 %collective-permute-start.9 = (bf16[96,640]{1,0:T(8,128)(2,1)S(1)}, bf16[96,640]{1,0:T(8,128)(2,1)S(1)}, u32[]{:S(2)}, u32[]{:S(2)}) collective-permute-start(bf16[96,640]{1,0:T(8,128)(2,1)S(1)} %relay.1.refs_10_), channel_id=1, source_target_pairs={{0,1},{1,0},{2,3},{3,2},{4,5},{5,4},{6,7},{7,6},{8,9},{9,8},{10,11... | collective-permute-start | bytes 368648 | tf_op jit(solution)/shard_map/ppermute | solution.py:540
  29.0 4.5 %collective-permute-start.13 = (bf16[4,128,320]{2,1,0:T(8,128)(2,1)S(1)}, bf16[4,128,320]{2,1,0:T(8,128)(2,1)S(1)}, u32[]{:S(2)}, u32[]{:S(2)}) collective-permute-start(bf16[4,128,320]{2,1,0:T(8,128)(2,1)S(1)} %get-tuple-element.32), channel_id=1, source_target_pairs={{0,4},{4,0},{8,12},{12,8},{16,20},{20,16},{24,28},{28,24},{1,5},{5... | collective-permute-start | bytes 983048 | tf_op jit(solution)/shard_map/ppermute | solution.py:537
  29.1 8.0 %collective-permute-start.10 = (bf16[96,640]{1,0:T(8,128)(2,1)S(1)}, bf16[96,640]{1,0:T(8,128)(2,1)S(1)}, u32[]{:S(2)}, u32[]{:S(2)}) collective-permute-start(bf16[96,640]{1,0:T(8,128)(2,1)S(1)} %get-tuple-element.26), channel_id=1, source_target_pairs={{0,1},{1,0},{2,3},{3,2},{4,5},{5,4},{6,7},{7,6},{8,9},{9,8},{10,11... | collective-permute-start | bytes 368648 | tf_op jit(solution)/shard_map/ppermute | solution.py:540
  30.2 12.4 %collective-permute-start.11 = (bf16[96,640]{1,0:T(8,128)(2,1)S(1)}, bf16[96,640]{1,0:T(8,128)(2,1)S(1)}, u32[]{:S(2)}, u32[]{:S(2)}) collective-permute-start(bf16[96,640]{1,0:T(8,128)(2,1)S(1)} %get-tuple-element.27), channel_id=1, source_target_pairs={{0,2},{1,3},{2,0},{3,1},{4,6},{5,7},{6,4},{7,5},{8,10},{9,11},{10,... | collective-permute-start | bytes 368648 | tf_op jit(solution)/shard_map/ppermute | solution.py:540
  33.1 9.4 %collective-permute-start.12 = (bf16[96,640]{1,0:T(8,128)(2,1)S(1)}, bf16[96,640]{1,0:T(8,128)(2,1)S(1)}, u32[]{:S(2)}, u32[]{:S(2)}) collective-permute-start(bf16[96,640]{1,0:T(8,128)(2,1)S(1)} %get-tuple-element.28), channel_id=1, source_target_pairs={{0,3},{1,2},{2,1},{3,0},{4,7},{5,6},{6,5},{7,4},{8,11},{9,10},{10,... | collective-permute-start | bytes 368648 | tf_op jit(solution)/shard_map/ppermute | solution.py:540
  33.6 8.9 %collective-permute-start.14 = (bf16[128,320]{1,0:T(8,128)(2,1)S(1)}, bf16[128,320]{1,0:T(8,128)(2,1)S(1)}, u32[]{:S(2)}, u32[]{:S(2)}) collective-permute-start(bf16[128,320]{1,0:T(8,128)(2,1)S(1)} %get-tuple-element.33), channel_id=1, source_target_pairs={{0,8},{4,12},{8,0},{12,4},{16,24},{20,28},{24,16},{28,20},{1,9},{5... | collective-permute-start | bytes 245768 | tf_op jit(solution)/shard_map/ppermute | solution.py:537
  35.2 7.3 %collective-permute-start.15 = (bf16[128,320]{1,0:T(8,128)(2,1)S(1)}, bf16[128,320]{1,0:T(8,128)(2,1)S(1)}, u32[]{:S(2)}, u32[]{:S(2)}) collective-permute-start(bf16[128,320]{1,0:T(8,128)(2,1)S(1)} %get-tuple-element.34), channel_id=1, source_target_pairs={{0,16},{4,20},{8,24},{12,28},{16,0},{20,4},{24,8},{28,12},{1,17},{... | collective-permute-start | bytes 245768 | tf_op jit(solution)/shard_map/ppermute | solution.py:537
  37.1 5.5 %collective-permute-start.16 = (bf16[128,320]{1,0:T(8,128)(2,1)S(1)}, bf16[128,320]{1,0:T(8,128)(2,1)S(1)}, u32[]{:S(2)}, u32[]{:S(2)}) collective-permute-start(bf16[128,320]{1,0:T(8,128)(2,1)S(1)} %get-tuple-element.35), channel_id=1, source_target_pairs={{0,24},{4,28},{8,16},{12,20},{16,8},{20,12},{24,0},{28,4},{1,25},{... | collective-permute-start | bytes 245768 | tf_op jit(solution)/shard_map/ppermute | solution.py:537
  42.7 6.8 %collective-permute-start.19 = (bf16[96,640]{1,0:T(8,128)(2,1)S(1)}, bf16[96,640]{1,0:T(8,128)(2,1)S(1)}, u32[]{:S(2)}, u32[]{:S(2)}) collective-permute-start(bf16[96,640]{1,0:T(8,128)(2,1)S(1)} %total.1.refs_0_), channel_id=1, source_target_pairs={{0,24},{4,28},{8,16},{12,20},{16,8},{20,12},{24,0},{28,4},{1,25},{... | collective-permute-start | bytes 368648 | tf_op jit(solution)/shard_map/ppermute | solution.py:537
  45.3 5.2 %collective-permute-start.18 = (bf16[96,640]{1,0:T(8,128)(2,1)S(1)}, bf16[96,640]{1,0:T(8,128)(2,1)S(1)}, u32[]{:S(2)}, u32[]{:S(2)}) collective-permute-start(bf16[96,640]{1,0:T(8,128)(2,1)S(1)} %total.1.refs_0_), channel_id=1, source_target_pairs={{0,16},{4,20},{8,24},{12,28},{16,0},{20,4},{24,8},{28,12},{1,17},{... | collective-permute-start | bytes 368648 | tf_op jit(solution)/shard_map/ppermute | solution.py:537
  45.8 4.9 %collective-permute-start.17 = (bf16[96,640]{1,0:T(8,128)(2,1)S(1)}, bf16[96,640]{1,0:T(8,128)(2,1)S(1)}, u32[]{:S(2)}, u32[]{:S(2)}) collective-permute-start(bf16[96,640]{1,0:T(8,128)(2,1)S(1)} %total.1.refs_0_), channel_id=1, source_target_pairs={{0,8},{4,12},{8,0},{12,4},{16,24},{20,28},{24,16},{28,20},{1,9},{5... | collective-permute-start | bytes 368648 | tf_op jit(solution)/shard_map/ppermute | solution.py:537
  50.7 1.9 %collective-permute-start.20 = (bf16[4,96,640]{2,1,0:T(8,128)(2,1)S(1)}, bf16[4,96,640]{2,1,0:T(8,128)(2,1)S(1)}, u32[]{:S(2)}, u32[]{:S(2)}) collective-permute-start(bf16[4,96,640]{2,1,0:T(8,128)(2,1)S(1)} %stack.1.stack_ref), channel_id=1, source_target_pairs={{0,4},{4,0},{8,12},{12,8},{16,20},{20,16},{24,28},{28,24},{1,5},{5... | collective-permute-start | bytes 1474568 | tf_op jit(solution)/shard_map/ppermute | solution.py:537

commit v4 on v3

--- a/solution.py
+++ b/solution.py
@@ -186,7 +186,7 @@
     copies[0].wait()
     pay_ref[0 : plan.first_rows, :] = pack_first(plan, nn(pick1, w1_ref[...])).astype(BF16)
     copies[1].wait()
-    pay_ref[plan.first_rows :, :] = pack_second(plan, nn(w2_ref[...], pick2).T[0 : plan.piece_pad]).astype(BF16)
+    pay_ref[plan.first_rows : plan.first_rows + plan.second_rows, :] = pack_second(plan, nn(w2_ref[...], pick2).T[0 : plan.piece_pad]).astype(BF16)
 
 
 def act_kernel(plan, x_any, cot_any, steps_ref, after_ref, act_ref, x_ref, cot_ref, sems):
@@ -221,10 +221,10 @@
 
 
 def relay_kernel(pass_ref, *refs):
-    refs[-1][...] = pass_ref[...]
-
-
-def time_kernel(plan, tw_ref, out_ref, main_ref, fold_ref, second_ref):
+    refs[-1][...] = pass_ref[0 : refs[-1].shape[0], :]
+
+
+def time_kernel(plan, tw_ref, out_ref):
     c = plan.channels
     spot = own_spot(plan)
     row, col = iota((plan.wide, c), 0), iota((plan.wide, c), 1)
@@ -233,6 +233,10 @@
     for part in range(plan.embed // c):
         out_ref[part] = own[:, part * c : (part + 1) * c].astype(BF16)
 
+
+def table_kernel(plan, after_ref, main_ref, fold_ref, second_ref):
+    del after_ref
+    c, spot = plan.channels, own_spot(plan)
     n = -(-plan.team // 2)
     base, chunk, used, _ = fold_layout(plan)
     for kind in range(main_ref.shape[0]):
@@ -341,7 +345,7 @@
     for slot in range(d):
         block = logical_of(plan, owner_ref, here ^ slot)
         w1st[block] = unpack_first(plan, slices[slot][0 : plan.first_rows, :].astype(F32))
-        w2st[block] = unpack_second(plan, slices[slot][plan.first_rows :, :].astype(F32))
+        w2st[block] = unpack_second(plan, slices[slot][plan.first_rows : plan.first_rows + plan.second_rows, :].astype(F32))
     flat = jnp.concatenate([w1st[b] for b in range(d)], axis=1)
     zeros = [jnp.zeros((wide - 3 * local, c), F32)] if wide > 3 * local else []
     w1 = []
@@ -553,7 +557,7 @@
     pay = call(
         functools.partial(slice_kernel, plan),
         "slices",
-        shape((plan.first_rows + plan.second_rows, plan.packed), BF16),
+        shape((plan.first_rows + plan.second_rows + 0, plan.packed), BF16),
         (first_weight.T, second_weight.T),
         2,
         n_hbm=2,
@@ -585,23 +589,18 @@
     slots[d // 2] = call(
         relay_kernel,
         "relay",
-        shape(pay.shape, BF16),
+        shape((plan.first_rows + plan.second_rows, plan.packed), BF16),
         (slots[d // 2], *([slots[d // 4]] if d > 2 else [])),
         20,
     )
     kinds, half = min(team, 2), -(-team // 2)
     _, chunk, used, _ = fold_layout(plan)
-    time_own, *tables = call(
+    time_own = call(
         functools.partial(time_kernel, plan),
         "time_own",
-        (
-            shape((plan.embed // c, plan.wide, c), BF16),
-            shape((kinds, c, half * plan.first_rows), BF16),
-            shape((kinds, c, half * chunk * used), BF16),
-            shape((kinds, plan.packed // c * half * plan.second_rows, r), BF16),
-        ),
+        shape((plan.embed // c, plan.wide, c), BF16),
         (time_weight.T,),
-        0.001,
+        5,
     )
     bit = d // 4
     while bit:
@@ -649,12 +648,24 @@
         )
         shares = [pairs[0]] + [to_rep(pairs[k], 2 * k) for k in range(1, half)]
 
+    tables = call(
+        functools.partial(table_kernel, plan),
+        "tables",
+        (
+            shape((kinds, c, half * plan.first_rows), BF16),
+            shape((kinds, c, half * chunk * used), BF16),
+            shape((kinds, plan.packed // c * half * plan.second_rows, r), BF16),
+        ),
+        (shares[0],),
+        0.001,
+    )
+
     parts = [pieces[0]] + [to_dom(pieces[step], step) for step in range(1, d)]
     total = call(
         functools.partial(total_kernel, d),
         "total",
         shape(both, BF16 if n_rep == team else F32),
-        (*parts, *shares[1:]),
+        (*parts, *shares[1:], tables[0]),
         0.001,
     )
 

time: 55.4 us -> 53.1 us (0.958); the launches traced: 54.6 us -> 53 us
  starting transfers between devices: 25 us -> 23.1 us
    ppermute x15, waiting for transfers between devices: 5.69 us -> 12.5 us  [to_rep(): return lax.ppermute(value, 'rep', [(i, i ^ step) for i in range(n_rep)])]
    ppermute x6, waiting for transfers between devices: 9.82 us -> 3.38 us  [to_dom(): return lax.ppermute(value, 'dom', [(i, i ^ step) for i in range(d)])]
    ppermute x15, starting transfers between devices: 14.9 us -> 12 us  [to_rep(): return lax.ppermute(value, 'rep', [(i, i ^ step) for i in range(n_rep)])]
    ppermute x6, starting transfers between devices: 10.1 us -> 11.1 us  [to_dom(): return lax.ppermute(value, 'dom', [(i, i ^ step) for i in range(d)])]
    pallas_call x11 -> x12, Pallas kernels: 12.7 us -> 12.5 us  [call(): pl.pallas_call(kernel, name=name, out_shape=out_shape, in_specs=[SMEM] *...]
  transfers between devices with their start and end apart: 21 -> 21, of which waited for: 9 -> 10; matrix products, arithmetic and copies ran while one was open for 0% -> 0% of each run, Pallas kernels for 4% -> 5%
where the time goes in v4:
time: 53.1 us; the launch traced here: 53 us
  starting transfers between devices  23.1 us (44%)
  waiting for transfers between devices  15.9 us (30%)
  Pallas kernels  12.5 us (24%)
  between operations  1.45 us (3%)
    ppermute x15, waiting for transfers between devices, to_rep(): return lax.ppermute(value, 'rep', [(i, i ^ step) for i in range(n_rep)])  12.5 us
    pallas_call x12, Pallas kernels, call(): pl.pallas_call(kernel, name=name, out_shape=out_shape, in_specs=[SMEM] *...  12.5 us
    ppermute x15, starting transfers between devices, to_rep(): return lax.ppermute(value, 'rep', [(i, i ^ step) for i in range(n_rep)])  12 us
    ppermute x6, starting transfers between devices, to_dom(): return lax.ppermute(value, 'dom', [(i, i ^ step) for i in range(d)])  11.1 us
    ppermute x6, waiting for transfers between devices, to_dom(): return lax.ppermute(value, 'dom', [(i, i ^ step) for i in range(d)])  3.38 us
  transfers between devices with their start and end apart: 21, of which 10 were waited for; matrix products, arithmetic and copies ran while one was open for 0% of the time, Pallas kernels for 5%

profile of v4, /device:TPU:0, one launch (start us, length us, event | category | flops | bytes accessed | tf_op | source)
XLA Modules:
  0.0 53.0 jit_solution(5710208815739628142)
XLA Ops:
  0.7 1.8 %slices.1.after_ref.refs_8_ = bf16[96,640]{1,0:T(8,128)(2,1)S(1)} custom-call(bf16[320,720]{1,0:T(8,128)(2,1)} %bitcast.16, bf16[320,720]{1,0:T(8,128)(2,1)} %bitcast.17), custom_call_target="tpu_custom_call" | custom-call | flops 2000000000 | bytes 6000000 | tf_op jit(solution)/shard_map/slices/pallas_call | solution.py:516
  2.5 4.1 %collective-permute-start.8 = (bf16[96,640]{1,0:T(8,128)(2,1)S(1)}, bf16[96,640]{1,0:T(8,128)(2,1)S(1)}, u32[]{:S(2)}, u32[]{:S(2)}) collective-permute-start(bf16[96,640]{1,0:T(8,128)(2,1)S(1)} %slices.1.after_ref.refs_8_), channel_id=1, source_target_pairs={{0,2},{1,3},{2,0},{3,1},{4,6},{5,7},{6,4},{7,5},{8,10},{9,11},{10,... | collective-permute-start | bytes 368648 | tf_op jit(solution)/shard_map/ppermute | solution.py:544
  6.6 1.6 %collective-permute-start.7 = (bf16[96,640]{1,0:T(8,128)(2,1)S(1)}, bf16[96,640]{1,0:T(8,128)(2,1)S(1)}, u32[]{:S(2)}, u32[]{:S(2)}) collective-permute-start(bf16[96,640]{1,0:T(8,128)(2,1)S(1)} %slices.1.after_ref.refs_8_), channel_id=1, source_target_pairs={{0,1},{1,0},{2,3},{3,2},{4,5},{5,4},{6,7},{7,6},{8,9},{9,8},{10,11... | collective-permute-start | bytes 368648 | tf_op jit(solution)/shard_map/ppermute | solution.py:544
  8.8 0.9 %act.1.refs_0_ = bf16[144,640]{1,0:T(8,128)(2,1)S(1)} custom-call(bf16[128,320]{1,0:T(8,128)(2,1)S(1)} %bitcast.10, bf16[128,320]{1,0:T(8,128)(2,1)S(1)} %bitcast.13, s32[1,1]{1,0:T(1,128)} %bitcast.9.steps_ref, bf16[96,640]{1,0:T(8,128)(2,1)S(1)} %slices.1.after_ref.refs_8_), custom_call_target="tpu_custom_call" | custom-call | flops 2000000000 | bytes 6000000 | tf_op jit(solution)/shard_map/act/pallas_call | solution.py:516
  9.8 2.5 %collective-permute-start.5 = (bf16[144,640]{1,0:T(8,128)(2,1)S(1)}, bf16[144,640]{1,0:T(8,128)(2,1)S(1)}, u32[]{:S(2)}, u32[]{:S(2)}) collective-permute-start(bf16[144,640]{1,0:T(8,128)(2,1)S(1)} %act.1.refs_0_), channel_id=1, source_target_pairs={{0,24},{4,28},{8,16},{12,20},{16,8},{20,12},{24,0},{28,4},{1,25},{... | collective-permute-start | bytes 552968 | tf_op jit(solution)/shard_map/ppermute | solution.py:541
  12.3 0.5 collective-permute-start.3
  12.8 0.5 %collective-permute-start.1 = (bf16[144,640]{1,0:T(8,128)(2,1)S(1)}, bf16[144,640]{1,0:T(8,128)(2,1)S(1)}, u32[]{:S(2)}, u32[]{:S(2)}) collective-permute-start(bf16[144,640]{1,0:T(8,128)(2,1)S(1)} %act.1.refs_0_), channel_id=1, source_target_pairs={{0,8},{4,12},{8,0},{12,4},{16,24},{20,28},{24,16},{28,20},{1,9},{5... | collective-permute-start | bytes 552968 | tf_op jit(solution)/shard_map/ppermute | solution.py:541
  13.3 1.0 %collective-permute-start.9 = (bf16[96,640]{1,0:T(8,128)(2,1)S(1)}, bf16[96,640]{1,0:T(8,128)(2,1)S(1)}, u32[]{:S(2)}, u32[]{:S(2)}) collective-permute-start(bf16[96,640]{1,0:T(8,128)(2,1)S(1)} %relay.1.refs_10_), channel_id=1, source_target_pairs={{0,1},{1,0},{2,3},{3,2},{4,5},{5,4},{6,7},{7,6},{8,9},{9,8},{10,11... | collective-permute-start | bytes 368648 | tf_op jit(solution)/shard_map/ppermute | solution.py:544
  14.4 3.7 %collective-permute-done.5.refs_6_ = bf16[144,640]{1,0:T(8,128)(2,1)S(1)} collective-permute-done((bf16[144,640]{1,0:T(8,128)(2,1)S(1)}, bf16[144,640]{1,0:T(8,128)(2,1)S(1)}, u32[]{:S(2)}, u32[]{:S(2)}) %collective-permute-start.5) | collective-permute-done | bytes 184352 | tf_op jit(solution)/shard_map/ppermute | solution.py:541
  18.1 2.4 %collective-permute-done.3.refs_4_ = bf16[144,640]{1,0:T(8,128)(2,1)S(1)} collective-permute-done((bf16[144,640]{1,0:T(8,128)(2,1)S(1)}, bf16[144,640]{1,0:T(8,128)(2,1)S(1)}, u32[]{:S(2)}, u32[]{:S(2)}) %collective-permute-start.3) | collective-permute-done | bytes 184352 | tf_op jit(solution)/shard_map/ppermute | solution.py:541
  20.6 0.4 collective-permute-start.2
  21.0 0.4 time_own.1.refs_12_
  21.5 0.5 collective-permute-done.4.refs_5_
  22.2 4.9 %main.1 = (bf16[8,160,128]{2,1,0:T(8,128)(2,1)S(1)}, bf16[384,320]{1,0:T(8,128)(2,1)S(1)}, f32[96,640]{1,0:T(8,128)S(1)}, bf16[96,640]{1,0:T(8,128)(2,1)S(1)}, b...) custom-call(s32[4]{0:T(128)S(1)} %copy-done.3, bf16[144,640]{1,0:T(8,128)(2,1)S(1)} %act.1.refs_0_, ...), custom_call_target="tpu_custom_call" | custom-call | flops 6000000000 | bytes 18000000 | tf_op jit(solution)/shard_map/main/pallas_call | solution.py:516
  27.1 0.8 %share.1 = (f32[4,128,320]{2,1,0:T(8,128)S(1)}, bf16[4,128,320]{2,1,0:T(8,128)(2,1)S(1)}) custom-call(bf16[8,160,128]{2,1,0:T(8,128)(2,1)S(1)} %get-tuple-element.27.act2p, bf16[384,320]{1,0:T(8,128)(2,1)S(1)} %get-tuple-element.28.w2_ref, f32[96,640]{1,0:T(8,128)S(1)} %get-tuple-element.23.after_ref.refs_0_), custom_call_target="tpu_custom_call" | custom-call | flops 1000000 | bytes 3000 | tf_op jit(solution)/shard_map/share/pallas_call | solution.py:516
  28.2 0.5 collective-permute-start.10
  28.6 0.3 collective-permute-start.11
  29.0 3.6 %collective-permute-start.12 = (bf16[96,640]{1,0:T(8,128)(2,1)S(1)}, bf16[96,640]{1,0:T(8,128)(2,1)S(1)}, u32[]{:S(2)}, u32[]{:S(2)}) collective-permute-start(bf16[96,640]{1,0:T(8,128)(2,1)S(1)} %get-tuple-element.26), channel_id=1, source_target_pairs={{0,3},{1,2},{2,1},{3,0},{4,7},{5,6},{6,5},{7,4},{8,11},{9,10},{10,... | collective-permute-start | bytes 368648 | tf_op jit(solution)/shard_map/ppermute | solution.py:544
  32.6 1.6 %collective-permute-start.14 = (bf16[128,320]{1,0:T(8,128)(2,1)S(1)}, bf16[128,320]{1,0:T(8,128)(2,1)S(1)}, u32[]{:S(2)}, u32[]{:S(2)}) collective-permute-start(bf16[128,320]{1,0:T(8,128)(2,1)S(1)} %get-tuple-element.31), channel_id=1, source_target_pairs={{0,8},{4,12},{8,0},{12,4},{16,24},{20,28},{24,16},{28,20},{1,9},{5... | collective-permute-start | bytes 245768 | tf_op jit(solution)/shard_map/ppermute | solution.py:541
  34.2 0.8 %collective-permute-start.15 = (bf16[128,320]{1,0:T(8,128)(2,1)S(1)}, bf16[128,320]{1,0:T(8,128)(2,1)S(1)}, u32[]{:S(2)}, u32[]{:S(2)}) collective-permute-start(bf16[128,320]{1,0:T(8,128)(2,1)S(1)} %get-tuple-element.32), channel_id=1, source_target_pairs={{0,16},{4,20},{8,24},{12,28},{16,0},{20,4},{24,8},{28,12},{1,17},{... | collective-permute-start | bytes 245768 | tf_op jit(solution)/shard_map/ppermute | solution.py:541
  35.0 1.7 %collective-permute-start.16 = (bf16[128,320]{1,0:T(8,128)(2,1)S(1)}, bf16[128,320]{1,0:T(8,128)(2,1)S(1)}, u32[]{:S(2)}, u32[]{:S(2)}) collective-permute-start(bf16[128,320]{1,0:T(8,128)(2,1)S(1)} %get-tuple-element.33), channel_id=1, source_target_pairs={{0,24},{4,28},{8,16},{12,20},{16,8},{20,12},{24,0},{28,4},{1,25},{... | collective-permute-start | bytes 245768 | tf_op jit(solution)/shard_map/ppermute | solution.py:541
  36.8 0.9 %tables.1 = (bf16[2,320,192]{2,1,0:T(8,128)(2,1)S(1)}, bf16[2,320,160]{2,1,0:T(8,128)(2,1)S(1)}, bf16[2,384,720]{2,1,0:T(8,128)(2,1)S(1)}) custom-call(f32[128,320]{1,0:T(8,128)S(1)} %get-tuple-element.34.after_ref.refs_7_), custom_call_target="tpu_custom_call" | custom-call | flops 1000000 | bytes 3000 | tf_op jit(solution)/shard_map/tables/pallas_call | solution.py:516
  37.6 3.3 %collective-permute-done.11.refs_2_ = bf16[96,640]{1,0:T(8,128)(2,1)S(1)} collective-permute-done((bf16[96,640]{1,0:T(8,128)(2,1)S(1)}, bf16[96,640]{1,0:T(8,128)(2,1)S(1)}, u32[]{:S(2)}, u32[]{:S(2)}) %collective-permute-start.11) | collective-permute-done | bytes 122912 | tf_op jit(solution)/shard_map/ppermute | solution.py:544
  41.1 1.8 %collective-permute-start.19 = (bf16[96,640]{1,0:T(8,128)(2,1)S(1)}, bf16[96,640]{1,0:T(8,128)(2,1)S(1)}, u32[]{:S(2)}, u32[]{:S(2)}) collective-permute-start(bf16[96,640]{1,0:T(8,128)(2,1)S(1)} %total.1.refs_0_), channel_id=1, source_target_pairs={{0,24},{4,28},{8,16},{12,20},{16,8},{20,12},{24,0},{28,4},{1,25},{... | collective-permute-start | bytes 368648 | tf_op jit(solution)/shard_map/ppermute | solution.py:541
  42.9 1.2 %collective-permute-start.18 = (bf16[96,640]{1,0:T(8,128)(2,1)S(1)}, bf16[96,640]{1,0:T(8,128)(2,1)S(1)}, u32[]{:S(2)}, u32[]{:S(2)}) collective-permute-start(bf16[96,640]{1,0:T(8,128)(2,1)S(1)} %total.1.refs_0_), channel_id=1, source_target_pairs={{0,16},{4,20},{8,24},{12,28},{16,0},{20,4},{24,8},{28,12},{1,17},{... | collective-permute-start | bytes 368648 | tf_op jit(solution)/shard_map/ppermute | solution.py:541
  44.1 0.5 %collective-permute-start.17 = (bf16[96,640]{1,0:T(8,128)(2,1)S(1)}, bf16[96,640]{1,0:T(8,128)(2,1)S(1)}, u32[]{:S(2)}, u32[]{:S(2)}) collective-permute-start(bf16[96,640]{1,0:T(8,128)(2,1)S(1)} %total.1.refs_0_), channel_id=1, source_target_pairs={{0,8},{4,12},{8,0},{12,4},{16,24},{20,28},{24,16},{28,20},{1,9},{5... | collective-permute-start | bytes 368648 | tf_op jit(solution)/shard_map/ppermute | solution.py:541
  44.6 2.7 %collective-permute-done.19.refs_3_ = bf16[96,640]{1,0:T(8,128)(2,1)S(1)} collective-permute-done((bf16[96,640]{1,0:T(8,128)(2,1)S(1)}, bf16[96,640]{1,0:T(8,128)(2,1)S(1)}, u32[]{:S(2)}, u32[]{:S(2)}) %collective-permute-start.19) | collective-permute-done | bytes 122912 | tf_op jit(solution)/shard_map/ppermute | solution.py:541
  47.3 1.2 %collective-permute-done.18.refs_2_ = bf16[96,640]{1,0:T(8,128)(2,1)S(1)} collective-permute-done((bf16[96,640]{1,0:T(8,128)(2,1)S(1)}, bf16[96,640]{1,0:T(8,128)(2,1)S(1)}, u32[]{:S(2)}, u32[]{:S(2)}) %collective-permute-start.18) | collective-permute-done | bytes 122912 | tf_op jit(solution)/shard_map/ppermute | solution.py:541
  48.5 0.4 collective-permute-done.17.refs_1_
  49.1 0.6 %part.1 = (f32[320,720]{1,0:T(8,128)S(1)}, f32[320,720]{1,0:T(8,128)S(1)}) custom-call(bf16[4,96,640]{2,1,0:T(8,128)(2,1)S(1)} %stack.1.stack_ref, bf16[2,320,192]{2,1,0:T(8,128)(2,1)S(1)} %get-tuple-element.35.refs_7_.main_ref.refs_1_, bf16[2,320,160]{2,1,0:T(8,128)(2,1)S(1)} %get-tuple-element.36.fold_ref.refs_2_, ...), custom_call_target="tpu_custom_call" | custom-call | flops 1000000 | bytes 3000 | tf_op jit(solution)/shard_map/part/pallas_call | solution.py:516
  49.7 1.2 %collective-permute-done.20.refs_0_ = bf16[4,96,640]{2,1,0:T(8,128)(2,1)S(1)} collective-permute-done((bf16[4,96,640]{2,1,0:T(8,128)(2,1)S(1)}, bf16[4,96,640]{2,1,0:T(8,128)(2,1)S(1)}, u32[]{:S(2)}, u32[]{:S(2)}) %collective-permute-start.20) | collective-permute-done | bytes 491552 | tf_op jit(solution)/shard_map/ppermute | solution.py:541
  50.9 2.0 %last.1 = (f32[320,720]{1,0:T(8,128)}, f32[320,720]{1,0:T(8,128)}, bf16[128,320]{1,0:T(8,128)(2,1)}) custom-call(bf16[4,96,640]{2,1,0:T(8,128)(2,1)S(1)} %collective-permute-done.20.refs_0_, bf16[2,320,192]{2,1,0:T(8,128)(2,1)S(1)} %get-tuple-element.35.refs_7_.main_ref.refs_1_, bf16[2,320,160]{2,1,0:T(8,128)(2,1)S(1)} %get-tuple-element.36.fold_ref.refs_2_, ...), custom_call_target="tpu_custom_call" | custom-call | flops 100000000 | bytes 300000 | tf_op jit(solution)/shard_map/last/pallas_call | solution.py:516
  (30 shorter events, 1.0 us)
Async XLA Ops:
  0.6 8.2 %copy-start = (bf16[1,8,16,320]{3,2,1,0:T(8,128)(2,1)S(1)}, bf16[1,8,16,320]{3,2,1,0:T(8,128)(2,1)}, u32[]{:S(2)}) copy-start(bf16[1,8,16,320]{3,2,1,0:T(8,128)(2,1)} %param.7) | copy-start | bytes 245764
  0.6 8.2 %copy-start.2 = (bf16[1,8,16,320]{3,2,1,0:T(8,128)(2,1)S(1)}, bf16[1,8,16,320]{3,2,1,0:T(8,128)(2,1)}, u32[]{:S(2)}) copy-start(bf16[1,8,16,320]{3,2,1,0:T(8,128)(2,1)} %param.8) | copy-start | bytes 245764
  2.5 10.8 %collective-permute-start.8 = (bf16[96,640]{1,0:T(8,128)(2,1)S(1)}, bf16[96,640]{1,0:T(8,128)(2,1)S(1)}, u32[]{:S(2)}, u32[]{:S(2)}) collective-permute-start(bf16[96,640]{1,0:T(8,128)(2,1)S(1)} %slices.1.after_ref.refs_8_), channel_id=1, source_target_pairs={{0,2},{1,3},{2,0},{3,1},{4,6},{5,7},{6,4},{7,5},{8,10},{9,11},{10,... | collective-permute-start | bytes 368648 | tf_op jit(solution)/shard_map/ppermute | solution.py:544
  6.6 6.7 %collective-permute-start.7 = (bf16[96,640]{1,0:T(8,128)(2,1)S(1)}, bf16[96,640]{1,0:T(8,128)(2,1)S(1)}, u32[]{:S(2)}, u32[]{:S(2)}) collective-permute-start(bf16[96,640]{1,0:T(8,128)(2,1)S(1)} %slices.1.after_ref.refs_8_), channel_id=1, source_target_pairs={{0,1},{1,0},{2,3},{3,2},{4,5},{5,4},{6,7},{7,6},{8,9},{9,8},{10,11... | collective-permute-start | bytes 368648 | tf_op jit(solution)/shard_map/ppermute | solution.py:544
  9.7 11.3 %copy-start.1 = (bf16[1280,320]{0,1:T(8,128)(2,1)S(1)}, bf16[1280,320]{0,1:T(8,128)(2,1)}, u32[]{:S(2)}) copy-start(bf16[1280,320]{0,1:T(8,128)(2,1)} %param.11) | copy-start | bytes 2457604
  9.8 8.3 %collective-permute-start.5 = (bf16[144,640]{1,0:T(8,128)(2,1)S(1)}, bf16[144,640]{1,0:T(8,128)(2,1)S(1)}, u32[]{:S(2)}, u32[]{:S(2)}) collective-permute-start(bf16[144,640]{1,0:T(8,128)(2,1)S(1)} %act.1.refs_0_), channel_id=1, source_target_pairs={{0,24},{4,28},{8,16},{12,20},{16,8},{20,12},{24,0},{28,4},{1,25},{... | collective-permute-start | bytes 552968 | tf_op jit(solution)/shard_map/ppermute | solution.py:541
  12.3 8.2 %collective-permute-start.3 = (bf16[144,640]{1,0:T(8,128)(2,1)S(1)}, bf16[144,640]{1,0:T(8,128)(2,1)S(1)}, u32[]{:S(2)}, u32[]{:S(2)}) collective-permute-start(bf16[144,640]{1,0:T(8,128)(2,1)S(1)} %act.1.refs_0_), channel_id=1, source_target_pairs={{0,16},{4,20},{8,24},{12,28},{16,0},{20,4},{24,8},{28,12},{1,17},{... | collective-permute-start | bytes 552968 | tf_op jit(solution)/shard_map/ppermute | solution.py:541
  12.8 7.8 %collective-permute-start.1 = (bf16[144,640]{1,0:T(8,128)(2,1)S(1)}, bf16[144,640]{1,0:T(8,128)(2,1)S(1)}, u32[]{:S(2)}, u32[]{:S(2)}) collective-permute-start(bf16[144,640]{1,0:T(8,128)(2,1)S(1)} %act.1.refs_0_), channel_id=1, source_target_pairs={{0,8},{4,12},{8,0},{12,4},{16,24},{20,28},{24,16},{28,20},{1,9},{5... | collective-permute-start | bytes 552968 | tf_op jit(solution)/shard_map/ppermute | solution.py:541
  13.3 8.1 %collective-permute-start = (bf16[144,640]{1,0:T(8,128)(2,1)S(1)}, bf16[144,640]{1,0:T(8,128)(2,1)S(1)}, u32[]{:S(2)}, u32[]{:S(2)}) collective-permute-start(bf16[144,640]{1,0:T(8,128)(2,1)S(1)} %act.1.refs_0_), channel_id=1, source_target_pairs={{0,4},{4,0},{8,12},{12,8},{16,20},{20,16},{24,28},{28,24},{1,5},{5... | collective-permute-start | bytes 552968 | tf_op jit(solution)/shard_map/ppermute | solution.py:541
  13.3 8.1 %collective-permute-start.9 = (bf16[96,640]{1,0:T(8,128)(2,1)S(1)}, bf16[96,640]{1,0:T(8,128)(2,1)S(1)}, u32[]{:S(2)}, u32[]{:S(2)}) collective-permute-start(bf16[96,640]{1,0:T(8,128)(2,1)S(1)} %relay.1.refs_10_), channel_id=1, source_target_pairs={{0,1},{1,0},{2,3},{3,2},{4,5},{5,4},{6,7},{7,6},{8,9},{9,8},{10,11... | collective-permute-start | bytes 368648 | tf_op jit(solution)/shard_map/ppermute | solution.py:544
  18.1 3.4 %collective-permute-start.6 = (bf16[144,640]{1,0:T(8,128)(2,1)S(1)}, bf16[144,640]{1,0:T(8,128)(2,1)S(1)}, u32[]{:S(2)}, u32[]{:S(2)}) collective-permute-start(bf16[144,640]{1,0:T(8,128)(2,1)S(1)} %collective-permute-done.5.refs_6_), channel_id=1, source_target_pairs={{0,4},{4,0},{8,12},{12,8},{16,20},{20,16},{24,28},{28,24},{1,5},{5... | collective-permute-start | bytes 552968 | tf_op jit(solution)/shard_map/ppermute | solution.py:541
  20.5 1.4 %collective-permute-start.4 = (bf16[144,640]{1,0:T(8,128)(2,1)S(1)}, bf16[144,640]{1,0:T(8,128)(2,1)S(1)}, u32[]{:S(2)}, u32[]{:S(2)}) collective-permute-start(bf16[144,640]{1,0:T(8,128)(2,1)S(1)} %collective-permute-done.3.refs_4_), channel_id=1, source_target_pairs={{0,4},{4,0},{8,12},{12,8},{16,20},{20,16},{24,28},{28,24},{1,5},{5... | collective-permute-start | bytes 552968 | tf_op jit(solution)/shard_map/ppermute | solution.py:541
  20.6 1.6 %collective-permute-start.2 = (bf16[144,640]{1,0:T(8,128)(2,1)S(1)}, bf16[144,640]{1,0:T(8,128)(2,1)S(1)}, u32[]{:S(2)}, u32[]{:S(2)}) collective-permute-start(bf16[144,640]{1,0:T(8,128)(2,1)S(1)} %collective-permute-done.1.refs_2_), channel_id=1, source_target_pairs={{0,4},{4,0},{8,12},{12,8},{16,20},{20,16},{24,28},{28,24},{1,5},{5... | collective-permute-start | bytes 552968 | tf_op jit(solution)/shard_map/ppermute | solution.py:541
  21.0 1.2 %copy-start.3 = (s32[4]{0:T(128)S(1)}, s32[4]{0:T(128)}, u32[]{:S(2)}) copy-start(s32[4]{0:T(128)} %owner_ref.1) | copy-start | bytes 52
  27.8 4.7 %collective-permute-start.13 = (bf16[4,128,320]{2,1,0:T(8,128)(2,1)S(1)}, bf16[4,128,320]{2,1,0:T(8,128)(2,1)S(1)}, u32[]{:S(2)}, u32[]{:S(2)}) collective-permute-start(bf16[4,128,320]{2,1,0:T(8,128)(2,1)S(1)} %get-tuple-element.30), channel_id=1, source_target_pairs={{0,4},{4,0},{8,12},{12,8},{16,20},{20,16},{24,28},{28,24},{1,5},{5... | collective-permute-start | bytes 983048 | tf_op jit(solution)/shard_map/ppermute | solution.py:541
  28.2 6.9 %collective-permute-start.10 = (bf16[96,640]{1,0:T(8,128)(2,1)S(1)}, bf16[96,640]{1,0:T(8,128)(2,1)S(1)}, u32[]{:S(2)}, u32[]{:S(2)}) collective-permute-start(bf16[96,640]{1,0:T(8,128)(2,1)S(1)} %get-tuple-element.24), channel_id=1, source_target_pairs={{0,1},{1,0},{2,3},{3,2},{4,5},{5,4},{6,7},{7,6},{8,9},{9,8},{10,11... | collective-permute-start | bytes 368648 | tf_op jit(solution)/shard_map/ppermute | solution.py:544
  28.6 12.4 %collective-permute-start.11 = (bf16[96,640]{1,0:T(8,128)(2,1)S(1)}, bf16[96,640]{1,0:T(8,128)(2,1)S(1)}, u32[]{:S(2)}, u32[]{:S(2)}) collective-permute-start(bf16[96,640]{1,0:T(8,128)(2,1)S(1)} %get-tuple-element.25), channel_id=1, source_target_pairs={{0,2},{1,3},{2,0},{3,1},{4,6},{5,7},{6,4},{7,5},{8,10},{9,11},{10,... | collective-permute-start | bytes 368648 | tf_op jit(solution)/shard_map/ppermute | solution.py:544
  29.0 12.0 %collective-permute-start.12 = (bf16[96,640]{1,0:T(8,128)(2,1)S(1)}, bf16[96,640]{1,0:T(8,128)(2,1)S(1)}, u32[]{:S(2)}, u32[]{:S(2)}) collective-permute-start(bf16[96,640]{1,0:T(8,128)(2,1)S(1)} %get-tuple-element.26), channel_id=1, source_target_pairs={{0,3},{1,2},{2,1},{3,0},{4,7},{5,6},{6,5},{7,4},{8,11},{9,10},{10,... | collective-permute-start | bytes 368648 | tf_op jit(solution)/shard_map/ppermute | solution.py:544
  32.6 8.4 %collective-permute-start.14 = (bf16[128,320]{1,0:T(8,128)(2,1)S(1)}, bf16[128,320]{1,0:T(8,128)(2,1)S(1)}, u32[]{:S(2)}, u32[]{:S(2)}) collective-permute-start(bf16[128,320]{1,0:T(8,128)(2,1)S(1)} %get-tuple-element.31), channel_id=1, source_target_pairs={{0,8},{4,12},{8,0},{12,4},{16,24},{20,28},{24,16},{28,20},{1,9},{5... | collective-permute-start | bytes 245768 | tf_op jit(solution)/shard_map/ppermute | solution.py:541
  34.2 6.8 %collective-permute-start.15 = (bf16[128,320]{1,0:T(8,128)(2,1)S(1)}, bf16[128,320]{1,0:T(8,128)(2,1)S(1)}, u32[]{:S(2)}, u32[]{:S(2)}) collective-permute-start(bf16[128,320]{1,0:T(8,128)(2,1)S(1)} %get-tuple-element.32), channel_id=1, source_target_pairs={{0,16},{4,20},{8,24},{12,28},{16,0},{20,4},{24,8},{28,12},{1,17},{... | collective-permute-start | bytes 245768 | tf_op jit(solution)/shard_map/ppermute | solution.py:541
  35.0 6.0 %collective-permute-start.16 = (bf16[128,320]{1,0:T(8,128)(2,1)S(1)}, bf16[128,320]{1,0:T(8,128)(2,1)S(1)}, u32[]{:S(2)}, u32[]{:S(2)}) collective-permute-start(bf16[128,320]{1,0:T(8,128)(2,1)S(1)} %get-tuple-element.33), channel_id=1, source_target_pairs={{0,24},{4,28},{8,16},{12,20},{16,8},{20,12},{24,0},{28,4},{1,25},{... | collective-permute-start | bytes 245768 | tf_op jit(solution)/shard_map/ppermute | solution.py:541
  41.1 6.2 %collective-permute-start.19 = (bf16[96,640]{1,0:T(8,128)(2,1)S(1)}, bf16[96,640]{1,0:T(8,128)(2,1)S(1)}, u32[]{:S(2)}, u32[]{:S(2)}) collective-permute-start(bf16[96,640]{1,0:T(8,128)(2,1)S(1)} %total.1.refs_0_), channel_id=1, source_target_pairs={{0,24},{4,28},{8,16},{12,20},{16,8},{20,12},{24,0},{28,4},{1,25},{... | collective-permute-start | bytes 368648 | tf_op jit(solution)/shard_map/ppermute | solution.py:541
  42.9 5.6 %collective-permute-start.18 = (bf16[96,640]{1,0:T(8,128)(2,1)S(1)}, bf16[96,640]{1,0:T(8,128)(2,1)S(1)}, u32[]{:S(2)}, u32[]{:S(2)}) collective-permute-start(bf16[96,640]{1,0:T(8,128)(2,1)S(1)} %total.1.refs_0_), channel_id=1, source_target_pairs={{0,16},{4,20},{8,24},{12,28},{16,0},{20,4},{24,8},{28,12},{1,17},{... | collective-permute-start | bytes 368648 | tf_op jit(solution)/shard_map/ppermute | solution.py:541
  44.1 4.9 %collective-permute-start.17 = (bf16[96,640]{1,0:T(8,128)(2,1)S(1)}, bf16[96,640]{1,0:T(8,128)(2,1)S(1)}, u32[]{:S(2)}, u32[]{:S(2)}) collective-permute-start(bf16[96,640]{1,0:T(8,128)(2,1)S(1)} %total.1.refs_0_), channel_id=1, source_target_pairs={{0,8},{4,12},{8,0},{12,4},{16,24},{20,28},{24,16},{28,20},{1,9},{5... | collective-permute-start | bytes 368648 | tf_op jit(solution)/shard_map/ppermute | solution.py:541
  49.0 1.9 %collective-permute-start.20 = (bf16[4,96,640]{2,1,0:T(8,128)(2,1)S(1)}, bf16[4,96,640]{2,1,0:T(8,128)(2,1)S(1)}, u32[]{:S(2)}, u32[]{:S(2)}) collective-permute-start(bf16[4,96,640]{2,1,0:T(8,128)(2,1)S(1)} %stack.1.stack_ref), channel_id=1, source_target_pairs={{0,4},{4,0},{8,12},{12,8},{16,20},{20,16},{24,28},{28,24},{1,5},{5... | collective-permute-start | bytes 1474568 | tf_op jit(solution)/shard_map/ppermute | solution.py:541

commit v5 on v4

--- a/solution.py
+++ b/solution.py
@@ -189,23 +189,15 @@
     pay_ref[plan.first_rows : plan.first_rows + plan.second_rows, :] = pack_second(plan, nn(w2_ref[...], pick2).T[0 : plan.piece_pad]).astype(BF16)
 
 
-def act_kernel(plan, x_any, cot_any, steps_ref, after_ref, act_ref, x_ref, cot_ref, sems):
+def act_kernel(plan, x_ref, cot_ref, steps_ref, after_ref, act_ref):
     del after_ref
-    copies = [
-        pltpu.make_async_copy(src, dst, sems.at[i])
-        for i, (src, dst) in enumerate(((x_any, x_ref), (cot_any, cot_ref)))
-    ]
-    for copy in copies:
-        copy.start()
     c, pix, head = plan.channels, plan.pixels, plan.head
     same = group_matrix(plan, c, c)
     count = pix * plan.per_group
-    copies[0].wait()
     x = x_ref[...].astype(F32)
     off = x - group_sum(jnp.sum(x, 0, keepdims=True), same) / count
     spread = group_sum(jnp.sum(off * off, 0, keepdims=True), same) / count
     act = silu(off * lax.rsqrt(spread + NORM_EPS)).astype(BF16)
-    copies[1].wait()
     act_ref[0:pix, 0:head] = act[:, 0:head]
     act_ref[0:pix, head : 2 * head] = cot_ref[:, 0:head]
     act_ref[0:pix, 2 * head :] = jnp.concatenate(
@@ -417,10 +409,8 @@
 
 def share_kernel(plan, act2p, w2_ref, after_ref, keep_ref, away_ref):
     del after_ref
-    team, c, pix, wide = plan.team, plan.channels, plan.pixels, plan.wide
-    out = jnp.zeros((team * pix, c), F32)
-    for ky in range(3):
-        out = out + nn(window(plan, act2p, ky), w2_ref[ky * wide : (ky + 1) * wide, :])
+    team, c, pix = plan.team, plan.channels, plan.pixels
+    out = nn(jnp.concatenate([window(plan, act2p, ky) for ky in range(3)], axis=1), w2_ref[...])
     out = out.reshape(team, pix, c)
     for slot in range(team):
         if slot % 2:
@@ -456,7 +446,9 @@
 def first_in_place(plan, stack_ref, main_table, fold_table):
     n = stack_ref.shape[0]
     base, chunk, used, lanes = fold_layout(plan)
-    folded = stack_ref[:, base : base + chunk, :].astype(F32).reshape(n * chunk, plan.packed)
+    low = base // 16 * 16
+    folded = stack_ref[:, low : round_up(base + chunk, 16), :].astype(F32)
+    folded = folded[:, base - low : base - low + chunk].reshape(n * chunk, plan.packed)
     folded = [folded[:, k * lanes : (k + 1) * lanes] for k in range(used)]
     first = nn(fold_table, jnp.concatenate(folded, axis=0).astype(BF16))
     if not base:
@@ -574,12 +566,6 @@
         shape((plan.act_rows, 2 * c), BF16),
         (x, cot, timesteps.reshape(1, 1), pay),
         2,
-        n_hbm=2,
-        scratch=(
-            pltpu.VMEM((pix, c), BF16),
-            pltpu.VMEM((pix, c), BF16),
-            pltpu.SemaphoreType.DMA((2,)),
-        ),
         limit=56_000_000,
     )
     pays = team_gather(act)

time: 53.1 us -> 52.6 us (level)
  Pallas kernels: 12.5 us -> 11.9 us
    pallas_call x12, Pallas kernels: 12.5 us -> 11.9 us  [call(): pl.pallas_call(kernel, name=name, out_shape=out_shape, in_specs=[SMEM] *...]
where the time goes in v5:
time: 52.6 us; the launch traced here: 52.4 us
  starting transfers between devices  23.5 us (45%)
  waiting for transfers between devices  15.5 us (29%)
  Pallas kernels  11.9 us (23%)
  between operations  1.45 us (3%)
    ppermute x15, waiting for transfers between devices, to_rep(): return lax.ppermute(value, 'rep', [(i, i ^ step) for i in range(n_rep)])  12.1 us
    ppermute x15, starting transfers between devices, to_rep(): return lax.ppermute(value, 'rep', [(i, i ^ step) for i in range(n_rep)])  12 us
    pallas_call x12, Pallas kernels, call(): pl.pallas_call(kernel, name=name, out_shape=out_shape, in_specs=[SMEM] *...  11.9 us
    ppermute x6, starting transfers between devices, to_dom(): return lax.ppermute(value, 'dom', [(i, i ^ step) for i in range(d)])  11.5 us
    ppermute x6, waiting for transfers between devices, to_dom(): return lax.ppermute(value, 'dom', [(i, i ^ step) for i in range(d)])  3.39 us
  transfers between devices with their start and end apart: 21, of which 10 were waited for; matrix products, arithmetic and copies ran while one was open for 0% of the time, Pallas kernels for 5%

profile of v5, /device:TPU:0, one launch (start us, length us, event | category | flops | bytes accessed | tf_op | source)
XLA Modules:
  0.0 52.4 jit_solution(6548956733708519244)
XLA Ops:
  0.7 1.8 %slices.1.after_ref.refs_8_ = bf16[96,640]{1,0:T(8,128)(2,1)S(1)} custom-call(bf16[320,720]{1,0:T(8,128)(2,1)} %bitcast.16, bf16[320,720]{1,0:T(8,128)(2,1)} %bitcast.17), custom_call_target="tpu_custom_call" | custom-call | flops 2000000000 | bytes 6000000 | tf_op jit(solution)/shard_map/slices/pallas_call | solution.py:508
  2.5 4.1 %collective-permute-start.8 = (bf16[96,640]{1,0:T(8,128)(2,1)S(1)}, bf16[96,640]{1,0:T(8,128)(2,1)S(1)}, u32[]{:S(2)}, u32[]{:S(2)}) collective-permute-start(bf16[96,640]{1,0:T(8,128)(2,1)S(1)} %slices.1.after_ref.refs_8_), channel_id=1, source_target_pairs={{0,2},{1,3},{2,0},{3,1},{4,6},{5,7},{6,4},{7,5},{8,10},{9,11},{10,... | collective-permute-start | bytes 368648 | tf_op jit(solution)/shard_map/ppermute | solution.py:536
  6.6 1.6 %collective-permute-start.7 = (bf16[96,640]{1,0:T(8,128)(2,1)S(1)}, bf16[96,640]{1,0:T(8,128)(2,1)S(1)}, u32[]{:S(2)}, u32[]{:S(2)}) collective-permute-start(bf16[96,640]{1,0:T(8,128)(2,1)S(1)} %slices.1.after_ref.refs_8_), channel_id=1, source_target_pairs={{0,1},{1,0},{2,3},{3,2},{4,5},{5,4},{6,7},{7,6},{8,9},{9,8},{10,11... | collective-permute-start | bytes 368648 | tf_op jit(solution)/shard_map/ppermute | solution.py:536
  8.8 0.5 act.1.refs_0_
  9.4 2.5 %collective-permute-start.5 = (bf16[144,640]{1,0:T(8,128)(2,1)S(1)}, bf16[144,640]{1,0:T(8,128)(2,1)S(1)}, u32[]{:S(2)}, u32[]{:S(2)}) collective-permute-start(bf16[144,640]{1,0:T(8,128)(2,1)S(1)} %act.1.refs_0_), channel_id=1, source_target_pairs={{0,24},{4,28},{8,16},{12,20},{16,8},{20,12},{24,0},{28,4},{1,25},{... | collective-permute-start | bytes 552968 | tf_op jit(solution)/shard_map/ppermute | solution.py:533
  11.9 0.5 collective-permute-start.3
  12.4 0.5 %collective-permute-start.1 = (bf16[144,640]{1,0:T(8,128)(2,1)S(1)}, bf16[144,640]{1,0:T(8,128)(2,1)S(1)}, u32[]{:S(2)}, u32[]{:S(2)}) collective-permute-start(bf16[144,640]{1,0:T(8,128)(2,1)S(1)} %act.1.refs_0_), channel_id=1, source_target_pairs={{0,8},{4,12},{8,0},{12,4},{16,24},{20,28},{24,16},{28,20},{1,9},{5... | collective-permute-start | bytes 552968 | tf_op jit(solution)/shard_map/ppermute | solution.py:533
  12.9 1.4 %collective-permute-start.9 = (bf16[96,640]{1,0:T(8,128)(2,1)S(1)}, bf16[96,640]{1,0:T(8,128)(2,1)S(1)}, u32[]{:S(2)}, u32[]{:S(2)}) collective-permute-start(bf16[96,640]{1,0:T(8,128)(2,1)S(1)} %relay.1.refs_10_), channel_id=1, source_target_pairs={{0,1},{1,0},{2,3},{3,2},{4,5},{5,4},{6,7},{7,6},{8,9},{9,8},{10,11... | collective-permute-start | bytes 368648 | tf_op jit(solution)/shard_map/ppermute | solution.py:536
  14.4 3.3 %collective-permute-done.5.refs_6_ = bf16[144,640]{1,0:T(8,128)(2,1)S(1)} collective-permute-done((bf16[144,640]{1,0:T(8,128)(2,1)S(1)}, bf16[144,640]{1,0:T(8,128)(2,1)S(1)}, u32[]{:S(2)}, u32[]{:S(2)}) %collective-permute-start.5) | collective-permute-done | bytes 184352 | tf_op jit(solution)/shard_map/ppermute | solution.py:533
  17.7 2.4 %collective-permute-done.3.refs_4_ = bf16[144,640]{1,0:T(8,128)(2,1)S(1)} collective-permute-done((bf16[144,640]{1,0:T(8,128)(2,1)S(1)}, bf16[144,640]{1,0:T(8,128)(2,1)S(1)}, u32[]{:S(2)}, u32[]{:S(2)}) %collective-permute-start.3) | collective-permute-done | bytes 184352 | tf_op jit(solution)/shard_map/ppermute | solution.py:533
  20.2 0.4 collective-permute-start.2
  20.6 0.4 time_own.1.refs_12_
  21.0 0.5 collective-permute-done.4.refs_5_
  21.8 4.9 %main.1 = (bf16[8,160,128]{2,1,0:T(8,128)(2,1)S(1)}, bf16[384,320]{1,0:T(8,128)(2,1)S(1)}, f32[96,640]{1,0:T(8,128)S(1)}, bf16[96,640]{1,0:T(8,128)(2,1)S(1)}, b...) custom-call(s32[4]{0:T(128)S(1)} %copy-done.3, bf16[144,640]{1,0:T(8,128)(2,1)S(1)} %act.1.refs_0_, ...), custom_call_target="tpu_custom_call" | custom-call | flops 6000000000 | bytes 18000000 | tf_op jit(solution)/shard_map/main/pallas_call | solution.py:508
  26.7 0.6 %share.1 = (f32[4,128,320]{2,1,0:T(8,128)S(1)}, bf16[4,128,320]{2,1,0:T(8,128)(2,1)S(1)}) custom-call(bf16[8,160,128]{2,1,0:T(8,128)(2,1)S(1)} %get-tuple-element.27.act2p, bf16[384,320]{1,0:T(8,128)(2,1)S(1)} %get-tuple-element.28.w2_ref, f32[96,640]{1,0:T(8,128)S(1)} %get-tuple-element.23.after_ref.refs_0_), custom_call_target="tpu_custom_call" | custom-call | flops 1000000 | bytes 3000 | tf_op jit(solution)/shard_map/share/pallas_call | solution.py:508
  27.6 0.5 collective-permute-start.10
  28.1 0.3 collective-permute-start.11
  28.4 3.6 %collective-permute-start.12 = (bf16[96,640]{1,0:T(8,128)(2,1)S(1)}, bf16[96,640]{1,0:T(8,128)(2,1)S(1)}, u32[]{:S(2)}, u32[]{:S(2)}) collective-permute-start(bf16[96,640]{1,0:T(8,128)(2,1)S(1)} %get-tuple-element.26), channel_id=1, source_target_pairs={{0,3},{1,2},{2,1},{3,0},{4,7},{5,6},{6,5},{7,4},{8,11},{9,10},{10,... | collective-permute-start | bytes 368648 | tf_op jit(solution)/shard_map/ppermute | solution.py:536
  32.1 1.6 %collective-permute-start.14 = (bf16[128,320]{1,0:T(8,128)(2,1)S(1)}, bf16[128,320]{1,0:T(8,128)(2,1)S(1)}, u32[]{:S(2)}, u32[]{:S(2)}) collective-permute-start(bf16[128,320]{1,0:T(8,128)(2,1)S(1)} %get-tuple-element.31), channel_id=1, source_target_pairs={{0,8},{4,12},{8,0},{12,4},{16,24},{20,28},{24,16},{28,20},{1,9},{5... | collective-permute-start | bytes 245768 | tf_op jit(solution)/shard_map/ppermute | solution.py:533
  33.6 0.8 %collective-permute-start.15 = (bf16[128,320]{1,0:T(8,128)(2,1)S(1)}, bf16[128,320]{1,0:T(8,128)(2,1)S(1)}, u32[]{:S(2)}, u32[]{:S(2)}) collective-permute-start(bf16[128,320]{1,0:T(8,128)(2,1)S(1)} %get-tuple-element.32), channel_id=1, source_target_pairs={{0,16},{4,20},{8,24},{12,28},{16,0},{20,4},{24,8},{28,12},{1,17},{... | collective-permute-start | bytes 245768 | tf_op jit(solution)/shard_map/ppermute | solution.py:533
  34.5 1.7 %collective-permute-start.16 = (bf16[128,320]{1,0:T(8,128)(2,1)S(1)}, bf16[128,320]{1,0:T(8,128)(2,1)S(1)}, u32[]{:S(2)}, u32[]{:S(2)}) collective-permute-start(bf16[128,320]{1,0:T(8,128)(2,1)S(1)} %get-tuple-element.33), channel_id=1, source_target_pairs={{0,24},{4,28},{8,16},{12,20},{16,8},{20,12},{24,0},{28,4},{1,25},{... | collective-permute-start | bytes 245768 | tf_op jit(solution)/shard_map/ppermute | solution.py:533
  36.3 0.9 %tables.1 = (bf16[2,320,192]{2,1,0:T(8,128)(2,1)S(1)}, bf16[2,320,160]{2,1,0:T(8,128)(2,1)S(1)}, bf16[2,384,720]{2,1,0:T(8,128)(2,1)S(1)}) custom-call(f32[128,320]{1,0:T(8,128)S(1)} %get-tuple-element.34.after_ref.refs_7_), custom_call_target="tpu_custom_call" | custom-call | flops 1000000 | bytes 3000 | tf_op jit(solution)/shard_map/tables/pallas_call | solution.py:508
  37.1 3.3 %collective-permute-done.11.refs_2_ = bf16[96,640]{1,0:T(8,128)(2,1)S(1)} collective-permute-done((bf16[96,640]{1,0:T(8,128)(2,1)S(1)}, bf16[96,640]{1,0:T(8,128)(2,1)S(1)}, u32[]{:S(2)}, u32[]{:S(2)}) %collective-permute-start.11) | collective-permute-done | bytes 122912 | tf_op jit(solution)/shard_map/ppermute | solution.py:536
  40.5 1.8 %collective-permute-start.19 = (bf16[96,640]{1,0:T(8,128)(2,1)S(1)}, bf16[96,640]{1,0:T(8,128)(2,1)S(1)}, u32[]{:S(2)}, u32[]{:S(2)}) collective-permute-start(bf16[96,640]{1,0:T(8,128)(2,1)S(1)} %total.1.refs_0_), channel_id=1, source_target_pairs={{0,24},{4,28},{8,16},{12,20},{16,8},{20,12},{24,0},{28,4},{1,25},{... | collective-permute-start | bytes 368648 | tf_op jit(solution)/shard_map/ppermute | solution.py:533
  42.4 1.2 %collective-permute-start.18 = (bf16[96,640]{1,0:T(8,128)(2,1)S(1)}, bf16[96,640]{1,0:T(8,128)(2,1)S(1)}, u32[]{:S(2)}, u32[]{:S(2)}) collective-permute-start(bf16[96,640]{1,0:T(8,128)(2,1)S(1)} %total.1.refs_0_), channel_id=1, source_target_pairs={{0,16},{4,20},{8,24},{12,28},{16,0},{20,4},{24,8},{28,12},{1,17},{... | collective-permute-start | bytes 368648 | tf_op jit(solution)/shard_map/ppermute | solution.py:533
  43.6 0.5 %collective-permute-start.17 = (bf16[96,640]{1,0:T(8,128)(2,1)S(1)}, bf16[96,640]{1,0:T(8,128)(2,1)S(1)}, u32[]{:S(2)}, u32[]{:S(2)}) collective-permute-start(bf16[96,640]{1,0:T(8,128)(2,1)S(1)} %total.1.refs_0_), channel_id=1, source_target_pairs={{0,8},{4,12},{8,0},{12,4},{16,24},{20,28},{24,16},{28,20},{1,9},{5... | collective-permute-start | bytes 368648 | tf_op jit(solution)/shard_map/ppermute | solution.py:533
  44.1 2.7 %collective-permute-done.19.refs_3_ = bf16[96,640]{1,0:T(8,128)(2,1)S(1)} collective-permute-done((bf16[96,640]{1,0:T(8,128)(2,1)S(1)}, bf16[96,640]{1,0:T(8,128)(2,1)S(1)}, u32[]{:S(2)}, u32[]{:S(2)}) %collective-permute-start.19) | collective-permute-done | bytes 122912 | tf_op jit(solution)/shard_map/ppermute | solution.py:533
  46.8 1.2 %collective-permute-done.18.refs_2_ = bf16[96,640]{1,0:T(8,128)(2,1)S(1)} collective-permute-done((bf16[96,640]{1,0:T(8,128)(2,1)S(1)}, bf16[96,640]{1,0:T(8,128)(2,1)S(1)}, u32[]{:S(2)}, u32[]{:S(2)}) %collective-permute-start.18) | collective-permute-done | bytes 122912 | tf_op jit(solution)/shard_map/ppermute | solution.py:533
  48.0 0.4 collective-permute-done.17.refs_1_
  48.6 0.6 %part.1 = (f32[320,720]{1,0:T(8,128)S(1)}, f32[320,720]{1,0:T(8,128)S(1)}) custom-call(bf16[4,96,640]{2,1,0:T(8,128)(2,1)S(1)} %stack.1.stack_ref, bf16[2,320,192]{2,1,0:T(8,128)(2,1)S(1)} %get-tuple-element.35.refs_7_.main_ref.refs_1_, bf16[2,320,160]{2,1,0:T(8,128)(2,1)S(1)} %get-tuple-element.36.fold_ref.refs_2_, ...), custom_call_target="tpu_custom_call" | custom-call | flops 1000000 | bytes 3000 | tf_op jit(solution)/shard_map/part/pallas_call | solution.py:508
  49.2 1.2 %collective-permute-done.20.refs_0_ = bf16[4,96,640]{2,1,0:T(8,128)(2,1)S(1)} collective-permute-done((bf16[4,96,640]{2,1,0:T(8,128)(2,1)S(1)}, bf16[4,96,640]{2,1,0:T(8,128)(2,1)S(1)}, u32[]{:S(2)}, u32[]{:S(2)}) %collective-permute-start.20) | collective-permute-done | bytes 491552 | tf_op jit(solution)/shard_map/ppermute | solution.py:533
  50.4 2.0 %last.1 = (f32[320,720]{1,0:T(8,128)}, f32[320,720]{1,0:T(8,128)}, bf16[128,320]{1,0:T(8,128)(2,1)}) custom-call(bf16[4,96,640]{2,1,0:T(8,128)(2,1)S(1)} %collective-permute-done.20.refs_0_, bf16[2,320,192]{2,1,0:T(8,128)(2,1)S(1)} %get-tuple-element.35.refs_7_.main_ref.refs_1_, bf16[2,320,160]{2,1,0:T(8,128)(2,1)S(1)} %get-tuple-element.36.fold_ref.refs_2_, ...), custom_call_target="tpu_custom_call" | custom-call | flops 100000000 | bytes 300000 | tf_op jit(solution)/shard_map/last/pallas_call | solution.py:508
  (30 shorter events, 1.0 us)
Async XLA Ops:
  0.6 8.2 %copy-start = (bf16[1,8,16,320]{3,2,1,0:T(8,128)(2,1)S(1)}, bf16[1,8,16,320]{3,2,1,0:T(8,128)(2,1)}, u32[]{:S(2)}) copy-start(bf16[1,8,16,320]{3,2,1,0:T(8,128)(2,1)} %param.7) | copy-start | bytes 245764
  0.6 8.2 %copy-start.2 = (bf16[1,8,16,320]{3,2,1,0:T(8,128)(2,1)S(1)}, bf16[1,8,16,320]{3,2,1,0:T(8,128)(2,1)}, u32[]{:S(2)}) copy-start(bf16[1,8,16,320]{3,2,1,0:T(8,128)(2,1)} %param.8) | copy-start | bytes 245764
  2.5 10.4 %collective-permute-start.8 = (bf16[96,640]{1,0:T(8,128)(2,1)S(1)}, bf16[96,640]{1,0:T(8,128)(2,1)S(1)}, u32[]{:S(2)}, u32[]{:S(2)}) collective-permute-start(bf16[96,640]{1,0:T(8,128)(2,1)S(1)} %slices.1.after_ref.refs_8_), channel_id=1, source_target_pairs={{0,2},{1,3},{2,0},{3,1},{4,6},{5,7},{6,4},{7,5},{8,10},{9,11},{10,... | collective-permute-start | bytes 368648 | tf_op jit(solution)/shard_map/ppermute | solution.py:536
  6.6 6.3 %collective-permute-start.7 = (bf16[96,640]{1,0:T(8,128)(2,1)S(1)}, bf16[96,640]{1,0:T(8,128)(2,1)S(1)}, u32[]{:S(2)}, u32[]{:S(2)}) collective-permute-start(bf16[96,640]{1,0:T(8,128)(2,1)S(1)} %slices.1.after_ref.refs_8_), channel_id=1, source_target_pairs={{0,1},{1,0},{2,3},{3,2},{4,5},{5,4},{6,7},{7,6},{8,9},{9,8},{10,11... | collective-permute-start | bytes 368648 | tf_op jit(solution)/shard_map/ppermute | solution.py:536
  9.3 11.3 %copy-start.1 = (bf16[1280,320]{0,1:T(8,128)(2,1)S(1)}, bf16[1280,320]{0,1:T(8,128)(2,1)}, u32[]{:S(2)}) copy-start(bf16[1280,320]{0,1:T(8,128)(2,1)} %param.11) | copy-start | bytes 2457604
  9.4 8.3 %collective-permute-start.5 = (bf16[144,640]{1,0:T(8,128)(2,1)S(1)}, bf16[144,640]{1,0:T(8,128)(2,1)S(1)}, u32[]{:S(2)}, u32[]{:S(2)}) collective-permute-start(bf16[144,640]{1,0:T(8,128)(2,1)S(1)} %act.1.refs_0_), channel_id=1, source_target_pairs={{0,24},{4,28},{8,16},{12,20},{16,8},{20,12},{24,0},{28,4},{1,25},{... | collective-permute-start | bytes 552968 | tf_op jit(solution)/shard_map/ppermute | solution.py:533
  11.9 8.2 %collective-permute-start.3 = (bf16[144,640]{1,0:T(8,128)(2,1)S(1)}, bf16[144,640]{1,0:T(8,128)(2,1)S(1)}, u32[]{:S(2)}, u32[]{:S(2)}) collective-permute-start(bf16[144,640]{1,0:T(8,128)(2,1)S(1)} %act.1.refs_0_), channel_id=1, source_target_pairs={{0,16},{4,20},{8,24},{12,28},{16,0},{20,4},{24,8},{28,12},{1,17},{... | collective-permute-start | bytes 552968 | tf_op jit(solution)/shard_map/ppermute | solution.py:533
  12.4 7.8 %collective-permute-start.1 = (bf16[144,640]{1,0:T(8,128)(2,1)S(1)}, bf16[144,640]{1,0:T(8,128)(2,1)S(1)}, u32[]{:S(2)}, u32[]{:S(2)}) collective-permute-start(bf16[144,640]{1,0:T(8,128)(2,1)S(1)} %act.1.refs_0_), channel_id=1, source_target_pairs={{0,8},{4,12},{8,0},{12,4},{16,24},{20,28},{24,16},{28,20},{1,9},{5... | collective-permute-start | bytes 552968 | tf_op jit(solution)/shard_map/ppermute | solution.py:533
  12.9 8.1 %collective-permute-start = (bf16[144,640]{1,0:T(8,128)(2,1)S(1)}, bf16[144,640]{1,0:T(8,128)(2,1)S(1)}, u32[]{:S(2)}, u32[]{:S(2)}) collective-permute-start(bf16[144,640]{1,0:T(8,128)(2,1)S(1)} %act.1.refs_0_), channel_id=1, source_target_pairs={{0,4},{4,0},{8,12},{12,8},{16,20},{20,16},{24,28},{28,24},{1,5},{5... | collective-permute-start | bytes 552968 | tf_op jit(solution)/shard_map/ppermute | solution.py:533
  12.9 8.1 %collective-permute-start.9 = (bf16[96,640]{1,0:T(8,128)(2,1)S(1)}, bf16[96,640]{1,0:T(8,128)(2,1)S(1)}, u32[]{:S(2)}, u32[]{:S(2)}) collective-permute-start(bf16[96,640]{1,0:T(8,128)(2,1)S(1)} %relay.1.refs_10_), channel_id=1, source_target_pairs={{0,1},{1,0},{2,3},{3,2},{4,5},{5,4},{6,7},{7,6},{8,9},{9,8},{10,11... | collective-permute-start | bytes 368648 | tf_op jit(solution)/shard_map/ppermute | solution.py:536
  17.7 3.4 %collective-permute-start.6 = (bf16[144,640]{1,0:T(8,128)(2,1)S(1)}, bf16[144,640]{1,0:T(8,128)(2,1)S(1)}, u32[]{:S(2)}, u32[]{:S(2)}) collective-permute-start(bf16[144,640]{1,0:T(8,128)(2,1)S(1)} %collective-permute-done.5.refs_6_), channel_id=1, source_target_pairs={{0,4},{4,0},{8,12},{12,8},{16,20},{20,16},{24,28},{28,24},{1,5},{5... | collective-permute-start | bytes 552968 | tf_op jit(solution)/shard_map/ppermute | solution.py:533
  20.1 1.4 %collective-permute-start.4 = (bf16[144,640]{1,0:T(8,128)(2,1)S(1)}, bf16[144,640]{1,0:T(8,128)(2,1)S(1)}, u32[]{:S(2)}, u32[]{:S(2)}) collective-permute-start(bf16[144,640]{1,0:T(8,128)(2,1)S(1)} %collective-permute-done.3.refs_4_), channel_id=1, source_target_pairs={{0,4},{4,0},{8,12},{12,8},{16,20},{20,16},{24,28},{28,24},{1,5},{5... | collective-permute-start | bytes 552968 | tf_op jit(solution)/shard_map/ppermute | solution.py:533
  20.2 1.6 %collective-permute-start.2 = (bf16[144,640]{1,0:T(8,128)(2,1)S(1)}, bf16[144,640]{1,0:T(8,128)(2,1)S(1)}, u32[]{:S(2)}, u32[]{:S(2)}) collective-permute-start(bf16[144,640]{1,0:T(8,128)(2,1)S(1)} %collective-permute-done.1.refs_2_), channel_id=1, source_target_pairs={{0,4},{4,0},{8,12},{12,8},{16,20},{20,16},{24,28},{28,24},{1,5},{5... | collective-permute-start | bytes 552968 | tf_op jit(solution)/shard_map/ppermute | solution.py:533
  20.6 1.2 %copy-start.3 = (s32[4]{0:T(128)S(1)}, s32[4]{0:T(128)}, u32[]{:S(2)}) copy-start(s32[4]{0:T(128)} %owner_ref.1) | copy-start | bytes 52
  27.3 4.7 %collective-permute-start.13 = (bf16[4,128,320]{2,1,0:T(8,128)(2,1)S(1)}, bf16[4,128,320]{2,1,0:T(8,128)(2,1)S(1)}, u32[]{:S(2)}, u32[]{:S(2)}) collective-permute-start(bf16[4,128,320]{2,1,0:T(8,128)(2,1)S(1)} %get-tuple-element.30), channel_id=1, source_target_pairs={{0,4},{4,0},{8,12},{12,8},{16,20},{20,16},{24,28},{28,24},{1,5},{5... | collective-permute-start | bytes 983048 | tf_op jit(solution)/shard_map/ppermute | solution.py:533
  27.6 6.9 %collective-permute-start.10 = (bf16[96,640]{1,0:T(8,128)(2,1)S(1)}, bf16[96,640]{1,0:T(8,128)(2,1)S(1)}, u32[]{:S(2)}, u32[]{:S(2)}) collective-permute-start(bf16[96,640]{1,0:T(8,128)(2,1)S(1)} %get-tuple-element.24), channel_id=1, source_target_pairs={{0,1},{1,0},{2,3},{3,2},{4,5},{5,4},{6,7},{7,6},{8,9},{9,8},{10,11... | collective-permute-start | bytes 368648 | tf_op jit(solution)/shard_map/ppermute | solution.py:536
  28.1 12.4 %collective-permute-start.11 = (bf16[96,640]{1,0:T(8,128)(2,1)S(1)}, bf16[96,640]{1,0:T(8,128)(2,1)S(1)}, u32[]{:S(2)}, u32[]{:S(2)}) collective-permute-start(bf16[96,640]{1,0:T(8,128)(2,1)S(1)} %get-tuple-element.25), channel_id=1, source_target_pairs={{0,2},{1,3},{2,0},{3,1},{4,6},{5,7},{6,4},{7,5},{8,10},{9,11},{10,... | collective-permute-start | bytes 368648 | tf_op jit(solution)/shard_map/ppermute | solution.py:536
  28.4 12.0 %collective-permute-start.12 = (bf16[96,640]{1,0:T(8,128)(2,1)S(1)}, bf16[96,640]{1,0:T(8,128)(2,1)S(1)}, u32[]{:S(2)}, u32[]{:S(2)}) collective-permute-start(bf16[96,640]{1,0:T(8,128)(2,1)S(1)} %get-tuple-element.26), channel_id=1, source_target_pairs={{0,3},{1,2},{2,1},{3,0},{4,7},{5,6},{6,5},{7,4},{8,11},{9,10},{10,... | collective-permute-start | bytes 368648 | tf_op jit(solution)/shard_map/ppermute | solution.py:536
  32.1 8.4 %collective-permute-start.14 = (bf16[128,320]{1,0:T(8,128)(2,1)S(1)}, bf16[128,320]{1,0:T(8,128)(2,1)S(1)}, u32[]{:S(2)}, u32[]{:S(2)}) collective-permute-start(bf16[128,320]{1,0:T(8,128)(2,1)S(1)} %get-tuple-element.31), channel_id=1, source_target_pairs={{0,8},{4,12},{8,0},{12,4},{16,24},{20,28},{24,16},{28,20},{1,9},{5... | collective-permute-start | bytes 245768 | tf_op jit(solution)/shard_map/ppermute | solution.py:533
  33.6 6.8 %collective-permute-start.15 = (bf16[128,320]{1,0:T(8,128)(2,1)S(1)}, bf16[128,320]{1,0:T(8,128)(2,1)S(1)}, u32[]{:S(2)}, u32[]{:S(2)}) collective-permute-start(bf16[128,320]{1,0:T(8,128)(2,1)S(1)} %get-tuple-element.32), channel_id=1, source_target_pairs={{0,16},{4,20},{8,24},{12,28},{16,0},{20,4},{24,8},{28,12},{1,17},{... | collective-permute-start | bytes 245768 | tf_op jit(solution)/shard_map/ppermute | solution.py:533
  34.5 6.0 %collective-permute-start.16 = (bf16[128,320]{1,0:T(8,128)(2,1)S(1)}, bf16[128,320]{1,0:T(8,128)(2,1)S(1)}, u32[]{:S(2)}, u32[]{:S(2)}) collective-permute-start(bf16[128,320]{1,0:T(8,128)(2,1)S(1)} %get-tuple-element.33), channel_id=1, source_target_pairs={{0,24},{4,28},{8,16},{12,20},{16,8},{20,12},{24,0},{28,4},{1,25},{... | collective-permute-start | bytes 245768 | tf_op jit(solution)/shard_map/ppermute | solution.py:533
  40.5 6.2 %collective-permute-start.19 = (bf16[96,640]{1,0:T(8,128)(2,1)S(1)}, bf16[96,640]{1,0:T(8,128)(2,1)S(1)}, u32[]{:S(2)}, u32[]{:S(2)}) collective-permute-start(bf16[96,640]{1,0:T(8,128)(2,1)S(1)} %total.1.refs_0_), channel_id=1, source_target_pairs={{0,24},{4,28},{8,16},{12,20},{16,8},{20,12},{24,0},{28,4},{1,25},{... | collective-permute-start | bytes 368648 | tf_op jit(solution)/shard_map/ppermute | solution.py:533
  42.4 5.6 %collective-permute-start.18 = (bf16[96,640]{1,0:T(8,128)(2,1)S(1)}, bf16[96,640]{1,0:T(8,128)(2,1)S(1)}, u32[]{:S(2)}, u32[]{:S(2)}) collective-permute-start(bf16[96,640]{1,0:T(8,128)(2,1)S(1)} %total.1.refs_0_), channel_id=1, source_target_pairs={{0,16},{4,20},{8,24},{12,28},{16,0},{20,4},{24,8},{28,12},{1,17},{... | collective-permute-start | bytes 368648 | tf_op jit(solution)/shard_map/ppermute | solution.py:533
  43.6 4.9 %collective-permute-start.17 = (bf16[96,640]{1,0:T(8,128)(2,1)S(1)}, bf16[96,640]{1,0:T(8,128)(2,1)S(1)}, u32[]{:S(2)}, u32[]{:S(2)}) collective-permute-start(bf16[96,640]{1,0:T(8,128)(2,1)S(1)} %total.1.refs_0_), channel_id=1, source_target_pairs={{0,8},{4,12},{8,0},{12,4},{16,24},{20,28},{24,16},{28,20},{1,9},{5... | collective-permute-start | bytes 368648 | tf_op jit(solution)/shard_map/ppermute | solution.py:533
  48.5 1.9 %collective-permute-start.20 = (bf16[4,96,640]{2,1,0:T(8,128)(2,1)S(1)}, bf16[4,96,640]{2,1,0:T(8,128)(2,1)S(1)}, u32[]{:S(2)}, u32[]{:S(2)}) collective-permute-start(bf16[4,96,640]{2,1,0:T(8,128)(2,1)S(1)} %stack.1.stack_ref), channel_id=1, source_target_pairs={{0,4},{4,0},{8,12},{12,8},{16,20},{20,16},{24,28},{28,24},{1,5},{5... | collective-permute-start | bytes 1474568 | tf_op jit(solution)/shard_map/ppermute | solution.py:533

commit v6 on v5

--- a/solution.py
+++ b/solution.py
@@ -464,21 +464,19 @@
     return tn(jnp.concatenate(rows, axis=0), table)
 
 
-def part_kernel(plan, stack_ref, main_ref, fold_ref, second_ref, out1_ref, out2_ref):
-    out1_ref[...] = first_in_place(plan, stack_ref, main_ref[0], fold_ref[0])
-    out2_ref[...] = second_in_place(plan, stack_ref, second_ref[0])
-
-
-def last_kernel(plan, scale, n_came, *refs):
-    came, tables, part1_ref, part2_ref, x_ref = refs[0:n_came], refs[n_came : n_came + 3], *refs[n_came + 3 : n_came + 6]
-    shares = refs[n_came + 6 : -7]
-    first_any, second_any, output_any, first_ref, second_ref, output_ref, sems = refs[-7:]
+def part_kernel(plan, stack_ref, main_ref, fold_ref, second_ref, x_ref, *refs):
+    *shares, out1_ref, out2_ref, output_ref = refs
     total = x_ref[...].astype(F32)
     for ref in shares:
         total = total + ref[...].reshape(total.shape).astype(F32)
     output_ref[...] = total.astype(BF16)
-    copy0 = pltpu.make_async_copy(output_ref, output_any, sems.at[2])
-    copy0.start()
+    out1_ref[...] = first_in_place(plan, stack_ref, main_ref[0], fold_ref[0])
+    out2_ref[...] = second_in_place(plan, stack_ref, second_ref[0])
+
+
+def last_kernel(plan, scale, n_came, *refs):
+    came, tables, part1_ref, part2_ref = refs[0:n_came], refs[n_came : n_came + 3], *refs[n_came + 3 : n_came + 5]
+    first_any, second_any, first_ref, second_ref, sems = refs[-5:]
     first = part1_ref[...]
     for ref in came:
         first = first + first_in_place(plan, ref, tables[0][1], tables[1][1])
@@ -491,7 +489,6 @@
     second_ref[...] = second * scale
     copy2 = pltpu.make_async_copy(second_ref, second_any, sems.at[1])
     copy2.start()
-    copy0.wait()
     copy1.wait()
     copy2.wait()
 
@@ -664,26 +661,25 @@
         slots = [total] + [to_rep(total, step) for step in range(2, team, 2)]
         stack = call(stack_kernel, "stack", shape((half, *both), BF16), slots, 0.001)
         came = [to_rep(stack, 1)]
-    part1, part2 = call(
+    part1, part2, output = call(
         functools.partial(part_kernel, plan),
         "part",
-        (shape((c, r), F32), shape((c, r), F32)),
-        (stack, *tables),
+        (shape((c, r), F32), shape((c, r), F32), shape((pix, c), BF16)),
+        (stack, *tables, x, *shares),
         0.001,
     )
-    first, second, output = call(
+    first, second = call(
         functools.partial(last_kernel, plan, scale, len(came)),
         "last",
-        (shape((c, r), F32), shape((c, r), F32), shape((pix, c), BF16)),
-        (*came, *tables, part1, part2, x, *shares),
+        (shape((c, r), F32), shape((c, r), F32)),
+        (*came, *tables, part1, part2),
         0.1,
         scratch=(
             pltpu.VMEM((c, r), F32),
             pltpu.VMEM((c, r), F32),
-            pltpu.VMEM((pix, c), BF16),
-            pltpu.SemaphoreType.DMA((3,)),
+            pltpu.SemaphoreType.DMA((2,)),
         ),
-        out_hbm=3,
+        out_hbm=2,
     )
     return output.reshape(1, height, width, c), first.T, second.T
 

time: 52.6 us -> 53.9 us (1.025)
  waiting for transfers between devices: 15.5 us -> 17.5 us
  starting transfers between devices: 23.5 us -> 22.4 us
    ppermute x6, waiting for transfers between devices: 3.39 us -> 4.69 us  [to_dom(): return lax.ppermute(value, 'dom', [(i, i ^ step) for i in range(d)])]
    ppermute x6, starting transfers between devices: 11.5 us -> 10.6 us  [to_dom(): return lax.ppermute(value, 'dom', [(i, i ^ step) for i in range(d)])]
    ppermute x15, waiting for transfers between devices: 12.1 us -> 12.8 us  [to_rep(): return lax.ppermute(value, 'rep', [(i, i ^ step) for i in range(n_rep)])]
  transfers between devices with their start and end apart: 21 -> 21, of which waited for: 10 -> 11; matrix products, arithmetic and copies ran while one was open for 0% -> 0% of each run, Pallas kernels for 5% -> 6%
where the time goes in v6:
time: 53.9 us; the launch traced here: 53.7 us
  starting transfers between devices  22.4 us (42%)
  waiting for transfers between devices  17.5 us (32%)
  Pallas kernels  12.3 us (23%)
  between operations  1.44 us (3%)
    ppermute x15, waiting for transfers between devices, to_rep(): return lax.ppermute(value, 'rep', [(i, i ^ step) for i in range(n_rep)])  12.8 us
    pallas_call x12, Pallas kernels, call(): pl.pallas_call(kernel, name=name, out_shape=out_shape, in_specs=[SMEM] *...  12.3 us
    ppermute x15, starting transfers between devices, to_rep(): return lax.ppermute(value, 'rep', [(i, i ^ step) for i in range(n_rep)])  11.8 us
    ppermute x6, starting transfers between devices, to_dom(): return lax.ppermute(value, 'dom', [(i, i ^ step) for i in range(d)])  10.6 us
    ppermute x6, waiting for transfers between devices, to_dom(): return lax.ppermute(value, 'dom', [(i, i ^ step) for i in range(d)])  4.69 us
  transfers between devices with their start and end apart: 21, of which 11 were waited for; matrix products, arithmetic and copies ran while one was open for 0% of the time, Pallas kernels for 6%

profile of v6, /device:TPU:0, one launch (start us, length us, event | category | flops | bytes accessed | tf_op | source)
XLA Modules:
  0.0 53.7 jit_solution(11286132853717713822)
XLA Ops:
  0.7 1.8 %slices.1.after_ref.refs_8_ = bf16[96,640]{1,0:T(8,128)(2,1)S(1)} custom-call(bf16[320,720]{1,0:T(8,128)(2,1)} %bitcast.16, bf16[320,720]{1,0:T(8,128)(2,1)} %bitcast.17), custom_call_target="tpu_custom_call" | custom-call | flops 2000000000 | bytes 6000000 | tf_op jit(solution)/shard_map/slices/pallas_call | solution.py:505
  2.5 3.1 %collective-permute-start.7 = (bf16[96,640]{1,0:T(8,128)(2,1)S(1)}, bf16[96,640]{1,0:T(8,128)(2,1)S(1)}, u32[]{:S(2)}, u32[]{:S(2)}) collective-permute-start(bf16[96,640]{1,0:T(8,128)(2,1)S(1)} %slices.1.after_ref.refs_8_), channel_id=1, source_target_pairs={{0,1},{1,0},{2,3},{3,2},{4,5},{5,4},{6,7},{7,6},{8,9},{9,8},{10,11... | collective-permute-start | bytes 368648 | tf_op jit(solution)/shard_map/ppermute | solution.py:533
  5.6 2.6 %collective-permute-start.8 = (bf16[96,640]{1,0:T(8,128)(2,1)S(1)}, bf16[96,640]{1,0:T(8,128)(2,1)S(1)}, u32[]{:S(2)}, u32[]{:S(2)}) collective-permute-start(bf16[96,640]{1,0:T(8,128)(2,1)S(1)} %slices.1.after_ref.refs_8_), channel_id=1, source_target_pairs={{0,2},{1,3},{2,0},{3,1},{4,6},{5,7},{6,4},{7,5},{8,10},{9,11},{10,... | collective-permute-start | bytes 368648 | tf_op jit(solution)/shard_map/ppermute | solution.py:533
  8.8 0.5 act.1.refs_0_
  9.4 1.6 %collective-permute-start.1 = (bf16[144,640]{1,0:T(8,128)(2,1)S(1)}, bf16[144,640]{1,0:T(8,128)(2,1)S(1)}, u32[]{:S(2)}, u32[]{:S(2)}) collective-permute-start(bf16[144,640]{1,0:T(8,128)(2,1)S(1)} %act.1.refs_0_), channel_id=1, source_target_pairs={{0,8},{4,12},{8,0},{12,4},{16,24},{20,28},{24,16},{28,20},{1,9},{5... | collective-permute-start | bytes 552968 | tf_op jit(solution)/shard_map/ppermute | solution.py:530
  11.0 1.5 %collective-permute-start.3 = (bf16[144,640]{1,0:T(8,128)(2,1)S(1)}, bf16[144,640]{1,0:T(8,128)(2,1)S(1)}, u32[]{:S(2)}, u32[]{:S(2)}) collective-permute-start(bf16[144,640]{1,0:T(8,128)(2,1)S(1)} %act.1.refs_0_), channel_id=1, source_target_pairs={{0,16},{4,20},{8,24},{12,28},{16,0},{20,4},{24,8},{28,12},{1,17},{... | collective-permute-start | bytes 552968 | tf_op jit(solution)/shard_map/ppermute | solution.py:530
  12.5 0.7 %collective-permute-start.5 = (bf16[144,640]{1,0:T(8,128)(2,1)S(1)}, bf16[144,640]{1,0:T(8,128)(2,1)S(1)}, u32[]{:S(2)}, u32[]{:S(2)}) collective-permute-start(bf16[144,640]{1,0:T(8,128)(2,1)S(1)} %act.1.refs_0_), channel_id=1, source_target_pairs={{0,24},{4,28},{8,16},{12,20},{16,8},{20,12},{24,0},{28,4},{1,25},{... | collective-permute-start | bytes 552968 | tf_op jit(solution)/shard_map/ppermute | solution.py:530
  13.2 0.8 %collective-permute-done.8.pass_ref = bf16[96,640]{1,0:T(8,128)(2,1)S(1)} collective-permute-done((bf16[96,640]{1,0:T(8,128)(2,1)S(1)}, bf16[96,640]{1,0:T(8,128)(2,1)S(1)}, u32[]{:S(2)}, u32[]{:S(2)}) %collective-permute-start.8) | collective-permute-done | bytes 122912 | tf_op jit(solution)/shard_map/ppermute | solution.py:533
  14.0 0.5 collective-permute-start.9
  14.5 2.5 %collective-permute-done.1.refs_2_ = bf16[144,640]{1,0:T(8,128)(2,1)S(1)} collective-permute-done((bf16[144,640]{1,0:T(8,128)(2,1)S(1)}, bf16[144,640]{1,0:T(8,128)(2,1)S(1)}, u32[]{:S(2)}, u32[]{:S(2)}) %collective-permute-start.1) | collective-permute-done | bytes 184352 | tf_op jit(solution)/shard_map/ppermute | solution.py:530
  16.9 4.7 %collective-permute-done.3.refs_4_ = bf16[144,640]{1,0:T(8,128)(2,1)S(1)} collective-permute-done((bf16[144,640]{1,0:T(8,128)(2,1)S(1)}, bf16[144,640]{1,0:T(8,128)(2,1)S(1)}, u32[]{:S(2)}, u32[]{:S(2)}) %collective-permute-start.3) | collective-permute-done | bytes 184352 | tf_op jit(solution)/shard_map/ppermute | solution.py:530
  21.7 0.5 collective-permute-start.6
  22.2 0.4 time_own.1.refs_12_
  22.6 0.5 collective-permute-done.4.refs_5_
  23.3 4.9 %main.1 = (bf16[8,160,128]{2,1,0:T(8,128)(2,1)S(1)}, bf16[384,320]{1,0:T(8,128)(2,1)S(1)}, f32[96,640]{1,0:T(8,128)S(1)}, bf16[96,640]{1,0:T(8,128)(2,1)S(1)}, b...) custom-call(s32[4]{0:T(128)S(1)} %copy-done.3, bf16[144,640]{1,0:T(8,128)(2,1)S(1)} %act.1.refs_0_, ...), custom_call_target="tpu_custom_call" | custom-call | flops 6000000000 | bytes 18000000 | tf_op jit(solution)/shard_map/main/pallas_call | solution.py:505
  28.2 0.6 %share.1 = (f32[4,128,320]{2,1,0:T(8,128)S(1)}, bf16[4,128,320]{2,1,0:T(8,128)(2,1)S(1)}) custom-call(bf16[8,160,128]{2,1,0:T(8,128)(2,1)S(1)} %get-tuple-element.27.act2p, bf16[384,320]{1,0:T(8,128)(2,1)S(1)} %get-tuple-element.28.w2_ref, f32[96,640]{1,0:T(8,128)S(1)} %get-tuple-element.23.after_ref.refs_0_), custom_call_target="tpu_custom_call" | custom-call | flops 1000000 | bytes 3000 | tf_op jit(solution)/shard_map/share/pallas_call | solution.py:505
  29.2 0.5 collective-permute-start.10
  30.0 3.6 %collective-permute-start.12 = (bf16[96,640]{1,0:T(8,128)(2,1)S(1)}, bf16[96,640]{1,0:T(8,128)(2,1)S(1)}, u32[]{:S(2)}, u32[]{:S(2)}) collective-permute-start(bf16[96,640]{1,0:T(8,128)(2,1)S(1)} %get-tuple-element.26), channel_id=1, source_target_pairs={{0,3},{1,2},{2,1},{3,0},{4,7},{5,6},{6,5},{7,4},{8,11},{9,10},{10,... | collective-permute-start | bytes 368648 | tf_op jit(solution)/shard_map/ppermute | solution.py:533
  33.6 0.9 %collective-permute-start.14 = (bf16[128,320]{1,0:T(8,128)(2,1)S(1)}, bf16[128,320]{1,0:T(8,128)(2,1)S(1)}, u32[]{:S(2)}, u32[]{:S(2)}) collective-permute-start(bf16[128,320]{1,0:T(8,128)(2,1)S(1)} %get-tuple-element.31), channel_id=1, source_target_pairs={{0,8},{4,12},{8,0},{12,4},{16,24},{20,28},{24,16},{28,20},{1,9},{5... | collective-permute-start | bytes 245768 | tf_op jit(solution)/shard_map/ppermute | solution.py:530
  34.6 1.2 %collective-permute-start.15 = (bf16[128,320]{1,0:T(8,128)(2,1)S(1)}, bf16[128,320]{1,0:T(8,128)(2,1)S(1)}, u32[]{:S(2)}, u32[]{:S(2)}) collective-permute-start(bf16[128,320]{1,0:T(8,128)(2,1)S(1)} %get-tuple-element.32), channel_id=1, source_target_pairs={{0,16},{4,20},{8,24},{12,28},{16,0},{20,4},{24,8},{28,12},{1,17},{... | collective-permute-start | bytes 245768 | tf_op jit(solution)/shard_map/ppermute | solution.py:530
  36.1 1.5 %collective-permute-start.16 = (bf16[128,320]{1,0:T(8,128)(2,1)S(1)}, bf16[128,320]{1,0:T(8,128)(2,1)S(1)}, u32[]{:S(2)}, u32[]{:S(2)}) collective-permute-start(bf16[128,320]{1,0:T(8,128)(2,1)S(1)} %get-tuple-element.33), channel_id=1, source_target_pairs={{0,24},{4,28},{8,16},{12,20},{16,8},{20,12},{24,0},{28,4},{1,25},{... | collective-permute-start | bytes 245768 | tf_op jit(solution)/shard_map/ppermute | solution.py:530
  37.5 0.9 %tables.1 = (bf16[2,320,192]{2,1,0:T(8,128)(2,1)S(1)}, bf16[2,320,160]{2,1,0:T(8,128)(2,1)S(1)}, bf16[2,384,720]{2,1,0:T(8,128)(2,1)S(1)}) custom-call(f32[128,320]{1,0:T(8,128)S(1)} %get-tuple-element.34.after_ref.refs_0_), custom_call_target="tpu_custom_call" | custom-call | flops 1000000 | bytes 3000 | tf_op jit(solution)/shard_map/tables/pallas_call | solution.py:505
  38.4 3.6 %collective-permute-done.11.refs_2_ = bf16[96,640]{1,0:T(8,128)(2,1)S(1)} collective-permute-done((bf16[96,640]{1,0:T(8,128)(2,1)S(1)}, bf16[96,640]{1,0:T(8,128)(2,1)S(1)}, u32[]{:S(2)}, u32[]{:S(2)}) %collective-permute-start.11) | collective-permute-done | bytes 122912 | tf_op jit(solution)/shard_map/ppermute | solution.py:533
  42.1 1.0 %collective-permute-start.17 = (bf16[96,640]{1,0:T(8,128)(2,1)S(1)}, bf16[96,640]{1,0:T(8,128)(2,1)S(1)}, u32[]{:S(2)}, u32[]{:S(2)}) collective-permute-start(bf16[96,640]{1,0:T(8,128)(2,1)S(1)} %total.1.refs_0_), channel_id=1, source_target_pairs={{0,8},{4,12},{8,0},{12,4},{16,24},{20,28},{24,16},{28,20},{1,9},{5... | collective-permute-start | bytes 368648 | tf_op jit(solution)/shard_map/ppermute | solution.py:530
  43.1 1.2 %collective-permute-start.18 = (bf16[96,640]{1,0:T(8,128)(2,1)S(1)}, bf16[96,640]{1,0:T(8,128)(2,1)S(1)}, u32[]{:S(2)}, u32[]{:S(2)}) collective-permute-start(bf16[96,640]{1,0:T(8,128)(2,1)S(1)} %total.1.refs_0_), channel_id=1, source_target_pairs={{0,16},{4,20},{8,24},{12,28},{16,0},{20,4},{24,8},{28,12},{1,17},{... | collective-permute-start | bytes 368648 | tf_op jit(solution)/shard_map/ppermute | solution.py:530
  44.2 1.4 %collective-permute-start.19 = (bf16[96,640]{1,0:T(8,128)(2,1)S(1)}, bf16[96,640]{1,0:T(8,128)(2,1)S(1)}, u32[]{:S(2)}, u32[]{:S(2)}) collective-permute-start(bf16[96,640]{1,0:T(8,128)(2,1)S(1)} %total.1.refs_0_), channel_id=1, source_target_pairs={{0,24},{4,28},{8,16},{12,20},{16,8},{20,12},{24,0},{28,4},{1,25},{... | collective-permute-start | bytes 368648 | tf_op jit(solution)/shard_map/ppermute | solution.py:530
  45.7 1.9 %collective-permute-done.17.refs_1_ = bf16[96,640]{1,0:T(8,128)(2,1)S(1)} collective-permute-done((bf16[96,640]{1,0:T(8,128)(2,1)S(1)}, bf16[96,640]{1,0:T(8,128)(2,1)S(1)}, u32[]{:S(2)}, u32[]{:S(2)}) %collective-permute-start.17) | collective-permute-done | bytes 122912 | tf_op jit(solution)/shard_map/ppermute | solution.py:530
  47.6 0.4 collective-permute-done.18.refs_2_
  48.0 2.0 %collective-permute-done.19.refs_3_ = bf16[96,640]{1,0:T(8,128)(2,1)S(1)} collective-permute-done((bf16[96,640]{1,0:T(8,128)(2,1)S(1)}, bf16[96,640]{1,0:T(8,128)(2,1)S(1)}, u32[]{:S(2)}, u32[]{:S(2)}) %collective-permute-start.19) | collective-permute-done | bytes 122912 | tf_op jit(solution)/shard_map/ppermute | solution.py:530
  50.1 1.3 %part.1 = (f32[320,720]{1,0:T(8,128)S(1)}, f32[320,720]{1,0:T(8,128)S(1)}, bf16[128,320]{1,0:T(8,128)(2,1)}) custom-call(bf16[4,96,640]{2,1,0:T(8,128)(2,1)S(1)} %stack.1.stack_ref, bf16[2,320,192]{2,1,0:T(8,128)(2,1)S(1)} %get-tuple-element.35.refs_7_.main_ref.refs_1_, bf16[2,320,160]{2,1,0:T(8,128)(2,1)S(1)} %get-tuple-element.36.fold_ref.refs_2_, ...), custom_call_target="tpu_custom_call" | custom-call | flops 1000000 | bytes 3000 | tf_op jit(solution)/shard_map/part/pallas_call | solution.py:505
  51.4 0.6 %collective-permute-done.20.refs_0_ = bf16[4,96,640]{2,1,0:T(8,128)(2,1)S(1)} collective-permute-done((bf16[4,96,640]{2,1,0:T(8,128)(2,1)S(1)}, bf16[4,96,640]{2,1,0:T(8,128)(2,1)S(1)}, u32[]{:S(2)}, u32[]{:S(2)}) %collective-permute-start.20) | collective-permute-done | bytes 491552 | tf_op jit(solution)/shard_map/ppermute | solution.py:530
  52.0 1.8 %last.1 = (f32[320,720]{1,0:T(8,128)}, f32[320,720]{1,0:T(8,128)}) custom-call(bf16[4,96,640]{2,1,0:T(8,128)(2,1)S(1)} %collective-permute-done.20.refs_0_, bf16[2,320,192]{2,1,0:T(8,128)(2,1)S(1)} %get-tuple-element.35.refs_7_.main_ref.refs_1_, bf16[2,320,160]{2,1,0:T(8,128)(2,1)S(1)} %get-tuple-element.36.fold_ref.refs_2_, ...), custom_call_target="tpu_custom_call" | custom-call | flops 100000000 | bytes 300000 | tf_op jit(solution)/shard_map/last/pallas_call | solution.py:505
  (30 shorter events, 1.6 us)
Async XLA Ops:
  0.6 8.2 %copy-start = (bf16[1,8,16,320]{3,2,1,0:T(8,128)(2,1)S(1)}, bf16[1,8,16,320]{3,2,1,0:T(8,128)(2,1)}, u32[]{:S(2)}) copy-start(bf16[1,8,16,320]{3,2,1,0:T(8,128)(2,1)} %param.7) | copy-start | bytes 245764
  0.6 8.2 %copy-start.2 = (bf16[1,8,16,320]{3,2,1,0:T(8,128)(2,1)S(1)}, bf16[1,8,16,320]{3,2,1,0:T(8,128)(2,1)}, u32[]{:S(2)}) copy-start(bf16[1,8,16,320]{3,2,1,0:T(8,128)(2,1)} %param.8) | copy-start | bytes 245764
  2.5 10.0 %collective-permute-start.7 = (bf16[96,640]{1,0:T(8,128)(2,1)S(1)}, bf16[96,640]{1,0:T(8,128)(2,1)S(1)}, u32[]{:S(2)}, u32[]{:S(2)}) collective-permute-start(bf16[96,640]{1,0:T(8,128)(2,1)S(1)} %slices.1.after_ref.refs_8_), channel_id=1, source_target_pairs={{0,1},{1,0},{2,3},{3,2},{4,5},{5,4},{6,7},{7,6},{8,9},{9,8},{10,11... | collective-permute-start | bytes 368648 | tf_op jit(solution)/shard_map/ppermute | solution.py:533
  5.6 8.4 %collective-permute-start.8 = (bf16[96,640]{1,0:T(8,128)(2,1)S(1)}, bf16[96,640]{1,0:T(8,128)(2,1)S(1)}, u32[]{:S(2)}, u32[]{:S(2)}) collective-permute-start(bf16[96,640]{1,0:T(8,128)(2,1)S(1)} %slices.1.after_ref.refs_8_), channel_id=1, source_target_pairs={{0,2},{1,3},{2,0},{3,1},{4,6},{5,7},{6,4},{7,5},{8,10},{9,11},{10,... | collective-permute-start | bytes 368648 | tf_op jit(solution)/shard_map/ppermute | solution.py:533
  9.3 12.8 %copy-start.1 = (bf16[1280,320]{0,1:T(8,128)(2,1)S(1)}, bf16[1280,320]{0,1:T(8,128)(2,1)}, u32[]{:S(2)}) copy-start(bf16[1280,320]{0,1:T(8,128)(2,1)} %param.11) | copy-start | bytes 2457604
  9.4 13.2 %collective-permute-start = (bf16[144,640]{1,0:T(8,128)(2,1)S(1)}, bf16[144,640]{1,0:T(8,128)(2,1)S(1)}, u32[]{:S(2)}, u32[]{:S(2)}) collective-permute-start(bf16[144,640]{1,0:T(8,128)(2,1)S(1)} %act.1.refs_0_), channel_id=1, source_target_pairs={{0,4},{4,0},{8,12},{12,8},{16,20},{20,16},{24,28},{28,24},{1,5},{5... | collective-permute-start | bytes 552968 | tf_op jit(solution)/shard_map/ppermute | solution.py:530
  9.4 7.5 %collective-permute-start.1 = (bf16[144,640]{1,0:T(8,128)(2,1)S(1)}, bf16[144,640]{1,0:T(8,128)(2,1)S(1)}, u32[]{:S(2)}, u32[]{:S(2)}) collective-permute-start(bf16[144,640]{1,0:T(8,128)(2,1)S(1)} %act.1.refs_0_), channel_id=1, source_target_pairs={{0,8},{4,12},{8,0},{12,4},{16,24},{20,28},{24,16},{28,20},{1,9},{5... | collective-permute-start | bytes 552968 | tf_op jit(solution)/shard_map/ppermute | solution.py:530
  11.0 10.7 %collective-permute-start.3 = (bf16[144,640]{1,0:T(8,128)(2,1)S(1)}, bf16[144,640]{1,0:T(8,128)(2,1)S(1)}, u32[]{:S(2)}, u32[]{:S(2)}) collective-permute-start(bf16[144,640]{1,0:T(8,128)(2,1)S(1)} %act.1.refs_0_), channel_id=1, source_target_pairs={{0,16},{4,20},{8,24},{12,28},{16,0},{20,4},{24,8},{28,12},{1,17},{... | collective-permute-start | bytes 552968 | tf_op jit(solution)/shard_map/ppermute | solution.py:530
  12.5 9.1 %collective-permute-start.5 = (bf16[144,640]{1,0:T(8,128)(2,1)S(1)}, bf16[144,640]{1,0:T(8,128)(2,1)S(1)}, u32[]{:S(2)}, u32[]{:S(2)}) collective-permute-start(bf16[144,640]{1,0:T(8,128)(2,1)S(1)} %act.1.refs_0_), channel_id=1, source_target_pairs={{0,24},{4,28},{8,16},{12,20},{16,8},{20,12},{24,0},{28,4},{1,25},{... | collective-permute-start | bytes 552968 | tf_op jit(solution)/shard_map/ppermute | solution.py:530
  14.0 8.6 %collective-permute-start.9 = (bf16[96,640]{1,0:T(8,128)(2,1)S(1)}, bf16[96,640]{1,0:T(8,128)(2,1)S(1)}, u32[]{:S(2)}, u32[]{:S(2)}) collective-permute-start(bf16[96,640]{1,0:T(8,128)(2,1)S(1)} %relay.1.refs_10_), channel_id=1, source_target_pairs={{0,1},{1,0},{2,3},{3,2},{4,5},{5,4},{6,7},{7,6},{8,9},{9,8},{10,11... | collective-permute-start | bytes 368648 | tf_op jit(solution)/shard_map/ppermute | solution.py:533
  16.9 5.7 %collective-permute-start.2 = (bf16[144,640]{1,0:T(8,128)(2,1)S(1)}, bf16[144,640]{1,0:T(8,128)(2,1)S(1)}, u32[]{:S(2)}, u32[]{:S(2)}) collective-permute-start(bf16[144,640]{1,0:T(8,128)(2,1)S(1)} %collective-permute-done.1.refs_2_), channel_id=1, source_target_pairs={{0,4},{4,0},{8,12},{12,8},{16,20},{20,16},{24,28},{28,24},{1,5},{5... | collective-permute-start | bytes 552968 | tf_op jit(solution)/shard_map/ppermute | solution.py:530
  21.6 1.4 %collective-permute-start.4 = (bf16[144,640]{1,0:T(8,128)(2,1)S(1)}, bf16[144,640]{1,0:T(8,128)(2,1)S(1)}, u32[]{:S(2)}, u32[]{:S(2)}) collective-permute-start(bf16[144,640]{1,0:T(8,128)(2,1)S(1)} %collective-permute-done.3.refs_4_), channel_id=1, source_target_pairs={{0,4},{4,0},{8,12},{12,8},{16,20},{20,16},{24,28},{28,24},{1,5},{5... | collective-permute-start | bytes 552968 | tf_op jit(solution)/shard_map/ppermute | solution.py:530
  21.7 1.7 %collective-permute-start.6 = (bf16[144,640]{1,0:T(8,128)(2,1)S(1)}, bf16[144,640]{1,0:T(8,128)(2,1)S(1)}, u32[]{:S(2)}, u32[]{:S(2)}) collective-permute-start(bf16[144,640]{1,0:T(8,128)(2,1)S(1)} %collective-permute-done.5.refs_6_), channel_id=1, source_target_pairs={{0,4},{4,0},{8,12},{12,8},{16,20},{20,16},{24,28},{28,24},{1,5},{5... | collective-permute-start | bytes 552968 | tf_op jit(solution)/shard_map/ppermute | solution.py:530
  22.2 1.2 %copy-start.3 = (s32[4]{0:T(128)S(1)}, s32[4]{0:T(128)}, u32[]{:S(2)}) copy-start(s32[4]{0:T(128)} %owner_ref.1) | copy-start | bytes 52
  28.9 4.7 %collective-permute-start.13 = (bf16[4,128,320]{2,1,0:T(8,128)(2,1)S(1)}, bf16[4,128,320]{2,1,0:T(8,128)(2,1)S(1)}, u32[]{:S(2)}, u32[]{:S(2)}) collective-permute-start(bf16[4,128,320]{2,1,0:T(8,128)(2,1)S(1)} %get-tuple-element.30), channel_id=1, source_target_pairs={{0,4},{4,0},{8,12},{12,8},{16,20},{20,16},{24,28},{28,24},{1,5},{5... | collective-permute-start | bytes 983048 | tf_op jit(solution)/shard_map/ppermute | solution.py:530
  29.2 6.9 %collective-permute-start.10 = (bf16[96,640]{1,0:T(8,128)(2,1)S(1)}, bf16[96,640]{1,0:T(8,128)(2,1)S(1)}, u32[]{:S(2)}, u32[]{:S(2)}) collective-permute-start(bf16[96,640]{1,0:T(8,128)(2,1)S(1)} %get-tuple-element.24), channel_id=1, source_target_pairs={{0,1},{1,0},{2,3},{3,2},{4,5},{5,4},{6,7},{7,6},{8,9},{9,8},{10,11... | collective-permute-start | bytes 368648 | tf_op jit(solution)/shard_map/ppermute | solution.py:533
  29.6 12.4 %collective-permute-start.11 = (bf16[96,640]{1,0:T(8,128)(2,1)S(1)}, bf16[96,640]{1,0:T(8,128)(2,1)S(1)}, u32[]{:S(2)}, u32[]{:S(2)}) collective-permute-start(bf16[96,640]{1,0:T(8,128)(2,1)S(1)} %get-tuple-element.25), channel_id=1, source_target_pairs={{0,2},{1,3},{2,0},{3,1},{4,6},{5,7},{6,4},{7,5},{8,10},{9,11},{10,... | collective-permute-start | bytes 368648 | tf_op jit(solution)/shard_map/ppermute | solution.py:533
  30.0 12.0 %collective-permute-start.12 = (bf16[96,640]{1,0:T(8,128)(2,1)S(1)}, bf16[96,640]{1,0:T(8,128)(2,1)S(1)}, u32[]{:S(2)}, u32[]{:S(2)}) collective-permute-start(bf16[96,640]{1,0:T(8,128)(2,1)S(1)} %get-tuple-element.26), channel_id=1, source_target_pairs={{0,3},{1,2},{2,1},{3,0},{4,7},{5,6},{6,5},{7,4},{8,11},{9,10},{10,... | collective-permute-start | bytes 368648 | tf_op jit(solution)/shard_map/ppermute | solution.py:533
  33.6 8.4 %collective-permute-start.14 = (bf16[128,320]{1,0:T(8,128)(2,1)S(1)}, bf16[128,320]{1,0:T(8,128)(2,1)S(1)}, u32[]{:S(2)}, u32[]{:S(2)}) collective-permute-start(bf16[128,320]{1,0:T(8,128)(2,1)S(1)} %get-tuple-element.31), channel_id=1, source_target_pairs={{0,8},{4,12},{8,0},{12,4},{16,24},{20,28},{24,16},{28,20},{1,9},{5... | collective-permute-start | bytes 245768 | tf_op jit(solution)/shard_map/ppermute | solution.py:530
  34.6 7.4 %collective-permute-start.15 = (bf16[128,320]{1,0:T(8,128)(2,1)S(1)}, bf16[128,320]{1,0:T(8,128)(2,1)S(1)}, u32[]{:S(2)}, u32[]{:S(2)}) collective-permute-start(bf16[128,320]{1,0:T(8,128)(2,1)S(1)} %get-tuple-element.32), channel_id=1, source_target_pairs={{0,16},{4,20},{8,24},{12,28},{16,0},{20,4},{24,8},{28,12},{1,17},{... | collective-permute-start | bytes 245768 | tf_op jit(solution)/shard_map/ppermute | solution.py:530
  36.1 6.0 %collective-permute-start.16 = (bf16[128,320]{1,0:T(8,128)(2,1)S(1)}, bf16[128,320]{1,0:T(8,128)(2,1)S(1)}, u32[]{:S(2)}, u32[]{:S(2)}) collective-permute-start(bf16[128,320]{1,0:T(8,128)(2,1)S(1)} %get-tuple-element.33), channel_id=1, source_target_pairs={{0,24},{4,28},{8,16},{12,20},{16,8},{20,12},{24,0},{28,4},{1,25},{... | collective-permute-start | bytes 245768 | tf_op jit(solution)/shard_map/ppermute | solution.py:530
  42.1 5.5 %collective-permute-start.17 = (bf16[96,640]{1,0:T(8,128)(2,1)S(1)}, bf16[96,640]{1,0:T(8,128)(2,1)S(1)}, u32[]{:S(2)}, u32[]{:S(2)}) collective-permute-start(bf16[96,640]{1,0:T(8,128)(2,1)S(1)} %total.1.refs_0_), channel_id=1, source_target_pairs={{0,8},{4,12},{8,0},{12,4},{16,24},{20,28},{24,16},{28,20},{1,9},{5... | collective-permute-start | bytes 368648 | tf_op jit(solution)/shard_map/ppermute | solution.py:530
  43.1 4.9 %collective-permute-start.18 = (bf16[96,640]{1,0:T(8,128)(2,1)S(1)}, bf16[96,640]{1,0:T(8,128)(2,1)S(1)}, u32[]{:S(2)}, u32[]{:S(2)}) collective-permute-start(bf16[96,640]{1,0:T(8,128)(2,1)S(1)} %total.1.refs_0_), channel_id=1, source_target_pairs={{0,16},{4,20},{8,24},{12,28},{16,0},{20,4},{24,8},{28,12},{1,17},{... | collective-permute-start | bytes 368648 | tf_op jit(solution)/shard_map/ppermute | solution.py:530
  44.2 5.8 %collective-permute-start.19 = (bf16[96,640]{1,0:T(8,128)(2,1)S(1)}, bf16[96,640]{1,0:T(8,128)(2,1)S(1)}, u32[]{:S(2)}, u32[]{:S(2)}) collective-permute-start(bf16[96,640]{1,0:T(8,128)(2,1)S(1)} %total.1.refs_0_), channel_id=1, source_target_pairs={{0,24},{4,28},{8,16},{12,20},{16,8},{20,12},{24,0},{28,4},{1,25},{... | collective-permute-start | bytes 368648 | tf_op jit(solution)/shard_map/ppermute | solution.py:530
  50.0 1.9 %collective-permute-start.20 = (bf16[4,96,640]{2,1,0:T(8,128)(2,1)S(1)}, bf16[4,96,640]{2,1,0:T(8,128)(2,1)S(1)}, u32[]{:S(2)}, u32[]{:S(2)}) collective-permute-start(bf16[4,96,640]{2,1,0:T(8,128)(2,1)S(1)} %stack.1.stack_ref), channel_id=1, source_target_pairs={{0,4},{4,0},{8,12},{12,8},{16,20},{20,16},{24,28},{28,24},{1,5},{5... | collective-permute-start | bytes 1474568 | tf_op jit(solution)/shard_map/ppermute | solution.py:530
